TPU v7x, 128 devices: a whole 4x4x4 slice. The times are simulated.
128 devices in a mesh: seq: 4 (over y), ep: 32 (over z, x, core).
Axes of the slice: x: 4, y: 4, z: 4, core: 2. Of those that a mesh axis runs over, the one named last changes fastest.
Arguments:
- queries: bfloat16 [4, 256, 4, 4096], P('seq', 'ep'), may hold values from -160 to 160
- fresh_key_values: bfloat16 [4, 256, 4, 1024], P('seq', 'ep'), may hold values from -6 to 6
- key_value_pages: bfloat16 [4, 768, 16, 1024], P('seq', 'ep'), may hold values from -6 to 6
- page_owner: int32 [4, 4096, 2], P('seq'), may hold values from 0 to 31, all different within a row; in each aligned block of 128 rows (0 to 127, 128 to 255, ..., all dimensions but the last counted through in order) at most 16 rows name the same one
- page_slot: int32 [4, 4096, 2], P('seq'), may hold values from 0 to 23
- page_count: int32 [4, 256], P(None, 'ep'), may hold values from 1 to 1024
- sinks: float32 [64], replicated, may hold values from 1 to 5
- hidden: bfloat16 [4, 256, 4, 2880], P('seq', 'ep'), may hold values from -6 to 6
- norm_gain: float32 [2880], replicated, may hold values from 0.1 to 1.9
- expert_ids: int32 [4, 256, 4, 4], P('seq', 'ep'), may hold values from 0 to 127, all different within a row; in each aligned block of 32 rows (0 to 31, 32 to 63, ..., all dimensions but the last counted through in order) at most 2 rows name the same one
- gate_prob: float32 [4, 256, 4, 4], P('seq', 'ep'), may hold values from 0.05 to 0.6
- gate_up: bfloat16 [128, 2880, 2880], P(('seq', 'ep')), may hold values from -0.109375 to 0.109375
- down_proj: bfloat16 [128, 1440, 2880], P(('seq', 'ep')), may hold values from -0.15625 to 0.15625
Outputs:
- attention: bfloat16 [4, 256, 4, 4096], P('seq', 'ep')
- mixture: bfloat16 [4, 256, 4, 2880], P('seq', 'ep')
Inputs may be any that keep to these rules, and one draw needn't show every extreme that they name: `page_owner`: each pair of pages names 2 different owners; in one segment the 256 pages of one ep index's prefix name one owner at most 16 times. `expert_ids`: each token names 4 different experts; the tokens of one device name one expert at most 2 times.
All inputs are finite; a program needn't handle non-finite values.
Results may differ from a plain program's by a relative error of at most 0.0068.
Values may be sent and summed in bfloat16 or wider, within the bound.
A program may use at most 192 MiB of HBM per device.

v0:
```python
import jax
import jax.numpy as jnp
from jax import lax
from jax.sharding import PartitionSpec as P

D = 2880
QUERY_HEADS = 64
KEY_VALUE_HEADS = 8
HEAD_WIDTH = 64
TOPK = 4
HID = 1440
SCORED_STEPS = 4
PAGE_TOKENS = 16
NPS = 256


SCALE = 0.125
NEGATIVE = -1e30
EPSILON = 1e-05


def softmax_parts(scores, shown):
    scores = jnp.where(shown, scores, NEGATIVE)
    maxima = jnp.max(scores, axis=-1)
    weights_full = jnp.where(shown, jnp.exp(scores - maxima[..., None]), 0.0)
    totals = jnp.sum(weights_full, axis=-1)
    return (maxima, totals, weights_full.astype(jnp.bfloat16))


def shared_scores(query_matrix, key_value_table, visible):
    prompt_batch, position_index, _ = query_matrix.shape
    prompt_length = key_value_table.shape[0]
    split_point = KEY_VALUE_HEADS * HEAD_WIDTH
    query_head_rows = query_matrix.reshape(
        prompt_batch, position_index, KEY_VALUE_HEADS, QUERY_HEADS // KEY_VALUE_HEADS, HEAD_WIDTH
    )
    key_head_rows = key_value_table[:, :split_point].reshape(
        prompt_length, KEY_VALUE_HEADS, HEAD_WIDTH
    )
    value_head_rows = key_value_table[:, split_point:].reshape(
        prompt_length, KEY_VALUE_HEADS, HEAD_WIDTH
    )
    scores = (
        jnp.einsum(
            "psvgd,kvd->psvgk", query_head_rows, key_head_rows, preferred_element_type=jnp.float32
        )
        * SCALE
    )
    maxima, totals, rounded = softmax_parts(scores, visible[:, None, None, None, :])
    outputs = jnp.einsum(
        "psvgk,kvd->psvgd", rounded, value_head_rows, preferred_element_type=jnp.float32
    )
    return (
        maxima.reshape(prompt_batch, position_index, QUERY_HEADS),
        totals.reshape(prompt_batch, position_index, QUERY_HEADS),
        outputs.reshape(prompt_batch, position_index, QUERY_HEADS * HEAD_WIDTH),
    )


def own_scores(query_matrix, key_value_table, visible):
    prompt_batch, position_index, _ = query_matrix.shape
    prompt_length = key_value_table.shape[1]
    split_point = KEY_VALUE_HEADS * HEAD_WIDTH
    query_head_rows = query_matrix.reshape(
        prompt_batch, position_index, KEY_VALUE_HEADS, QUERY_HEADS // KEY_VALUE_HEADS, HEAD_WIDTH
    )
    key_head_rows = key_value_table[:, :, :split_point].reshape(
        prompt_batch, prompt_length, KEY_VALUE_HEADS, HEAD_WIDTH
    )
    value_head_rows = key_value_table[:, :, split_point:].reshape(
        prompt_batch, prompt_length, KEY_VALUE_HEADS, HEAD_WIDTH
    )
    scores = (
        jnp.einsum(
            "psvgd,pkvd->psvgk", query_head_rows, key_head_rows, preferred_element_type=jnp.float32
        )
        * SCALE
    )
    maxima, totals, rounded = softmax_parts(scores, visible[:, :, None, None, :])
    outputs = jnp.einsum(
        "psvgk,pkvd->psvgd", rounded, value_head_rows, preferred_element_type=jnp.float32
    )
    return (
        maxima.reshape(prompt_batch, position_index, QUERY_HEADS),
        totals.reshape(prompt_batch, position_index, QUERY_HEADS),
        outputs.reshape(prompt_batch, position_index, QUERY_HEADS * HEAD_WIDTH),
    )


def per_device(
    queries,
    fresh_key_values,
    key_value_pages,
    page_owner,
    page_slot,
    page_count,
    sinks,
    hidden,
    norm_gain,
    expert_ids,
    gate_prob,
    gate_up,
    down_proj,
):
    seq_size = lax.axis_size("seq")
    ep_size = lax.axis_size("ep")
    seq_index = lax.axis_index("seq")
    ep_index = lax.axis_index("ep")
    batch = queries.shape[1]
    rows = seq_size * batch
    feature_columns = 2 * KEY_VALUE_HEADS * HEAD_WIDTH
    column = lax.all_gather(queries, "seq", axis=0, tiled=True).reshape(
        rows, SCORED_STEPS, QUERY_HEADS * HEAD_WIDTH
    )
    owners = page_owner[0].reshape(ep_size, NPS)
    slots = page_slot[0].reshape(ep_size, NPS)
    my_owner = lax.dynamic_index_in_dim(owners, ep_index, 0, keepdims=False)
    capacity = max(2, 2 * NPS // ep_size)
    onehot = (owners[:, :, None] == jnp.arange(ep_size, dtype=jnp.int32)[None, None, :]).astype(
        jnp.int32
    )
    ranks = jnp.sum((jnp.cumsum(onehot, axis=1) - 1) * onehot, axis=-1)
    placed = jnp.where(owners == ep_index, ranks, capacity)
    picks = (
        jnp.zeros((ep_size, capacity), jnp.int32)
        .at[jnp.arange(ep_size, dtype=jnp.int32)[:, None], placed]
        .set(slots, mode="drop")
    )
    outgoing = key_value_pages[0][picks]
    incoming = lax.all_to_all(outgoing, "ep", split_axis=0, concat_axis=0, tiled=True)
    my_rank = lax.dynamic_index_in_dim(ranks, ep_index, 0, keepdims=False)
    page_rows = incoming[my_owner, my_rank]
    keys = page_rows.reshape(NPS * PAGE_TOKENS, feature_columns)
    counts = page_count.reshape(rows)
    live = (seq_index * NPS + jnp.arange(NPS, dtype=jnp.int32))[None, :] < counts[:, None]
    visible = jnp.repeat(live, PAGE_TOKENS, axis=1)
    block = 4
    blocks = rows // block

    def score_block(pieces):
        return shared_scores(pieces[0], keys, pieces[1])

    seg_max, seg_total, seg_out = lax.map(
        score_block,
        (
            column.reshape(blocks, block, SCORED_STEPS, QUERY_HEADS * HEAD_WIDTH),
            visible.reshape(blocks, block, NPS * PAGE_TOKENS),
        ),
    )
    seg_max, seg_total, seg_out = (
        lax.all_to_all(
            seg_max.reshape(seq_size, batch, SCORED_STEPS, QUERY_HEADS),
            "seq",
            split_axis=0,
            concat_axis=0,
            tiled=True,
        ),
        lax.all_to_all(
            seg_total.reshape(seq_size, batch, SCORED_STEPS, QUERY_HEADS),
            "seq",
            split_axis=0,
            concat_axis=0,
            tiled=True,
        ),
        lax.all_to_all(
            seg_out.reshape(seq_size, batch, SCORED_STEPS, QUERY_HEADS * HEAD_WIDTH),
            "seq",
            split_axis=0,
            concat_axis=0,
            tiled=True,
        ),
    )
    causal = jnp.arange(SCORED_STEPS)[:, None] >= jnp.arange(SCORED_STEPS)[None, :]
    own_visible = jnp.broadcast_to(causal[None], (batch, SCORED_STEPS, SCORED_STEPS))
    own_max, own_total, own_out = own_scores(queries[0], fresh_key_values[0], own_visible)
    highest = jnp.maximum(jnp.max(seg_max, axis=0), own_max)
    highest = jnp.maximum(highest, sinks)
    factor = jnp.exp(seg_max - highest[None])
    own_factor = jnp.exp(own_max - highest)
    denominator = (
        jnp.sum(seg_total * factor, axis=0) + own_total * own_factor + jnp.exp(sinks - highest)
    )
    numerator = jnp.sum(
        seg_out * jnp.repeat(factor, HEAD_WIDTH, axis=-1), axis=0
    ) + own_out * jnp.repeat(own_factor, HEAD_WIDTH, axis=-1)
    attention = (
        (numerator / jnp.repeat(denominator, HEAD_WIDTH, axis=-1))
        .astype(jnp.bfloat16)
        .reshape(queries.shape)
    )
    experts_all = seq_size * ep_size * gate_up.shape[0]
    tokens_here = batch * SCORED_STEPS
    slots_per = max(2, 2 * tokens_here * TOPK // experts_all)
    flat_hidden = hidden.reshape(tokens_here, D).astype(jnp.float32)
    meansq = jnp.mean(flat_hidden * flat_hidden, axis=-1, keepdims=True)
    normed = (flat_hidden * lax.rsqrt(meansq + EPSILON) * norm_gain).astype(jnp.bfloat16)
    chosen = expert_ids.reshape(tokens_here * TOPK)
    expert_hot = (chosen[:, None] == jnp.arange(experts_all, dtype=jnp.int32)[None, :]).astype(
        jnp.int32
    )
    expert_rank = jnp.sum((jnp.cumsum(expert_hot, axis=0) - 1) * expert_hot, axis=-1)
    repeated = jnp.repeat(normed, TOPK, axis=0)
    buffer = (
        jnp.zeros((experts_all, slots_per, D), jnp.bfloat16).at[chosen, expert_rank].set(repeated)
    )
    arrived = lax.all_to_all(buffer, ("seq", "ep"), split_axis=0, concat_axis=0, tiled=True)
    flat_rows = arrived.reshape(-1, D)
    projected = jnp.dot(flat_rows, gate_up[0], preferred_element_type=jnp.float32)
    gate = projected[:, :HID]
    upper = projected[:, HID:]
    active = ((upper + 1.0) * gate * jax.nn.sigmoid(1.702 * gate)).astype(jnp.bfloat16)
    result = jnp.dot(active, down_proj[0], preferred_element_type=jnp.float32).astype(jnp.bfloat16)
    finished = result.reshape(arrived.shape)
    returned = lax.all_to_all(finished, ("seq", "ep"), split_axis=0, concat_axis=0, tiled=True)
    picked = returned[chosen, expert_rank].astype(jnp.float32)
    weighted = picked * gate_prob.reshape(tokens_here * TOPK, 1)
    mixture = (
        jnp.sum(weighted.reshape(tokens_here, TOPK, D), axis=1)
        .astype(jnp.bfloat16)
        .reshape(hidden.shape)
    )
    return (attention, mixture)


def solution(mesh):
    return jax.shard_map(
        per_device,
        mesh=mesh,
        in_specs=(
            P("seq", "ep", None, None),
            P("seq", "ep", None, None),
            P("seq", "ep", None, None),
            P("seq", None, None),
            P("seq", None, None),
            P(None, "ep"),
            P(),
            P("seq", "ep", None, None),
            P(),
            P("seq", "ep", None, None),
            P("seq", "ep", None, None),
            P(("seq", "ep"), None, None),
            P(("seq", "ep"), None, None),
        ),
        out_specs=(P("seq", "ep", None, None), P("seq", "ep", None, None)),
        check_vma=False,
    )
```

profile of v0, /device:TPU:0, one launch (start us, length us, event | category | flops | bytes accessed | tf_op | source)
XLA Modules:
  0.0 675.4 jit_solution(136346154357795344)
XLA Ops:
  12.8 1.9 broadcast_in_dim.119
  14.7 25.7 %scatter_fusion = bf16[128,2,2880]{2,1,0:T(2,128)(2,1)} fusion(bf16[128,2,2880]{2,1,0:T(2,128)(2,1)} %broadcast_in_dim.119, s32[128]{0:T(128)S(1)} %get-tuple-element.90, bf16[128,2880]{1,0:T(8,128)(2,1)S(1)} %reshape.355), kind=kCustom, calls=%fused_computation.3 | custom fusion | bytes 2212864 | tf_op jit(solution)/shard_map/scatter | solution.py:204
  40.4 11.7 %all-to-all-start.4 = ((bf16[128,2,2880]{2,1,0:T(2,128)(2,1)}), bf16[128,2,2880]{2,1,0:T(2,128)(2,1)}, u32[]{:S(2)}, u32[]{:S(2)}) async-start(bf16[128,2,2880]{2,1,0:T(2,128)(2,1)} %scatter_fusion), calls=%async_computation.4 | async-start | bytes 3014656 | tf_op jit(solution)/shard_map/all_to_all | solution.py:206
  56.5 32.3 %reduce-window.6 = s32[32,32,2,128]{3,1,2,0:T(8,128)S(1)} reduce-window(s32[32,32,2,128]{3,1,2,0:T(8,128)} %fusion.30, s32[]{:T(128)} %copy.192), window={size=1x1x1x128 pad=0_0x0_0x0_0x127_0}, to_apply=%region_0.1 | reduce-window | flops 33292288 | bytes 2097156 | tf_op jit(solution)/shard_map/reduce-window
  90.6 1.6 eq.58
  94.7 30.4 %scatter_custom_fusion.1 = s32[512]{0:T(512)S(1)} fusion(s32[8192]{0:T(1024)S(1)} %bitcast.155, s32[8192]{0:T(1024)S(1)} %reshape.361, s32[]{:T(128)} %copy.192), kind=kCustom, calls=%fused_computation.96 | custom fusion | bytes 2052
  125.4 13.8 %gather_fusion = bf16[512,16,1024]{2,1,0:T(8,128)(2,1)} fusion(bf16[24,16,1024]{2,1,0:T(8,128)(2,1)S(1)} %bitcast.140, s32[1024]{0:T(1024)S(1)} %pad_clamp_fusion), kind=kCustom, calls=%fused_computation | custom fusion | bytes 33556480 | tf_op jit(solution)/shard_map/gather | solution.py:129
  139.3 7.4 %all-to-all-start = ((bf16[32,16,16,1024]{3,2,1,0:T(8,128)(2,1)}), bf16[32,16,16,1024]{3,2,1,0:T(8,128)(2,1)}, u32[]{:S(2)}, u32[]{:S(2)}) async-start(bf16[32,16,16,1024]{3,2,1,0:T(8,128)(2,1)} %bitcast.143), calls=%async_computation | async-start | bytes 33554432 | tf_op jit(solution)/shard_map/all_to_all | solution.py:130
  149.4 2.3 reshape_reshape.6
  151.8 3.5 reshape.325
  155.3 12.7 %fusion.16 = f32[256,2880]{0,1:T(8,128)} fusion(bf16[256,2880]{1,0:T(8,128)(2,1)S(1)} %reshape.325, bf16[1,2880,2880]{2,1,0:T(8,128)(2,1)} %param.26), kind=kOutput, calls=%fused_computation.26 | convolution fusion | flops 4246732800 | bytes 21012480 | tf_op jit(solution)/shard_map/dot_general | solution.py:208
  168.0 9.3 %fusion.20 = bf16[256,2880]{0,1:T(8,128)(2,1)} fusion(bf16[1,1440,2880]{2,1,0:T(8,128)(2,1)} %param.27, f32[256,2880]{0,1:T(8,128)} %fusion.16), kind=kOutput, calls=%fused_computation.30 | convolution fusion | flops 2127052800 | bytes 12718080 | tf_op jit(solution)/shard_map/dot_general | solution.py:212
  177.3 1.8 copy.130
  180.6 2.0 copy.107
  182.6 177.3 %all-to-all-done = bf16[32,16,16,1024]{3,2,1,0:T(8,128)(2,1)} async-done(((bf16[32,16,16,1024]{3,2,1,0:T(8,128)(2,1)}), bf16[32,16,16,1024]{3,2,1,0:T(8,128)(2,1)}, u32[]{:S(2)}, u32[]{:S(2)}) %all-to-all-start) | async-done | bytes 16777248 | tf_op jit(solution)/shard_map/all_to_all | solution.py:130
  359.9 6.1 all-to-all-start.5
  366.0 15.8 %gather_fusion.1 = bf16[256,16,1024]{2,1,0:T(8,128)(2,1)} fusion(bf16[32,16,16,1024]{3,2,1,0:T(8,128)(2,1)} %all-to-all-done, s32[256]{0:T(256)S(1)} %bitcast.145), kind=kCustom, calls=%fused_computation.1 | custom fusion | bytes 16779264 | tf_op jit(solution)/shard_map/gather | solution.py:132
  381.8 11.2 %copy.116 = bf16[4096,1024]{0,1:T(8,128)(2,1)} copy(bf16[4096,1024]{1,0:T(8,128)(2,1)} %bitcast.144) | data formatting | bytes 16777216 | tf_op jit(solution)/shard_map/while | solution.py:143
  393.1 220.7 %while.14 = (s32[]{:T(128)}, f32[8,4,4,64]{3,2,1,0:T(4,128)}, f32[8,4,4,64]{3,2,1,0:T(4,128)}, f32[8,4,4,4096]{3,2,1,0:T(4,128)}, pred[8,4,4096]{2,1,0:T(4,128)(...) while((s32[]{:T(128)}, f32[8,4,4,64]{3,2,1,0:T(4,128)}, ...), condition=%wide.region_7.8_spmd, body=%wide.region_4.7_spmd.sunk | while | flops 1128265728 | bytes 153642160 | solution.py:143
  393.4 5.1 fusion.76
  398.6 2.9 bitcast_reduce_fusion.2
  401.5 7.9 %fusion.78 = f32[4,4,8,8,64]{4,3,1,0,2:T(8,128)} fusion(bf16[4096,8,64,1,1]{0,2,4,3,1:T(8,128)(2,1)} %bitcast.142, f32[8,4,4,8,4096]{4,3,2,1,0:T(8,128)S(1)} %get-tuple-element.156, f32[4,4,8,8]{3,1,0,2:T(4,128)S(1)} %get-tuple-element.157, pred[4,4096]{1,0:T(4,128)(4,1)S(1)} %dynamic-slice_bitcast_fusion.2), kind=kOutput, calls=%fused_computation.15.clone.1 | convolution fusion | flops 557842432 | bytes 21254144 | tf_op jit(solution)/shard_map/while/body/eval_jaxpr/psvgk,kvd->psvgd/dot_general | solution.py:50
  411.4 8.4 %fusion.77 = f32[4,4,8,8]{3,1,0,2:T(4,128)S(1)} fusion(f32[8,4,4,8,4096]{4,3,2,1,0:T(8,128)} %copy-done.2, f32[4,4,8,8]{3,1,0,2:T(4,128)S(1)} %get-tuple-element.157, pred[4,4096]{1,0:T(4,128)(4,1)S(1)} %dynamic-slice_bitcast_fusion.2), kind=kLoop, calls=%fused_computation.11.clone.1 | loop fusion | flops 20970496 | bytes 16801792 | tf_op jit(solution)/shard_map/while/body/eval_jaxpr/reduce_sum | solution.py:26
  421.0 5.1 fusion.76
  426.2 2.9 bitcast_reduce_fusion.2
  429.1 7.9 %fusion.78 = f32[4,4,8,8,64]{4,3,1,0,2:T(8,128)} fusion(bf16[4096,8,64,1,1]{0,2,4,3,1:T(8,128)(2,1)} %bitcast.142, f32[8,4,4,8,4096]{4,3,2,1,0:T(8,128)S(1)} %get-tuple-element.156, f32[4,4,8,8]{3,1,0,2:T(4,128)S(1)} %get-tuple-element.157, pred[4,4096]{1,0:T(4,128)(4,1)S(1)} %dynamic-slice_bitcast_fusion.2), kind=kOutput, calls=%fused_computation.15.clone.1 | convolution fusion | flops 557842432 | bytes 21254144 | tf_op jit(solution)/shard_map/while/body/eval_jaxpr/psvgk,kvd->psvgd/dot_general | solution.py:50
  439.0 8.4 %fusion.77 = f32[4,4,8,8]{3,1,0,2:T(4,128)S(1)} fusion(f32[8,4,4,8,4096]{4,3,2,1,0:T(8,128)} %copy-done.2, f32[4,4,8,8]{3,1,0,2:T(4,128)S(1)} %get-tuple-element.157, pred[4,4096]{1,0:T(4,128)(4,1)S(1)} %dynamic-slice_bitcast_fusion.2), kind=kLoop, calls=%fused_computation.11.clone.1 | loop fusion | flops 20970496 | bytes 16801792 | tf_op jit(solution)/shard_map/while/body/eval_jaxpr/reduce_sum | solution.py:26
  448.6 5.1 fusion.76
  453.8 2.9 bitcast_reduce_fusion.2
  456.6 7.9 %fusion.78 = f32[4,4,8,8,64]{4,3,1,0,2:T(8,128)} fusion(bf16[4096,8,64,1,1]{0,2,4,3,1:T(8,128)(2,1)} %bitcast.142, f32[8,4,4,8,4096]{4,3,2,1,0:T(8,128)S(1)} %get-tuple-element.156, f32[4,4,8,8]{3,1,0,2:T(4,128)S(1)} %get-tuple-element.157, pred[4,4096]{1,0:T(4,128)(4,1)S(1)} %dynamic-slice_bitcast_fusion.2), kind=kOutput, calls=%fused_computation.15.clone.1 | convolution fusion | flops 557842432 | bytes 21254144 | tf_op jit(solution)/shard_map/while/body/eval_jaxpr/psvgk,kvd->psvgd/dot_general | solution.py:50
  466.6 8.4 %fusion.77 = f32[4,4,8,8]{3,1,0,2:T(4,128)S(1)} fusion(f32[8,4,4,8,4096]{4,3,2,1,0:T(8,128)} %copy-done.2, f32[4,4,8,8]{3,1,0,2:T(4,128)S(1)} %get-tuple-element.157, pred[4,4096]{1,0:T(4,128)(4,1)S(1)} %dynamic-slice_bitcast_fusion.2), kind=kLoop, calls=%fused_computation.11.clone.1 | loop fusion | flops 20970496 | bytes 16801792 | tf_op jit(solution)/shard_map/while/body/eval_jaxpr/reduce_sum | solution.py:26
  476.2 5.1 fusion.76
  481.3 2.9 bitcast_reduce_fusion.2
  484.2 7.9 %fusion.78 = f32[4,4,8,8,64]{4,3,1,0,2:T(8,128)} fusion(bf16[4096,8,64,1,1]{0,2,4,3,1:T(8,128)(2,1)} %bitcast.142, f32[8,4,4,8,4096]{4,3,2,1,0:T(8,128)S(1)} %get-tuple-element.156, f32[4,4,8,8]{3,1,0,2:T(4,128)S(1)} %get-tuple-element.157, pred[4,4096]{1,0:T(4,128)(4,1)S(1)} %dynamic-slice_bitcast_fusion.2), kind=kOutput, calls=%fused_computation.15.clone.1 | convolution fusion | flops 557842432 | bytes 21254144 | tf_op jit(solution)/shard_map/while/body/eval_jaxpr/psvgk,kvd->psvgd/dot_general | solution.py:50
  494.2 8.4 %fusion.77 = f32[4,4,8,8]{3,1,0,2:T(4,128)S(1)} fusion(f32[8,4,4,8,4096]{4,3,2,1,0:T(8,128)} %copy-done.2, f32[4,4,8,8]{3,1,0,2:T(4,128)S(1)} %get-tuple-element.157, pred[4,4096]{1,0:T(4,128)(4,1)S(1)} %dynamic-slice_bitcast_fusion.2), kind=kLoop, calls=%fused_computation.11.clone.1 | loop fusion | flops 20970496 | bytes 16801792 | tf_op jit(solution)/shard_map/while/body/eval_jaxpr/reduce_sum | solution.py:26
  503.8 5.1 fusion.76
  508.9 2.9 bitcast_reduce_fusion.2
  511.8 7.9 %fusion.78 = f32[4,4,8,8,64]{4,3,1,0,2:T(8,128)} fusion(bf16[4096,8,64,1,1]{0,2,4,3,1:T(8,128)(2,1)} %bitcast.142, f32[8,4,4,8,4096]{4,3,2,1,0:T(8,128)S(1)} %get-tuple-element.156, f32[4,4,8,8]{3,1,0,2:T(4,128)S(1)} %get-tuple-element.157, pred[4,4096]{1,0:T(4,128)(4,1)S(1)} %dynamic-slice_bitcast_fusion.2), kind=kOutput, calls=%fused_computation.15.clone.1 | convolution fusion | flops 557842432 | bytes 21254144 | tf_op jit(solution)/shard_map/while/body/eval_jaxpr/psvgk,kvd->psvgd/dot_general | solution.py:50
  521.8 8.4 %fusion.77 = f32[4,4,8,8]{3,1,0,2:T(4,128)S(1)} fusion(f32[8,4,4,8,4096]{4,3,2,1,0:T(8,128)} %copy-done.2, f32[4,4,8,8]{3,1,0,2:T(4,128)S(1)} %get-tuple-element.157, pred[4,4096]{1,0:T(4,128)(4,1)S(1)} %dynamic-slice_bitcast_fusion.2), kind=kLoop, calls=%fused_computation.11.clone.1 | loop fusion | flops 20970496 | bytes 16801792 | tf_op jit(solution)/shard_map/while/body/eval_jaxpr/reduce_sum | solution.py:26
  531.4 5.1 fusion.76
  536.5 2.9 bitcast_reduce_fusion.2
  539.4 7.9 %fusion.78 = f32[4,4,8,8,64]{4,3,1,0,2:T(8,128)} fusion(bf16[4096,8,64,1,1]{0,2,4,3,1:T(8,128)(2,1)} %bitcast.142, f32[8,4,4,8,4096]{4,3,2,1,0:T(8,128)S(1)} %get-tuple-element.156, f32[4,4,8,8]{3,1,0,2:T(4,128)S(1)} %get-tuple-element.157, pred[4,4096]{1,0:T(4,128)(4,1)S(1)} %dynamic-slice_bitcast_fusion.2), kind=kOutput, calls=%fused_computation.15.clone.1 | convolution fusion | flops 557842432 | bytes 21254144 | tf_op jit(solution)/shard_map/while/body/eval_jaxpr/psvgk,kvd->psvgd/dot_general | solution.py:50
  549.3 8.4 %fusion.77 = f32[4,4,8,8]{3,1,0,2:T(4,128)S(1)} fusion(f32[8,4,4,8,4096]{4,3,2,1,0:T(8,128)} %copy-done.2, f32[4,4,8,8]{3,1,0,2:T(4,128)S(1)} %get-tuple-element.157, pred[4,4096]{1,0:T(4,128)(4,1)S(1)} %dynamic-slice_bitcast_fusion.2), kind=kLoop, calls=%fused_computation.11.clone.1 | loop fusion | flops 20970496 | bytes 16801792 | tf_op jit(solution)/shard_map/while/body/eval_jaxpr/reduce_sum | solution.py:26
  559.0 5.1 fusion.76
  564.1 2.9 bitcast_reduce_fusion.2
  567.0 7.9 %fusion.78 = f32[4,4,8,8,64]{4,3,1,0,2:T(8,128)} fusion(bf16[4096,8,64,1,1]{0,2,4,3,1:T(8,128)(2,1)} %bitcast.142, f32[8,4,4,8,4096]{4,3,2,1,0:T(8,128)S(1)} %get-tuple-element.156, f32[4,4,8,8]{3,1,0,2:T(4,128)S(1)} %get-tuple-element.157, pred[4,4096]{1,0:T(4,128)(4,1)S(1)} %dynamic-slice_bitcast_fusion.2), kind=kOutput, calls=%fused_computation.15.clone.1 | convolution fusion | flops 557842432 | bytes 21254144 | tf_op jit(solution)/shard_map/while/body/eval_jaxpr/psvgk,kvd->psvgd/dot_general | solution.py:50
  576.9 8.4 %fusion.77 = f32[4,4,8,8]{3,1,0,2:T(4,128)S(1)} fusion(f32[8,4,4,8,4096]{4,3,2,1,0:T(8,128)} %copy-done.2, f32[4,4,8,8]{3,1,0,2:T(4,128)S(1)} %get-tuple-element.157, pred[4,4096]{1,0:T(4,128)(4,1)S(1)} %dynamic-slice_bitcast_fusion.2), kind=kLoop, calls=%fused_computation.11.clone.1 | loop fusion | flops 20970496 | bytes 16801792 | tf_op jit(solution)/shard_map/while/body/eval_jaxpr/reduce_sum | solution.py:26
  586.5 5.1 fusion.76
  591.7 2.9 bitcast_reduce_fusion.2
  594.6 7.9 %fusion.78 = f32[4,4,8,8,64]{4,3,1,0,2:T(8,128)} fusion(bf16[4096,8,64,1,1]{0,2,4,3,1:T(8,128)(2,1)} %bitcast.142, f32[8,4,4,8,4096]{4,3,2,1,0:T(8,128)S(1)} %get-tuple-element.156, f32[4,4,8,8]{3,1,0,2:T(4,128)S(1)} %get-tuple-element.157, pred[4,4096]{1,0:T(4,128)(4,1)S(1)} %dynamic-slice_bitcast_fusion.2), kind=kOutput, calls=%fused_computation.15.clone.1 | convolution fusion | flops 557842432 | bytes 21254144 | tf_op jit(solution)/shard_map/while/body/eval_jaxpr/psvgk,kvd->psvgd/dot_general | solution.py:50
  604.5 8.4 %fusion.77 = f32[4,4,8,8]{3,1,0,2:T(4,128)S(1)} fusion(f32[8,4,4,8,4096]{4,3,2,1,0:T(8,128)} %copy-done.2, f32[4,4,8,8]{3,1,0,2:T(4,128)S(1)} %get-tuple-element.157, pred[4,4096]{1,0:T(4,128)(4,1)S(1)} %dynamic-slice_bitcast_fusion.2), kind=kLoop, calls=%fused_computation.11.clone.1 | loop fusion | flops 20970496 | bytes 16801792 | tf_op jit(solution)/shard_map/while/body/eval_jaxpr/reduce_sum | solution.py:26
  613.8 1.6 reshape.378
  615.4 3.7 all-to-all-start.2
  620.6 3.9 all-to-all-done.2
  624.5 3.3 all-to-all-start.3
  628.6 4.6 all-to-all-done.3
  633.2 4.6 all-to-all-start.1
  638.4 2.5 fusion.63
  642.9 3.1 gather_fusion.2
  650.5 2.6 broadcast_in_dim.115
  653.0 3.9 reshape.316
  658.3 2.5 reshape.322
  662.1 2.5 reshape.319
  664.5 2.8 multiply_reduce_fusion
  (249 shorter events, 57.1 us)
Async XLA Ops:
  7.2 118.3 %copy-start = (bf16[1,24,16,1024]{3,2,1,0:T(8,128)(2,1)S(1)}, bf16[1,24,16,1024]{3,2,1,0:T(8,128)(2,1)}, u32[]{:S(2)}) copy-start(bf16[1,24,16,1024]{3,2,1,0:T(8,128)(2,1)} %param.17) | copy-start | bytes 2359300
  14.7 37.4 %copy-start.10 = (s32[1,4096,2]{1,2,0:T(2,128)S(1)}, s32[1,4096,2]{1,2,0:T(2,128)}, u32[]{:S(2)}) copy-start(s32[1,4096,2]{1,2,0:T(2,128)} %param.18) | copy-start | bytes 98308
  40.4 98.8 %all-to-all-start.4 = ((bf16[128,2,2880]{2,1,0:T(2,128)(2,1)}), bf16[128,2,2880]{2,1,0:T(2,128)(2,1)}, u32[]{:S(2)}, u32[]{:S(2)}) async-start(bf16[128,2,2880]{2,1,0:T(2,128)(2,1)} %scatter_fusion), calls=%async_computation.4 | async-start | bytes 3014656 | tf_op jit(solution)/shard_map/all_to_all | solution.py:206
  56.5 36.2 %copy-start.16 = (s32[2]{0:T(128)S(1)}, s32[2]{0:T(128)}, u32[]{:S(2)}) copy-start(s32[2]{0:T(128)} %constant.105) | copy-start | bytes 28
  56.5 36.3 %copy-start.15 = (s32[2]{0:T(128)S(1)}, s32[2]{0:T(128)}, u32[]{:S(2)}) copy-start(s32[2]{0:T(128)} %constant.108) | copy-start | bytes 28
  56.5 36.4 %copy-start.11 = (s32[1,4096,2]{1,2,0:T(2,128)S(1)}, s32[1,4096,2]{1,2,0:T(2,128)}, u32[]{:S(2)}) copy-start(s32[1,4096,2]{1,2,0:T(2,128)} %param.19) | copy-start | bytes 98308
  139.3 7.4 %copy-start.8 = (bf16[1,8,4,4096]{3,2,1,0:T(4,128)(2,1)S(1)}, bf16[1,8,4,4096]{3,2,1,0:T(4,128)(2,1)}, u32[]{:S(2)}) copy-start(bf16[1,8,4,4096]{3,2,1,0:T(4,128)(2,1)} %param.15) | copy-start | bytes 786436
  139.3 8.4 %copy-start.14 = (s32[4,8]{1,0:T(4,128)S(1)}, s32[4,8]{1,0:T(4,128)}, u32[]{:S(2)}) copy-start(s32[4,8]{1,0:T(4,128)} %param.20) | copy-start | bytes 388
  139.3 220.6 %all-to-all-start = ((bf16[32,16,16,1024]{3,2,1,0:T(8,128)(2,1)}), bf16[32,16,16,1024]{3,2,1,0:T(8,128)(2,1)}, u32[]{:S(2)}, u32[]{:S(2)}) async-start(bf16[32,16,16,1024]{3,2,1,0:T(8,128)(2,1)} %bitcast.143), calls=%async_computation | async-start | bytes 33554432 | tf_op jit(solution)/shard_map/all_to_all | solution.py:130
  146.7 33.9 %all-gather.2.cloned.1.call-start = ((), (), s32[]{:S(2)}) async-start(), calls=%async_computation.6 | async-start | bytes 1310720 | tf_op jit(solution)/shard_map/all_gather | solution.py:112
  359.9 255.5 %all-to-all-start.5 = ((bf16[128,2,2880]{2,1,0:T(2,128)(2,1)}), bf16[128,2,2880]{2,1,0:T(2,128)(2,1)}, u32[]{:S(2)}, u32[]{:S(2)}) async-start(bf16[128,2,2880]{2,1,0:T(2,128)(2,1)} %reshape.326), calls=%async_computation.5 | async-start | bytes 3014656 | tf_op jit(solution)/shard_map/all_to_all | solution.py:214
  393.1 5.5 copy-start.4
  401.4 7.9 %copy-start.2 = (f32[8,4,4,8,4096]{4,3,2,1,0:T(8,128)}, f32[8,4,4,8,4096]{4,3,2,1,0:T(8,128)S(1)}, u32[]{:S(2)}) copy-start(f32[8,4,4,8,4096]{4,3,2,1,0:T(8,128)S(1)} %get-tuple-element.156) | copy-start | bytes 50331652 | tf_op jit(solution)/shard_map/while
  411.4 9.3 %copy-start.5 = (bf16[8,4,4,4096]{3,2,1,0:T(4,128)(2,1)S(1)}, bf16[8,4,4,4096]{3,2,1,0:T(4,128)(2,1)}, u32[]{:S(2)}) copy-start(bf16[8,4,4,4096]{3,2,1,0:T(4,128)(2,1)} %copy-done.4) | copy-start | bytes 3145732 | tf_op jit(solution)/shard_map/while
  420.7 5.5 copy-start.4
  429.0 7.9 %copy-start.2 = (f32[8,4,4,8,4096]{4,3,2,1,0:T(8,128)}, f32[8,4,4,8,4096]{4,3,2,1,0:T(8,128)S(1)}, u32[]{:S(2)}) copy-start(f32[8,4,4,8,4096]{4,3,2,1,0:T(8,128)S(1)} %get-tuple-element.156) | copy-start | bytes 50331652 | tf_op jit(solution)/shard_map/while
  439.0 9.3 %copy-start.5 = (bf16[8,4,4,4096]{3,2,1,0:T(4,128)(2,1)S(1)}, bf16[8,4,4,4096]{3,2,1,0:T(4,128)(2,1)}, u32[]{:S(2)}) copy-start(bf16[8,4,4,4096]{3,2,1,0:T(4,128)(2,1)} %copy-done.4) | copy-start | bytes 3145732 | tf_op jit(solution)/shard_map/while
  448.2 5.5 copy-start.4
  456.6 7.9 %copy-start.2 = (f32[8,4,4,8,4096]{4,3,2,1,0:T(8,128)}, f32[8,4,4,8,4096]{4,3,2,1,0:T(8,128)S(1)}, u32[]{:S(2)}) copy-start(f32[8,4,4,8,4096]{4,3,2,1,0:T(8,128)S(1)} %get-tuple-element.156) | copy-start | bytes 50331652 | tf_op jit(solution)/shard_map/while
  466.6 9.3 %copy-start.5 = (bf16[8,4,4,4096]{3,2,1,0:T(4,128)(2,1)S(1)}, bf16[8,4,4,4096]{3,2,1,0:T(4,128)(2,1)}, u32[]{:S(2)}) copy-start(bf16[8,4,4,4096]{3,2,1,0:T(4,128)(2,1)} %copy-done.4) | copy-start | bytes 3145732 | tf_op jit(solution)/shard_map/while
  475.8 5.5 copy-start.4
  484.2 7.9 %copy-start.2 = (f32[8,4,4,8,4096]{4,3,2,1,0:T(8,128)}, f32[8,4,4,8,4096]{4,3,2,1,0:T(8,128)S(1)}, u32[]{:S(2)}) copy-start(f32[8,4,4,8,4096]{4,3,2,1,0:T(8,128)S(1)} %get-tuple-element.156) | copy-start | bytes 50331652 | tf_op jit(solution)/shard_map/while
  494.2 9.3 %copy-start.5 = (bf16[8,4,4,4096]{3,2,1,0:T(4,128)(2,1)S(1)}, bf16[8,4,4,4096]{3,2,1,0:T(4,128)(2,1)}, u32[]{:S(2)}) copy-start(bf16[8,4,4,4096]{3,2,1,0:T(4,128)(2,1)} %copy-done.4) | copy-start | bytes 3145732 | tf_op jit(solution)/shard_map/while
  503.4 5.5 copy-start.4
  511.8 7.9 %copy-start.2 = (f32[8,4,4,8,4096]{4,3,2,1,0:T(8,128)}, f32[8,4,4,8,4096]{4,3,2,1,0:T(8,128)S(1)}, u32[]{:S(2)}) copy-start(f32[8,4,4,8,4096]{4,3,2,1,0:T(8,128)S(1)} %get-tuple-element.156) | copy-start | bytes 50331652 | tf_op jit(solution)/shard_map/while
  521.8 9.3 %copy-start.5 = (bf16[8,4,4,4096]{3,2,1,0:T(4,128)(2,1)S(1)}, bf16[8,4,4,4096]{3,2,1,0:T(4,128)(2,1)}, u32[]{:S(2)}) copy-start(bf16[8,4,4,4096]{3,2,1,0:T(4,128)(2,1)} %copy-done.4) | copy-start | bytes 3145732 | tf_op jit(solution)/shard_map/while
  531.0 5.5 copy-start.4
  539.4 7.9 %copy-start.2 = (f32[8,4,4,8,4096]{4,3,2,1,0:T(8,128)}, f32[8,4,4,8,4096]{4,3,2,1,0:T(8,128)S(1)}, u32[]{:S(2)}) copy-start(f32[8,4,4,8,4096]{4,3,2,1,0:T(8,128)S(1)} %get-tuple-element.156) | copy-start | bytes 50331652 | tf_op jit(solution)/shard_map/while
  549.3 9.3 %copy-start.5 = (bf16[8,4,4,4096]{3,2,1,0:T(4,128)(2,1)S(1)}, bf16[8,4,4,4096]{3,2,1,0:T(4,128)(2,1)}, u32[]{:S(2)}) copy-start(bf16[8,4,4,4096]{3,2,1,0:T(4,128)(2,1)} %copy-done.4) | copy-start | bytes 3145732 | tf_op jit(solution)/shard_map/while
  558.6 5.5 copy-start.4
  567.0 7.9 %copy-start.2 = (f32[8,4,4,8,4096]{4,3,2,1,0:T(8,128)}, f32[8,4,4,8,4096]{4,3,2,1,0:T(8,128)S(1)}, u32[]{:S(2)}) copy-start(f32[8,4,4,8,4096]{4,3,2,1,0:T(8,128)S(1)} %get-tuple-element.156) | copy-start | bytes 50331652 | tf_op jit(solution)/shard_map/while
  576.9 9.3 %copy-start.5 = (bf16[8,4,4,4096]{3,2,1,0:T(4,128)(2,1)S(1)}, bf16[8,4,4,4096]{3,2,1,0:T(4,128)(2,1)}, u32[]{:S(2)}) copy-start(bf16[8,4,4,4096]{3,2,1,0:T(4,128)(2,1)} %copy-done.4) | copy-start | bytes 3145732 | tf_op jit(solution)/shard_map/while
  586.2 5.5 copy-start.4
  594.6 7.9 %copy-start.2 = (f32[8,4,4,8,4096]{4,3,2,1,0:T(8,128)}, f32[8,4,4,8,4096]{4,3,2,1,0:T(8,128)S(1)}, u32[]{:S(2)}) copy-start(f32[8,4,4,8,4096]{4,3,2,1,0:T(8,128)S(1)} %get-tuple-element.156) | copy-start | bytes 50331652 | tf_op jit(solution)/shard_map/while
  604.5 9.3 %copy-start.5 = (bf16[8,4,4,4096]{3,2,1,0:T(4,128)(2,1)S(1)}, bf16[8,4,4,4096]{3,2,1,0:T(4,128)(2,1)}, u32[]{:S(2)}) copy-start(bf16[8,4,4,4096]{3,2,1,0:T(4,128)(2,1)} %copy-done.4) | copy-start | bytes 3145732 | tf_op jit(solution)/shard_map/while
  613.8 24.0 %copy-start.9 = (bf16[1,8,4,4096]{3,2,1,0:T(4,128)(2,1)S(1)}, bf16[1,8,4,4096]{3,2,1,0:T(4,128)(2,1)}, u32[]{:S(2)}) copy-start(bf16[1,8,4,4096]{3,2,1,0:T(4,128)(2,1)} %param.15) | copy-start | bytes 786436
  615.4 9.1 %all-to-all-start.2 = ((f32[4,1,2048]{2,1,0:T(1,128)}), f32[4,1,2048]{2,1,0:T(1,128)S(1)}, u32[]{:S(2)}, u32[]{:S(2)}) async-start(f32[4,1,2048]{2,1,0:T(1,128)} %reshape.378), calls=%async_computation.2 | async-start | bytes 65536 | tf_op jit(solution)/shard_map/all_to_all | solution.py:151
  624.5 8.7 %all-to-all-start.3 = ((f32[4,1,2048]{2,1,0:T(1,128)}), f32[4,1,2048]{2,1,0:T(1,128)S(1)}, u32[]{:S(2)}, u32[]{:S(2)}) async-start(f32[4,1,2048]{2,1,0:T(1,128)} %reshape.380), calls=%async_computation.3 | async-start | bytes 65536 | tf_op jit(solution)/shard_map/all_to_all | solution.py:158
  633.2 31.3 %all-to-all-start.1 = ((f32[4,8,4,4096]{3,2,1,0:T(4,128)}), f32[4,8,4,4096]{3,2,1,0:T(4,128)}, u32[]{:S(2)}, u32[]{:S(2)}) async-start(f32[4,8,4,4096]{3,2,1,0:T(4,128)} %bitcast.148), calls=%async_computation.1 | async-start | bytes 4194304 | tf_op jit(solution)/shard_map/all_to_all | solution.py:165
  638.4 4.4 copy-start.12
  638.4 4.5 copy-start.3
  642.9 7.5 %copy-start.13 = (f32[64]{0:T(128)S(1)}, f32[64]{0:T(128)}, u32[]{:S(2)}) copy-start(f32[64]{0:T(128)} %param.21) | copy-start | bytes 772
  660.7 7.6 %copy-start.1 = (bf16[1,24,16,1024]{3,2,1,0:T(8,128)(2,1)S(1)}, bf16[1,24,16,1024]{3,2,1,0:T(8,128)(2,1)}, u32[]{:S(2)}) copy-start(bf16[1,24,16,1024]{3,2,1,0:T(8,128)(2,1)} %param.17) | copy-start | bytes 2359300
  664.5 2.9 copy-start.6
  664.5 2.9 copy-start.7
Sparse Core Ops, SparseCore 0:
  149.7 25.4 all-gather.1
where the time goes:
time: 684 us; the launch traced here: 675 us
  local copies, waits for them, and re-layouts  215 us (31%)
  waiting for transfers between devices  186 us (27%)
  other arithmetic  111 us (16%)
  matrix products  111 us (16%)
  starting transfers between devices  36.8 us (5%)
  between operations  14.8 us (2%)
    all_to_all x1, waiting for transfers between devices, per_device(): lax.all_to_all(outgoing, 'ep', split_axis=0, concat_axis=0, tiled=True)  177 us
    reduce_sum x9, other arithmetic, softmax_parts(): totals = jnp.sum(weights_full, axis=-1)  67.8 us
    dot_general x8, matrix products, shared_scores(): jnp.einsum('psvgk,kvd->psvgd', rounded, value_head_rows, preferred_elemen...  63 us
    slice x8, local copies, waits for them, and re-layouts, shared_scores(): key_value_table[:, split_point:]  41.2 us
    unnamed x39, local copies, waits for them, and re-layouts  37 us
    another operation x4, other arithmetic  32.4 us
    scatter x1, local copies, waits for them, and re-layouts, per_device(): jnp.zeros((experts_all, slots_per, D), jnp.bfloat16).at[chosen, expert_rank]  25.7 us
    dot_general x8, matrix products, shared_scores(): jnp.einsum('psvgd,kvd->psvgk', query_head_rows, key_head_rows, preferred_...  23 us
  transfers between devices with their start and end apart: 7, of which 3 were waited for; matrix products, arithmetic and copies ran while one was open for 59% of the time, Pallas kernels for 0%

commit v1 on v0

v1 whole, which is shorter than its diff:
```python
import functools

import jax
import jax.numpy as jnp
from jax import lax
from jax.experimental import pallas as pl
from jax.experimental.pallas import tpu as pltpu
from jax.sharding import PartitionSpec as P

D = 2880
QUERY_HEADS = 64
KEY_VALUE_HEADS = 8
GROUP = QUERY_HEADS // KEY_VALUE_HEADS
HEAD_WIDTH = 64
TOPK = 4
HID = 1440
SCORED_STEPS = 4
PAGE_TOKENS = 16
NPS = 256
PAGES = 24
PROMPTS = 8
N_SEQ = 4
N_EP = 32
ROWS = PROMPTS * SCORED_STEPS
HEAD_COLUMNS = GROUP * HEAD_WIDTH
NEGATIVE = -1e30
FLOOR = -1e29
EPSILON = 1e-05
MESH = pl.DeviceIdType.MESH
F32 = jnp.float32
BF16 = jnp.bfloat16
HIGHEST = lax.Precision.HIGHEST


def place():
    y = lax.axis_index("seq")
    ep = lax.axis_index("ep")
    return y, lax.div(ep, 8), lax.rem(lax.div(ep, 2), 4), lax.rem(ep, 2)


def device(y, z, x, c):
    return (y, z * 8 + x * 2 + c)


def head_of(y, x):
    return lax.div(y, 2) * 4 + x


def nt(a, b, precision=None):
    return lax.dot_general(
        a, b, (((1,), (1,)), ((), ())), preferred_element_type=F32, precision=precision
    )


def nn(a, b, precision=None):
    return lax.dot_general(
        a, b, (((1,), (0,)), ((), ())), preferred_element_type=F32, precision=precision
    )


def iota(shape, axis):
    return lax.broadcasted_iota(jnp.int32, shape, axis)


def exchange_kernel(
    q_ref, f_ref, page_ref, table_ref, count_ref,
    q_all, f_all, pool, tables, counts,
    relay, f_relay,
    q_send, q_recv, f_send, f_recv, a_send, a_recv, z_send, z_recv, c_send, c_recv,
    i_send, i_recv, local,
):
    y, z, x, c = place()
    mate = 3 - y

    def at(dy, dx):
        return device(lax.rem(y + dy, 4), z, lax.rem(x + dx, 4), c)

    plane = [(dy, dx) for dy in range(4) for dx in range(4) if (dy, dx) != (0, 0)]
    up = device(y, lax.rem(z + 1, 4), x, c)
    down = device(y, lax.rem(z + 3, 4), x, c)
    twin = device(y, z, x, 1 - c)

    barrier = pltpu.get_barrier_semaphore()
    for peer in [at(dy, dx) for dy, dx in plane] + [up, down, twin]:
        pl.semaphore_signal(barrier, inc=1, device_id=peer, device_id_type=MESH)

    for h in range(KEY_VALUE_HEADS):
        low, high = h * HEAD_WIDTH, (h + 1) * HEAD_WIDTH
        split = KEY_VALUE_HEADS * HEAD_WIDTH
        rows = jnp.concatenate(
            [page_ref[:, low:high], page_ref[:, split + low : split + high]], axis=1
        )
        relay[h] = rows.reshape(PAGES, PAGE_TOKENS, 2 * HEAD_WIDTH)
        f_relay[h] = jnp.concatenate(
            [f_ref[:, low:high], f_ref[:, split + low : split + high]], axis=1
        )
    pl.semaphore_wait(barrier, len(plane) + 3)

    def spot(segment_slot, zz, xx, cc):
        return pool.at[segment_slot, pl.ds((zz * 8 + xx * 2 + cc) * PAGES, PAGES)]

    order = [(0, 0), (0, 1), (0, 3), (1, 0), (1, 1), (1, 3), (0, 2), (1, 2)]
    first = []
    for n, (p, dx) in enumerate(order):
        yy = y if p == 0 else mate
        xx = lax.rem(x + dx, 4)
        target = spot(lax.div(y, 2), z, x, c)
        source = relay.at[head_of(yy, xx)]
        if (p, dx) == (0, 0):
            copy = pltpu.make_async_copy(source, target, local.at[0])
        else:
            copy = pltpu.make_async_remote_copy(
                source, target, a_send.at[n], a_recv.at[n],
                device_id=device(yy, z, xx, c), device_id_type=MESH,
            )
        copy.start()
        first.append(copy)

    small = []
    mine = pltpu.make_async_copy(table_ref, tables.at[lax.div(y, 2)], local.at[1])
    mine.start()
    small.append(mine)
    mine = pltpu.make_async_copy(count_ref, counts.at[x], local.at[2])
    mine.start()
    small.append(mine)
    other = pltpu.make_async_remote_copy(
        table_ref, tables.at[lax.div(y, 2)], i_send.at[0], i_recv.at[0],
        device_id=device(mate, z, x, c), device_id_type=MESH,
    )
    other.start()
    small.append(other)
    for dx in range(1, 4):
        other = pltpu.make_async_remote_copy(
            count_ref, counts.at[x], i_send.at[dx], i_recv.at[dx],
            device_id=at(0, dx), device_id_type=MESH,
        )
        other.start()
        small.append(other)

    for dy in range(4):
        for dx in range(4):
            n = dy * 4 + dx
            h = head_of(lax.rem(y + dy, 4), lax.rem(x + dx, 4))
            q_source = q_ref.at[:, pl.ds(pl.multiple_of(h * HEAD_COLUMNS, HEAD_COLUMNS), HEAD_COLUMNS)]
            f_source = f_relay.at[h]
            slot = x * 4 + y
            if n == 0:
                copies = [
                    pltpu.make_async_copy(q_source, q_all.at[slot], local.at[3]),
                    pltpu.make_async_copy(f_source, f_all.at[slot], local.at[4]),
                ]
            else:
                copies = [
                    pltpu.make_async_remote_copy(
                        q_source, q_all.at[slot], q_send.at[n], q_recv.at[n],
                        device_id=at(dy, dx), device_id_type=MESH,
                    ),
                    pltpu.make_async_remote_copy(
                        f_source, f_all.at[slot], f_send.at[n], f_recv.at[n],
                        device_id=at(dy, dx), device_id_type=MESH,
                    ),
                ]
            for copy in copies:
                copy.start()
            small.extend(copies)

    def chunk(n):
        p, dx = order[n]
        yy = y if p == 0 else mate
        return lax.div(yy, 2), lax.rem(x - dx + 4, 4)

    def pass_on(n, zz, way, peer):
        segment_slot, xx = chunk(n)
        block = spot(segment_slot, zz, xx, c)
        sends, recvs = (c_send, c_recv) if way >= 3 else (z_send, z_recv)
        number = (way - 3 if way >= 3 else way) * 8 + n
        copy = pltpu.make_async_remote_copy(
            block, block, sends.at[number], recvs.at[number],
            device_id=peer, device_id_type=MESH,
        )
        copy.start()
        return copy

    upward, downward, further, across = [], [], [], []
    for n in range(8):
        if n == 0:
            first[n].wait()
        else:
            first[n].wait_recv()
        upward.append(pass_on(n, z, 0, up))
        downward.append(pass_on(n, z, 1, down))
        across.append(pass_on(n, z, 3, twin))
    for n in range(8):
        upward[n].wait_recv()
        if n % 2 == 0:
            further.append(pass_on(n, lax.rem(z + 3, 4), 2, up))
        across.append(pass_on(n, lax.rem(z + 3, 4), 4, twin))
        downward[n].wait_recv()
        if n % 2 == 1:
            further.append(pass_on(n, lax.rem(z + 1, 4), 2, down))
        across.append(pass_on(n, lax.rem(z + 1, 4), 5, twin))
    for n in range(8):
        further[n].wait_recv()
        across.append(pass_on(n, lax.rem(z + 2, 4), 6, twin))
    for copy in across:
        copy.wait()
    for copy in first[1:] + upward + downward + further:
        copy.wait_send()
    for copy in small:
        copy.wait()


def exchange(queries, fresh, pages, table, count):
    vmem = pl.BlockSpec(memory_space=pltpu.VMEM)
    anywhere = pl.BlockSpec(memory_space=pl.ANY)
    dma = pltpu.SemaphoreType.DMA
    return pl.pallas_call(
        exchange_kernel,
        out_shape=(
            jax.ShapeDtypeStruct((16, ROWS, HEAD_COLUMNS), BF16),
            jax.ShapeDtypeStruct((16, ROWS, 2 * HEAD_WIDTH), BF16),
            jax.ShapeDtypeStruct((2, N_EP * PAGES, PAGE_TOKENS, 2 * HEAD_WIDTH), BF16),
            jax.ShapeDtypeStruct((2, 8, 128), jnp.int32),
            jax.ShapeDtypeStruct((4, 8, 128), jnp.int32),
        ),
        in_specs=[vmem] * 5,
        out_specs=(anywhere,) * 5,
        scratch_shapes=[
            pltpu.VMEM((KEY_VALUE_HEADS, PAGES, PAGE_TOKENS, 2 * HEAD_WIDTH), BF16),
            pltpu.VMEM((KEY_VALUE_HEADS, ROWS, 2 * HEAD_WIDTH), BF16),
            dma((16,)), dma((16,)), dma((16,)), dma((16,)), dma((8,)), dma((8,)),
            dma((24,)), dma((24,)), dma((32,)), dma((32,)), dma((4,)), dma((4,)), dma((5,)),
        ],
        compiler_params=pltpu.CompilerParams(
            collective_id=1, has_side_effects=True, vmem_limit_bytes=16 << 20
        ),
        name="exchange",
    )(queries, fresh, pages, table, count)


BK = 1024
HALF = BK // 2
GK = 512
KEYS = 2 * NPS * PAGE_TOKENS
CHUNKS = 4
COLS = 256
VROWS = 80


def score_kernel(
    tables, counts, sinks, q_all, f_all, pool, o_ref, lse_ref,
    kv, vt, qs, f_sorted, limit_ref, m_ref, acc, sorted_out, s0, s1,
):
    y = lax.axis_index("seq")
    outer_pair = jnp.logical_or(y == 0, y == 3)
    pick = (iota((VROWS, 128), 0) + HEAD_WIDTH == iota((VROWS, 128), 1)).astype(BF16)
    sink_row = sinks[0:1, :]

    def values_of(rows):
        moved = nt(pick, rows)
        return jnp.where(iota(moved.shape, 0) >= HEAD_WIDTH, 1.0, moved).astype(BF16)

    def unit(e, carry):
        c = counts[e][0:1, :].astype(F32)
        n_row = jnp.where(
            outer_pair,
            jnp.minimum(c, 256.0) + jnp.maximum(c - 768.0, 0.0),
            jnp.clip(c - 256.0, 0.0, 512.0),
        )
        i0 = iota((128, 128), 0)
        i1 = iota((128, 128), 1)
        n_col = jnp.sum(jnp.where(i0 == i1, n_row, 0.0), axis=1, keepdims=True)
        ahead = jnp.logical_or(n_col > n_row, jnp.logical_and(n_col == n_row, i0 < i1))
        pos_row = jnp.sum(jnp.where(ahead, 1.0, 0.0), axis=0, keepdims=True)
        behind = jnp.logical_or(n_row > n_col, jnp.logical_and(n_col == n_row, i1 < i0))
        pos_col = jnp.sum(jnp.where(behind, 1.0, 0.0), axis=1, keepdims=True)
        perm = (pos_row == i0.astype(F32)).astype(BF16)
        perm_t = (pos_col == i1.astype(F32)).astype(BF16)
        q_sorted = (nn(perm, q_all[pl.ds(e * 4, 4)].reshape(128, HEAD_COLUMNS)) * 0.125).astype(BF16)
        f_sorted[...] = nn(perm, f_all[pl.ds(e * 4, 4)].reshape(128, 128)).astype(BF16)
        none = jnp.zeros((ROWS, HEAD_WIDTH), BF16)
        lane_row = lax.rem(iota((128, COLS), 1), ROWS).astype(F32)
        longest = []
        for ch in range(CHUNKS):
            for g in range(GROUP):
                piece = q_sorted[ch * ROWS : (ch + 1) * ROWS, g * HEAD_WIDTH : (g + 1) * HEAD_WIDTH]
                qs[ch, g * ROWS : (g + 1) * ROWS, :] = jnp.concatenate([piece, none], axis=1)
            member = pos_col == lane_row + float(ch * ROWS)
            limit = jnp.sum(jnp.where(member, n_col, 0.0), axis=0, keepdims=True) * PAGE_TOKENS
            limit_ref[ch] = jnp.broadcast_to(limit, (8, COLS))
            longest.append(jnp.max(limit).astype(jnp.int32))
            rows = f_sorted[ch * ROWS : (ch + 1) * ROWS, :]
            s = nt(rows, qs[ch])
            ki = iota((ROWS, COLS), 0)
            ri = lax.rem(iota((ROWS, COLS), 1), ROWS)
            seen = jnp.logical_and(
                lax.div(ki, SCORED_STEPS) == lax.div(ri, SCORED_STEPS), ki <= ri
            )
            s = jnp.where(seen, s, NEGATIVE)
            m0 = jnp.maximum(jnp.max(s, axis=0, keepdims=True), sink_row)
            p = jnp.exp(s - m0).astype(BF16)
            start = nn(values_of(rows), p)
            start = start + jnp.where(
                iota((VROWS, COLS), 0) >= HEAD_WIDTH, jnp.exp(sink_row - m0), 0.0
            )
            m_ref[ch] = jnp.broadcast_to(jnp.where(outer_pair, m0, FLOOR), (8, COLS))
            acc[ch] = jnp.where(outer_pair, start, 0.0)

        def gather(kb, carry):
            p0 = kb * (GK // PAGE_TOKENS)
            ss = lax.div(p0, NPS)
            within = lax.rem(p0, NPS)
            row = e * 2 + lax.div(within, 128)
            lane = lax.rem(within, 128)
            base = pl.multiple_of(kb * GK, GK)
            rows = [
                pool[tables[ss, row, lane + i] + ss * (N_EP * PAGES)]
                for i in range(GK // PAGE_TOKENS)
            ]
            found = jnp.concatenate(rows, axis=0)
            kv[pl.ds(base, GK), :] = found
            vt[kb] = values_of(found)
            return carry

        lax.fori_loop(0, lax.div(longest[0] + (BK - 1), BK) * (BK // GK), gather, 0)

        key = iota((HALF, COLS), 0).astype(F32)
        for ch in range(CHUNKS):
            q = qs[ch]
            limit = limit_ref[ch][0:1, :]

            def scores(start):
                return nt(kv[pl.ds(pl.multiple_of(start, HALF), HALF), :], q)

            def absorb(s, start, state):
                before, total = state
                s = jnp.where(key < limit - start.astype(F32), s, NEGATIVE)
                after = jnp.maximum(before, jnp.max(s, axis=0, keepdims=True))
                p = jnp.exp(s - after).astype(BF16)
                values = vt[lax.div(start, GK)]
                return after, total * jnp.exp(before - after) + nn(values, p)

            def block(kb, state):
                start = kb * BK
                s1[...] = scores(start + HALF)
                state = absorb(s0[...], start, state)
                s0[...] = scores(jnp.minimum(start + BK, KEYS - HALF))
                return absorb(s1[...], start + HALF, state)

            s0[...] = scores(0)
            state = (m_ref[ch][0:1, :], acc[ch])
            state = lax.fori_loop(0, lax.div(longest[ch] + (BK - 1), BK), block, state)
            m_ref[ch] = jnp.broadcast_to(state[0], (8, COLS))
            acc[ch] = state[1]

        lse = jnp.zeros((8, 128), F32)
        for ch in range(CHUNKS):
            total = jnp.maximum(acc[ch][HEAD_WIDTH : HEAD_WIDTH + 1, :], 1e-30)
            out = acc[ch][0:HEAD_WIDTH, :] / total
            padded = jnp.concatenate([out, jnp.zeros_like(out)], axis=0)
            turned = padded.T.astype(BF16)
            for g in range(GROUP):
                sorted_out[ch * ROWS : (ch + 1) * ROWS, g * HEAD_WIDTH : (g + 1) * HEAD_WIDTH] = (
                    turned[g * ROWS : (g + 1) * ROWS, 0:HEAD_WIDTH]
                )
            row = m_ref[ch][0:1, :] + jnp.log(total)
            mine = lax.div(iota((8, COLS), 1), ROWS) == iota((8, COLS), 0)
            member = (pos_col == lane_row + float(ch * ROWS)).astype(F32)
            lse = lse + nt(jnp.where(mine, row, 0.0), member, HIGHEST)
        lse_ref[e] = lse
        o_ref[e] = nn(perm_t, sorted_out[...]).astype(BF16)
        return carry

    lax.fori_loop(0, 4, unit, 0)


def score(tables, counts, sinks, q_all, f_all, pool):
    vmem = pl.BlockSpec(memory_space=pltpu.VMEM)
    return pl.pallas_call(
        score_kernel,
        out_shape=(
            jax.ShapeDtypeStruct((4, 128, HEAD_COLUMNS), BF16),
            jax.ShapeDtypeStruct((4, 8, 128), F32),
        ),
        in_specs=[pl.BlockSpec(memory_space=pltpu.SMEM)] + [vmem] * 5,
        out_specs=(vmem, vmem),
        scratch_shapes=[
            pltpu.VMEM((KEYS, 128), BF16),
            pltpu.VMEM((KEYS // GK, VROWS, GK), BF16),
            pltpu.VMEM((CHUNKS, COLS, 128), BF16),
            pltpu.VMEM((128, 128), BF16),
            pltpu.VMEM((CHUNKS, 8, COLS), F32),
            pltpu.VMEM((CHUNKS, 8, COLS), F32),
            pltpu.VMEM((CHUNKS, VROWS, COLS), F32),
            pltpu.VMEM((128, HEAD_COLUMNS), BF16),
            pltpu.VMEM((HALF, COLS), F32),
            pltpu.VMEM((HALF, COLS), F32),
        ],
        compiler_params=pltpu.CompilerParams(vmem_limit_bytes=40 << 20),
        cost_estimate=pl.CostEstimate(
            flops=25_000_000_000, bytes_accessed=8_000_000, transcendentals=20_000_000
        ),
        name="score",
    )(tables, counts, sinks, q_all, f_all, pool)


def merge_kernel(o_ref, lse_ref, out_ref, o_all, lse_all, o_send, o_recv, l_send, l_recv, local):
    y, z, x, c = place()

    def at(dy, dx):
        return device(lax.rem(y + dy, 4), z, lax.rem(x + dx, 4), c)

    plane = [(dy, dx) for dy in range(4) for dx in range(4) if (dy, dx) != (0, 0)]
    barrier = pltpu.get_barrier_semaphore()
    for dy, dx in plane:
        pl.semaphore_signal(barrier, inc=1, device_id=at(dy, dx), device_id_type=MESH)
    pl.semaphore_wait(barrier, len(plane))
    inner_pair = jnp.logical_or(y == 1, y == 2).astype(jnp.int32)
    slot = inner_pair * 8 + head_of(y, x)
    copies = []
    for dy in range(4):
        for dx in range(4):
            n = dy * 4 + dx
            q = lax.rem(y + dy, 4)
            e = lax.rem(x + dx, 4)
            o_source = o_ref.at[e, pl.ds(pl.multiple_of(q * ROWS, ROWS), ROWS)]
            if n == 0:
                pair = [
                    pltpu.make_async_copy(o_source, o_all.at[slot], local.at[0]),
                    pltpu.make_async_copy(lse_ref.at[e], lse_all.at[slot], local.at[1]),
                ]
            else:
                pair = [
                    pltpu.make_async_remote_copy(
                        o_source, o_all.at[slot], o_send.at[n], o_recv.at[n],
                        device_id=at(dy, dx), device_id_type=MESH,
                    ),
                    pltpu.make_async_remote_copy(
                        lse_ref.at[e], lse_all.at[slot], l_send.at[n], l_recv.at[n],
                        device_id=at(dy, dx), device_id_type=MESH,
                    ),
                ]
            for copy in pair:
                copy.start()
            copies.extend(pair)
    for copy in copies:
        copy.wait()
    mine = (iota((ROWS, 128), 1) == iota((ROWS, 128), 0) + y * ROWS).astype(F32)
    logs = nt(mine, lse_all[...].reshape(128, 128), HIGHEST)
    log0, log1 = logs[:, :64], logs[:, 64:]
    top = jnp.maximum(log0, log1)
    w0, w1 = jnp.exp(log0 - top), jnp.exp(log1 - top)
    share0, share1 = w0 / (w0 + w1), w1 / (w0 + w1)
    parts = []
    for share in (share0, share1):
        high = share.astype(BF16)
        parts.append((high, (share - high.astype(F32)).astype(BF16)))
    for h in range(KEY_VALUE_HEADS):
        shape = (64, HEAD_COLUMNS)
        spread = (iota(shape, 0) == lax.div(iota(shape, 1), HEAD_WIDTH) + h * GROUP).astype(BF16)
        wide = [nn(high, spread) + nn(low, spread) for high, low in parts]
        result = wide[0] * o_all[h].astype(F32) + wide[1] * o_all[8 + h].astype(F32)
        out_ref[:, h * HEAD_COLUMNS : (h + 1) * HEAD_COLUMNS] = result.astype(BF16)


def merge(o, lse):
    vmem = pl.BlockSpec(memory_space=pltpu.VMEM)
    dma = pltpu.SemaphoreType.DMA
    return pl.pallas_call(
        merge_kernel,
        out_shape=jax.ShapeDtypeStruct((ROWS, QUERY_HEADS * HEAD_WIDTH), BF16),
        in_specs=[vmem, vmem],
        out_specs=vmem,
        scratch_shapes=[
            pltpu.VMEM((16, ROWS, HEAD_COLUMNS), BF16),
            pltpu.VMEM((16, 8, 128), F32),
            dma((16,)), dma((16,)), dma((16,)), dma((16,)), dma((2,)),
        ],
        compiler_params=pltpu.CompilerParams(
            collective_id=2, has_side_effects=True, vmem_limit_bytes=16 << 20
        ),
        name="merge",
    )(o, lse)


def per_device(
    queries, fresh_key_values, key_value_pages, page_owner, page_slot, page_count, sinks,
    hidden, norm_gain, expert_ids, gate_prob, gate_up, down_proj,
):
    y, z, x, c = place()

    flat_hidden = hidden.reshape(ROWS, D).astype(F32)
    meansq = jnp.mean(flat_hidden * flat_hidden, axis=-1, keepdims=True)
    normed = (flat_hidden * lax.rsqrt(meansq + EPSILON) * norm_gain).astype(BF16)
    chosen = expert_ids.reshape(ROWS * TOPK)
    number = jnp.arange(ROWS * TOPK, dtype=jnp.int32)
    same = jnp.logical_and(chosen[:, None] == chosen[None, :], number[None, :] < number[:, None])
    rank = jnp.sum(same.astype(jnp.int32), axis=1)
    slots = (chosen * 2 + rank).reshape(ROWS, TOPK)
    hit = slots[None, :, :] == jnp.arange(256, dtype=jnp.int32)[:, None, None]
    spread = jnp.any(hit, axis=-1).astype(BF16)
    buffer = jnp.dot(spread, normed, preferred_element_type=F32).astype(BF16)
    weights = jnp.sum(
        jnp.where(
            slots[:, :, None] == jnp.arange(256, dtype=jnp.int32)[None, None, :],
            gate_prob.reshape(ROWS, TOPK, 1),
            0.0,
        ),
        axis=1,
    )
    arrived = lax.all_to_all(buffer, ("seq", "ep"), split_axis=0, concat_axis=0, tiled=True)

    index = (page_owner * PAGES + page_slot).reshape(4, 4, 2, NPS)
    index = lax.dynamic_index_in_dim(index, z, 0, keepdims=False)
    index = lax.dynamic_index_in_dim(index, c, 1, keepdims=False)
    table = index.reshape(8, 128)
    count = jnp.broadcast_to(jnp.repeat(page_count.reshape(32), 4)[None, :], (8, 128))
    q_all, f_all, pool, tables, counts = exchange(
        queries.reshape(ROWS, QUERY_HEADS * HEAD_WIDTH),
        fresh_key_values.reshape(ROWS, 2 * KEY_VALUE_HEADS * HEAD_WIDTH),
        key_value_pages.reshape(PAGES * PAGE_TOKENS, 2 * KEY_VALUE_HEADS * HEAD_WIDTH),
        table,
        count,
    )
    head_sinks = lax.dynamic_slice_in_dim(sinks, head_of(y, x) * GROUP, GROUP)
    sink_rows = jnp.broadcast_to(jnp.repeat(head_sinks, ROWS)[None, :], (8, COLS))
    o, lse = score(
        tables, counts, sink_rows, q_all, f_all,
        pool.reshape(2 * N_EP * PAGES, PAGE_TOKENS, 2 * HEAD_WIDTH),
    )
    attention = merge(o, lse).reshape(queries.shape)

    projected = jnp.dot(arrived, gate_up[0], preferred_element_type=F32)
    gate, upper = projected[:, :HID], projected[:, HID:]
    active = ((upper + 1.0) * gate * jax.nn.sigmoid(1.702 * gate)).astype(BF16)
    result = jnp.dot(active, down_proj[0], preferred_element_type=F32).astype(BF16)
    returned = lax.all_to_all(result, ("seq", "ep"), split_axis=0, concat_axis=0, tiled=True)
    high = weights.astype(BF16)
    low = (weights - high.astype(F32)).astype(BF16)
    mixture = (
        jnp.dot(high, returned, preferred_element_type=F32)
        + jnp.dot(low, returned, preferred_element_type=F32)
    ).astype(BF16).reshape(hidden.shape)
    return (attention, mixture)


def solution(mesh):
    return jax.shard_map(
        per_device,
        mesh=mesh,
        in_specs=(
            P("seq", "ep", None, None),
            P("seq", "ep", None, None),
            P("seq", "ep", None, None),
            P("seq", None, None),
            P("seq", None, None),
            P(None, "ep"),
            P(),
            P("seq", "ep", None, None),
            P(),
            P("seq", "ep", None, None),
            P("seq", "ep", None, None),
            P(("seq", "ep"), None, None),
            P(("seq", "ep"), None, None),
        ),
        out_specs=(P("seq", "ep", None, None), P("seq", "ep", None, None)),
        check_vma=False,
    )
```

time: 684 us -> 204 us (0.30); the launches traced: 675 us -> 204 us
  local copies, waits for them, and re-layouts: 215 us -> 22.5 us
  waiting for transfers between devices: 186 us -> 0.01 us
  Pallas kernels: 0 us -> 133 us
  other arithmetic: 111 us -> 2.22 us
  matrix products: 111 us -> 24.1 us
  starting transfers between devices: 36.8 us -> 20.9 us
  between operations: 14.8 us -> 0.98 us
    all_to_all x5 -> x1, waiting for transfers between devices: 186 us -> 0.01 us  [per_device(): lax.all_to_all(result, ('seq', 'ep'), split_axis=0, concat_axis=0, tiled=...]
    pallas_call x0 -> x3, Pallas kernels: none -> 133 us  [the longest x1 68.8 us: score(): pl.pallas_call(score_kernel, out_shape=(jax.ShapeDtypeStruct((4, 128, HEA...]
    dot_general x20 -> x5, matrix products: 111 us -> 24.1 us  [the longest x1 12.8 us: per_device(): projected = jnp.dot(arrived, gate_up[0], preferred_element_type=F32)]
    reduce_sum x14 -> x2, other arithmetic: 72.3 us -> 0.28 us  [the longest x1 0.18 us: per_device(): rank = jnp.sum(same.astype(jnp.int32), axis=1)]
    slice x11 -> x0, local copies, waits for them, and re-layouts: 42.7 us -> none  [the longest x8 41.2 us: shared_scores(): key_value_table[:, split_point:]]
    gather x3 -> x0, local copies, waits for them, and re-layouts: 32.8 us -> none  [the longest x1 15.8 us: per_device(): page_rows = incoming[my_owner, my_rank]]
    another operation x5 -> x0, other arithmetic: 32.6 us -> none
    unnamed x39 -> x22, local copies, waits for them, and re-layouts: 37 us -> 6.36 us
  transfers between devices with their start and end apart: 7 -> 2, of which waited for: 3 -> 0; matrix products, arithmetic and copies ran while one was open for 59% -> 2% of each run, Pallas kernels for 0% -> 65%
where the time goes in v1:
time: 204 us
  Pallas kernels  133 us (65%)
  matrix products  24.1 us (12%)
  local copies, waits for them, and re-layouts  22.5 us (11%)
  starting transfers between devices  20.9 us (10%)
  other arithmetic  2.22 us (1%)
    pallas_call x1, Pallas kernels, score(): pl.pallas_call(score_kernel, out_shape=(jax.ShapeDtypeStruct((4, 128, HEA...  68.8 us
    pallas_call x1, Pallas kernels, exchange(): pl.pallas_call(exchange_kernel, out_shape=(jax.ShapeDtypeStruct((16, ROWS...  47.8 us
    pallas_call x1, Pallas kernels, merge(): pl.pallas_call(merge_kernel, out_shape=jax.ShapeDtypeStruct((ROWS, QUERY_...  16.6 us
    dot_general x1, matrix products, per_device(): projected = jnp.dot(arrived, gate_up[0], preferred_element_type=F32)  12.8 us
    all_to_all x1, starting transfers between devices, per_device(): lax.all_to_all(buffer, ('seq', 'ep'), split_axis=0, concat_axis=0, tiled=...  11.6 us
    all_to_all x1, starting transfers between devices, per_device(): lax.all_to_all(result, ('seq', 'ep'), split_axis=0, concat_axis=0, tiled=...  9.29 us
    dot_general x1, matrix products, per_device(): jnp.dot(active, down_proj[0], preferred_element_type=F32).astype(BF16)  9.22 us
    unnamed x22, local copies, waits for them, and re-layouts  6.36 us
  transfers between devices with their start and end apart: 2, of which 0 were waited for; matrix products, arithmetic and copies ran while one was open for 2% of the time, Pallas kernels for 65%

profile of v1, /device:TPU:0, one launch (start us, length us, event | category | flops | bytes accessed | tf_op | source)
XLA Modules:
  0.0 203.8 jit_solution(1990526212259609061)
XLA Ops:
  0.6 0.8 copy.34
  1.4 0.7 broadcast_multiply_fusion
  2.1 1.0 reshape.97
  3.1 1.1 multiply_reduce_fusion
  4.2 0.1 eq.20
  4.3 0.2 convert_reduce_fusion
  4.5 0.1 reduce_sum.30
  4.6 0.1 copy.35
  4.7 0.1 copy.33
  4.8 0.1 mul.67
  4.9 0.1 fusion.16
  5.0 0.1 rsqrt.12
  5.1 1.4 convolution_convert_fusion
  6.5 1.0 copy.37
  7.5 1.5 all_to_all.16
  9.0 0.0 copy-start.5
  9.0 0.0 copy-start.6
  9.0 11.6 %all-to-all-start = ((bf16[128,2,2880]{2,1,0:T(2,128)(2,1)}), bf16[128,2,2880]{2,1,0:T(2,128)(2,1)}, u32[]{:S(2)}, u32[]{:S(2)}) async-start(bf16[128,2,2880]{2,1,0:T(2,128)(2,1)} %all_to_all.16), calls=%async_computation | async-start | bytes 3014656 | tf_op jit(solution)/shard_map/all_to_all | solution.py:511
  20.7 0.0 copy-done.5
  20.7 0.0 copy-done.6
  20.7 0.6 copy.32
  21.4 0.0 copy-start.3
  21.4 0.0 copy-start.4
  21.4 0.0 copy-start.8
  21.4 0.0 copy-start.9
  21.4 0.0 copy-start
  21.4 1.2 reshape.91
  22.7 0.0 copy-done.3
  22.7 0.1 reshape.88.q_ref
  22.7 0.0 copy-done.4
  22.8 0.0 copy-done.8
  22.8 0.1 reshape.93
  22.9 0.1 broadcast_in_dim.40
  23.0 0.1 broadcast_in_dim.41
  23.1 0.0 copy-done.9
  23.1 0.1 dynamic_slice.10
  23.2 0.1 broadcast_in_dim.43
  23.2 0.1 broadcast_in_dim.44
  23.3 0.0 copy-done
  23.3 47.8 %exchange.1 = (bf16[16,32,512]{2,1,0:T(8,128)(2,1)S(1)}, bf16[16,32,128]{2,1,0:T(8,128)(2,1)S(1)}, bf16[2,768,16,128]{3,2,1,0:T(8,128)(2,1)S(1)}, s32[2,8,128]{2,1,0:T(8,128)S(1)}, s32[4,8,128]{2,1,0:T(8,128)S(1)}) custom-call(bf16[32,4096]{1,0:T(8,128)(2,1)S(1)} %reshape.88.q_ref, bf16[32,1024]{1,0:T(8,128)(2,1)S(1)} %reshape.89.f_ref, ...), custom_call_target="tpu_custom_call" | custom-call | tf_op jit(solution)/shard_map/exchange/pallas_call | solution.py:217
  71.2 0.0 copy-start.1
  71.2 2.6 %copy-done.1 = bf16[2,768,16,128]{3,2,1,0:T(8,128)(2,1)} copy-done((bf16[2,768,16,128]{3,2,1,0:T(8,128)(2,1)}, bf16[2,768,16,128]{3,2,1,0:T(8,128)(2,1)S(1)}, u32[]{:S(2)}) %copy-start.1) | copy-done | bytes 6291480
  73.8 0.0 all-to-all-done
  73.8 3.5 %all_to_all.18 = bf16[256,2880]{1,0:T(8,128)(2,1)S(1)} reshape(bf16[128,2,2880]{2,1,0:T(2,128)(2,1)} %all-to-all-done) | data formatting | bytes 2949120 | tf_op jit(solution)/shard_map/all_to_all | solution.py:511
  77.3 12.8 %fusion = f32[256,2880]{0,1:T(8,128)} fusion(bf16[256,2880]{1,0:T(8,128)(2,1)S(1)} %all_to_all.18, bf16[1,2880,2880]{2,1,0:T(8,128)(2,1)} %param.24), kind=kOutput, calls=%fused_computation | convolution fusion | flops 4246732800 | bytes 21012480 | tf_op jit(solution)/shard_map/dot_general | solution.py:533
  90.1 9.2 %fusion.4 = bf16[256,2880]{0,1:T(8,128)(2,1)} fusion(bf16[1,1440,2880]{2,1,0:T(8,128)(2,1)} %param.25, f32[256,2880]{0,1:T(8,128)} %fusion), kind=kOutput, calls=%fused_computation.5 | convolution fusion | flops 2127052800 | bytes 12718080 | tf_op jit(solution)/shard_map/dot_general | solution.py:536
  99.3 1.8 copy.38
  101.1 1.5 all_to_all.19
  102.6 9.3 %all-to-all-start.1 = ((bf16[128,2,2880]{2,1,0:T(2,128)(2,1)}), bf16[128,2,2880]{2,1,0:T(2,128)(2,1)S(1)}, u32[]{:S(2)}, u32[]{:S(2)}) async-start(bf16[128,2,2880]{2,1,0:T(2,128)(2,1)} %all_to_all.19), calls=%async_computation.1 | async-start | bytes 3014656 | tf_op jit(solution)/shard_map/all_to_all | solution.py:537
  111.9 0.0 copy-start.2
  111.9 2.8 %copy-done.2 = bf16[2,768,16,128]{3,2,1,0:T(8,128)(2,1)S(1)} copy-done((bf16[2,768,16,128]{3,2,1,0:T(8,128)(2,1)S(1)}, bf16[2,768,16,128]{3,2,1,0:T(8,128)(2,1)}, u32[]{:S(2)}) %copy-start.2) | copy-done | bytes 6291480
  114.7 0.0 copy-start.7
  114.7 68.8 %score.1 = (bf16[4,128,512]{2,1,0:T(8,128)(2,1)S(1)}, f32[4,8,128]{2,1,0:T(8,128)S(1)}) custom-call(s32[2,8,128]{2,1,0:T(8,128)S(1)} %get-tuple-element.9.tables, s32[4,8,128]{2,1,0:T(8,128)S(1)} %get-tuple-element.10.counts, f32[8,256]{1,0:T(8,128)S(1)} %broadcast_in_dim.45.sinks, bf16[16,32,512]{2,1,0:T(8,128)(2,1)S(1)} %get-tuple-element.11.q_all, ...), custom_call_target="tpu_custom_call" | custom-call | flops 24999999488 | bytes 8000000 | tf_op jit(solution)/shard_map/score/pallas_call | solution.py:379
  183.4 16.6 %merge.1 = bf16[32,4096]{1,0:T(8,128)(2,1)S(1)} custom-call(bf16[4,128,512]{2,1,0:T(8,128)(2,1)S(1)} %get-tuple-element.14.o_ref, f32[4,8,128]{2,1,0:T(8,128)S(1)} %get-tuple-element.15.lse_ref), custom_call_target="tpu_custom_call" | custom-call | tf_op jit(solution)/shard_map/merge/pallas_call | solution.py:469
  200.0 0.8 reshape.95
  200.8 0.0 copy-done.7
  200.8 0.1 copy.36
  200.9 0.1 broadcast_in_dim.46
  201.0 0.1 select_reduce_fusion
  201.1 0.0 all-to-all-done.1
  201.1 1.2 all_to_all.21
  202.3 0.4 fusion.19
  202.7 0.4 fusion.7
  203.1 0.7 reshape.96
  (7 shorter events, 0.1 us)
Async XLA Ops:
  9.0 11.6 %copy-start.5 = (s32[1,4096,2]{1,2,0:T(2,128)S(1)}, s32[1,4096,2]{1,2,0:T(2,128)}, u32[]{:S(2)}) copy-start(s32[1,4096,2]{1,2,0:T(2,128)} %param.17) | copy-start | bytes 98308
  9.0 11.7 %copy-start.6 = (s32[1,4096,2]{1,2,0:T(2,128)S(1)}, s32[1,4096,2]{1,2,0:T(2,128)}, u32[]{:S(2)}) copy-start(s32[1,4096,2]{1,2,0:T(2,128)} %param.16) | copy-start | bytes 98308
  9.0 64.8 %all-to-all-start = ((bf16[128,2,2880]{2,1,0:T(2,128)(2,1)}), bf16[128,2,2880]{2,1,0:T(2,128)(2,1)}, u32[]{:S(2)}, u32[]{:S(2)}) async-start(bf16[128,2,2880]{2,1,0:T(2,128)(2,1)} %all_to_all.16), calls=%async_computation | async-start | bytes 3014656 | tf_op jit(solution)/shard_map/all_to_all | solution.py:511
  21.4 1.3 copy-start.3
  21.4 1.4 copy-start.4
  21.4 1.4 copy-start.8
  21.4 1.7 copy-start.9
  21.4 1.9 copy-start
  71.2 2.7 %copy-start.1 = (bf16[2,768,16,128]{3,2,1,0:T(8,128)(2,1)}, bf16[2,768,16,128]{3,2,1,0:T(8,128)(2,1)S(1)}, u32[]{:S(2)}) copy-start(bf16[2,768,16,128]{3,2,1,0:T(8,128)(2,1)S(1)} %get-tuple-element.13) | copy-start | bytes 18874372
  102.6 98.5 %all-to-all-start.1 = ((bf16[128,2,2880]{2,1,0:T(2,128)(2,1)}), bf16[128,2,2880]{2,1,0:T(2,128)(2,1)S(1)}, u32[]{:S(2)}, u32[]{:S(2)}) async-start(bf16[128,2,2880]{2,1,0:T(2,128)(2,1)} %all_to_all.19), calls=%async_computation.1 | async-start | bytes 3014656 | tf_op jit(solution)/shard_map/all_to_all | solution.py:537
  111.9 2.8 %copy-start.2 = (bf16[2,768,16,128]{3,2,1,0:T(8,128)(2,1)S(1)}, bf16[2,768,16,128]{3,2,1,0:T(8,128)(2,1)}, u32[]{:S(2)}) copy-start(bf16[2,768,16,128]{3,2,1,0:T(8,128)(2,1)} %copy-done.1) | copy-start | bytes 18874372
  114.7 86.2 %copy-start.7 = (f32[1,8,4,4]{1,3,2,0:T(4,128)S(1)}, f32[1,8,4,4]{1,3,2,0:T(4,128)}, u32[]{:S(2)}) copy-start(f32[1,8,4,4]{1,3,2,0:T(4,128)} %param.23) | copy-start | bytes 1540

commit v2 on v1

--- a/solution.py
+++ b/solution.py
@@ -239,58 +239,63 @@
 
 
 BK = 1024
-HALF = BK // 2
-GK = 512
+GK = 2048
 KEYS = 2 * NPS * PAGE_TOKENS
+UNITS = 4
 CHUNKS = 4
 COLS = 256
 VROWS = 80
 
 
+def values_of(rows):
+    pick = (iota((VROWS, 128), 0) + HEAD_WIDTH == iota((VROWS, 128), 1)).astype(BF16)
+    moved = nt(pick, rows)
+    return jnp.where(iota(moved.shape, 0) >= HEAD_WIDTH, 1.0, moved).astype(BF16)
+
+
 def score_kernel(
     tables, counts, sinks, q_all, f_all, pool, o_ref, lse_ref,
-    kv, vt, qs, f_sorted, limit_ref, m_ref, acc, sorted_out, s0, s1,
+    kv, vt, qs, limit_ref, m_ref, acc, sorted_out, s0, s1, lengths,
 ):
     y = lax.axis_index("seq")
     outer_pair = jnp.logical_or(y == 0, y == 3)
-    pick = (iota((VROWS, 128), 0) + HEAD_WIDTH == iota((VROWS, 128), 1)).astype(BF16)
     sink_row = sinks[0:1, :]
-
-    def values_of(rows):
-        moved = nt(pick, rows)
-        return jnp.where(iota(moved.shape, 0) >= HEAD_WIDTH, 1.0, moved).astype(BF16)
-
-    def unit(e, carry):
+    i0 = iota((128, 128), 0)
+    i1 = iota((128, 128), 1)
+    lane_row = lax.rem(iota((128, COLS), 1), ROWS).astype(F32)
+
+    def ordering(e):
         c = counts[e][0:1, :].astype(F32)
         n_row = jnp.where(
             outer_pair,
             jnp.minimum(c, 256.0) + jnp.maximum(c - 768.0, 0.0),
             jnp.clip(c - 256.0, 0.0, 512.0),
         )
-        i0 = iota((128, 128), 0)
-        i1 = iota((128, 128), 1)
         n_col = jnp.sum(jnp.where(i0 == i1, n_row, 0.0), axis=1, keepdims=True)
+        behind = jnp.logical_or(n_row > n_col, jnp.logical_and(n_col == n_row, i1 < i0))
+        pos_col = jnp.sum(jnp.where(behind, 1.0, 0.0), axis=1, keepdims=True)
+        return n_row, n_col, pos_col
+
+    for e in range(UNITS):
+        n_row, n_col, pos_col = ordering(e)
         ahead = jnp.logical_or(n_col > n_row, jnp.logical_and(n_col == n_row, i0 < i1))
         pos_row = jnp.sum(jnp.where(ahead, 1.0, 0.0), axis=0, keepdims=True)
-        behind = jnp.logical_or(n_row > n_col, jnp.logical_and(n_col == n_row, i1 < i0))
-        pos_col = jnp.sum(jnp.where(behind, 1.0, 0.0), axis=1, keepdims=True)
         perm = (pos_row == i0.astype(F32)).astype(BF16)
-        perm_t = (pos_col == i1.astype(F32)).astype(BF16)
-        q_sorted = (nn(perm, q_all[pl.ds(e * 4, 4)].reshape(128, HEAD_COLUMNS)) * 0.125).astype(BF16)
-        f_sorted[...] = nn(perm, f_all[pl.ds(e * 4, 4)].reshape(128, 128)).astype(BF16)
+        q_sorted = nn(perm, q_all[e * 4 : e * 4 + 4].reshape(128, HEAD_COLUMNS)) * 0.125
+        q_sorted = q_sorted.astype(BF16)
+        f_sorted = nn(perm, f_all[e * 4 : e * 4 + 4].reshape(128, 128)).astype(BF16)
         none = jnp.zeros((ROWS, HEAD_WIDTH), BF16)
-        lane_row = lax.rem(iota((128, COLS), 1), ROWS).astype(F32)
-        longest = []
         for ch in range(CHUNKS):
+            u = e * CHUNKS + ch
             for g in range(GROUP):
                 piece = q_sorted[ch * ROWS : (ch + 1) * ROWS, g * HEAD_WIDTH : (g + 1) * HEAD_WIDTH]
-                qs[ch, g * ROWS : (g + 1) * ROWS, :] = jnp.concatenate([piece, none], axis=1)
+                qs[u, g * ROWS : (g + 1) * ROWS, :] = jnp.concatenate([piece, none], axis=1)
             member = pos_col == lane_row + float(ch * ROWS)
             limit = jnp.sum(jnp.where(member, n_col, 0.0), axis=0, keepdims=True) * PAGE_TOKENS
-            limit_ref[ch] = jnp.broadcast_to(limit, (8, COLS))
-            longest.append(jnp.max(limit).astype(jnp.int32))
+            limit_ref[u] = jnp.broadcast_to(limit, (8, COLS))
+            lengths[u] = jnp.max(limit).astype(jnp.int32)
             rows = f_sorted[ch * ROWS : (ch + 1) * ROWS, :]
-            s = nt(rows, qs[ch])
+            s = nt(rows, qs[u])
             ki = iota((ROWS, COLS), 0)
             ri = lax.rem(iota((ROWS, COLS), 1), ROWS)
             seen = jnp.logical_and(
@@ -303,75 +308,95 @@
             start = start + jnp.where(
                 iota((VROWS, COLS), 0) >= HEAD_WIDTH, jnp.exp(sink_row - m0), 0.0
             )
-            m_ref[ch] = jnp.broadcast_to(jnp.where(outer_pair, m0, FLOOR), (8, COLS))
-            acc[ch] = jnp.where(outer_pair, start, 0.0)
-
+            m_ref[u] = jnp.broadcast_to(jnp.where(outer_pair, m0, FLOOR), (8, COLS))
+            acc[u] = jnp.where(outer_pair, start, 0.0)
+
+    def unit(e, carry):
         def gather(kb, carry):
             p0 = kb * (GK // PAGE_TOKENS)
             ss = lax.div(p0, NPS)
-            within = lax.rem(p0, NPS)
-            row = e * 2 + lax.div(within, 128)
-            lane = lax.rem(within, 128)
-            base = pl.multiple_of(kb * GK, GK)
+            row = e * 2 + lax.div(lax.rem(p0, NPS), 128)
             rows = [
-                pool[tables[ss, row, lane + i] + ss * (N_EP * PAGES)]
-                for i in range(GK // PAGE_TOKENS)
+                pool[tables[ss, row, i] + ss * (N_EP * PAGES)] for i in range(GK // PAGE_TOKENS)
             ]
-            found = jnp.concatenate(rows, axis=0)
-            kv[pl.ds(base, GK), :] = found
-            vt[kb] = values_of(found)
+            for i in range(GK // BK):
+                part = rows[i * (BK // PAGE_TOKENS) : (i + 1) * (BK // PAGE_TOKENS)]
+                found = jnp.concatenate(part, axis=0)
+                kv[pl.ds(pl.multiple_of(kb * GK + i * BK, BK), BK), :] = found
+                vt[kb * (GK // BK) + i] = values_of(found)
             return carry
 
-        lax.fori_loop(0, lax.div(longest[0] + (BK - 1), BK) * (BK // GK), gather, 0)
-
-        key = iota((HALF, COLS), 0).astype(F32)
-        for ch in range(CHUNKS):
-            q = qs[ch]
-            limit = limit_ref[ch][0:1, :]
-
-            def scores(start):
-                return nt(kv[pl.ds(pl.multiple_of(start, HALF), HALF), :], q)
-
-            def absorb(s, start, state):
-                before, total = state
-                s = jnp.where(key < limit - start.astype(F32), s, NEGATIVE)
-                after = jnp.maximum(before, jnp.max(s, axis=0, keepdims=True))
-                p = jnp.exp(s - after).astype(BF16)
-                values = vt[lax.div(start, GK)]
-                return after, total * jnp.exp(before - after) + nn(values, p)
-
-            def block(kb, state):
-                start = kb * BK
-                s1[...] = scores(start + HALF)
-                state = absorb(s0[...], start, state)
-                s0[...] = scores(jnp.minimum(start + BK, KEYS - HALF))
-                return absorb(s1[...], start + HALF, state)
-
-            s0[...] = scores(0)
-            state = (m_ref[ch][0:1, :], acc[ch])
-            state = lax.fori_loop(0, lax.div(longest[ch] + (BK - 1), BK), block, state)
-            m_ref[ch] = jnp.broadcast_to(state[0], (8, COLS))
-            acc[ch] = state[1]
-
+        lax.fori_loop(0, lax.div(lengths[e * CHUNKS] + (GK - 1), GK), gather, 0)
+
+        key = iota((BK, COLS), 0).astype(F32)
+
+        def produce(store, u, kb):
+            keys = kv[pl.ds(pl.multiple_of(kb * BK, BK), BK), :]
+            s = nt(keys, qs[u])
+            limit = limit_ref[u][0:1, :] - (kb * BK).astype(F32)
+            s = jnp.where(key < limit, s, NEGATIVE)
+            store[...] = s
+            return jnp.max(s, axis=0, keepdims=True)
+
+        def absorb(store, u, kb, top):
+            before = m_ref[u][0:1, :]
+            after = jnp.maximum(before, top)
+            p = jnp.exp(store[...] - after).astype(BF16)
+            acc[u] = acc[u] * jnp.exp(before - after) + nn(vt[kb], p)
+            m_ref[u] = jnp.broadcast_to(after, (8, COLS))
+
+        def chunk(ch, top):
+            u = e * CHUNKS + ch
+            count = lax.div(lengths[u] + (BK - 1), BK)
+            after_u = e * CHUNKS + jnp.minimum(ch + 1, CHUNKS - 1)
+
+            def pair(i, top):
+                last = 2 * i + 2 >= count
+                next_top = produce(s1, u, 2 * i + 1)
+                absorb(s0, u, 2 * i, top)
+                top = produce(s0, jnp.where(last, after_u, u), jnp.where(last, 0, 2 * i + 2))
+                absorb(s1, u, 2 * i + 1, next_top)
+                return top
+
+            top = lax.fori_loop(0, lax.div(count, 2), pair, top)
+
+            def odd(top):
+                absorb(s0, u, count - 1, top)
+                return produce(s0, after_u, jnp.int32(0))
+
+            return lax.cond(lax.rem(count, 2) == 1, odd, lambda top: top, top)
+
+        used = sum([(lengths[e * CHUNKS + ch] > 0).astype(jnp.int32) for ch in range(CHUNKS)])
+
+        @pl.when(used > 0)
+        def _():
+            top = produce(s0, e * CHUNKS, jnp.int32(0))
+            lax.fori_loop(0, used, chunk, top)
+
+        return carry
+
+    lax.fori_loop(0, UNITS, unit, 0)
+
+    for e in range(UNITS):
+        _, _, pos_col = ordering(e)
+        perm_t = (pos_col == i1.astype(F32)).astype(BF16)
         lse = jnp.zeros((8, 128), F32)
         for ch in range(CHUNKS):
-            total = jnp.maximum(acc[ch][HEAD_WIDTH : HEAD_WIDTH + 1, :], 1e-30)
-            out = acc[ch][0:HEAD_WIDTH, :] / total
+            u = e * CHUNKS + ch
+            total = jnp.maximum(acc[u][HEAD_WIDTH : HEAD_WIDTH + 1, :], 1e-30)
+            out = acc[u][0:HEAD_WIDTH, :] / total
             padded = jnp.concatenate([out, jnp.zeros_like(out)], axis=0)
             turned = padded.T.astype(BF16)
             for g in range(GROUP):
-                sorted_out[ch * ROWS : (ch + 1) * ROWS, g * HEAD_WIDTH : (g + 1) * HEAD_WIDTH] = (
+                sorted_out[e, ch * ROWS : (ch + 1) * ROWS, g * HEAD_WIDTH : (g + 1) * HEAD_WIDTH] = (
                     turned[g * ROWS : (g + 1) * ROWS, 0:HEAD_WIDTH]
                 )
-            row = m_ref[ch][0:1, :] + jnp.log(total)
+            row = m_ref[u][0:1, :] + jnp.log(total)
             mine = lax.div(iota((8, COLS), 1), ROWS) == iota((8, COLS), 0)
             member = (pos_col == lane_row + float(ch * ROWS)).astype(F32)
             lse = lse + nt(jnp.where(mine, row, 0.0), member, HIGHEST)
         lse_ref[e] = lse
-        o_ref[e] = nn(perm_t, sorted_out[...]).astype(BF16)
-        return carry
-
-    lax.fori_loop(0, 4, unit, 0)
+        o_ref[e] = nn(perm_t, sorted_out[e]).astype(BF16)
 
 
 def score(tables, counts, sinks, q_all, f_all, pool):
@@ -379,22 +404,22 @@
     return pl.pallas_call(
         score_kernel,
         out_shape=(
-            jax.ShapeDtypeStruct((4, 128, HEAD_COLUMNS), BF16),
-            jax.ShapeDtypeStruct((4, 8, 128), F32),
+            jax.ShapeDtypeStruct((UNITS, 128, HEAD_COLUMNS), BF16),
+            jax.ShapeDtypeStruct((UNITS, 8, 128), F32),
         ),
         in_specs=[pl.BlockSpec(memory_space=pltpu.SMEM)] + [vmem] * 5,
         out_specs=(vmem, vmem),
         scratch_shapes=[
             pltpu.VMEM((KEYS, 128), BF16),
-            pltpu.VMEM((KEYS // GK, VROWS, GK), BF16),
-            pltpu.VMEM((CHUNKS, COLS, 128), BF16),
-            pltpu.VMEM((128, 128), BF16),
-            pltpu.VMEM((CHUNKS, 8, COLS), F32),
-            pltpu.VMEM((CHUNKS, 8, COLS), F32),
-            pltpu.VMEM((CHUNKS, VROWS, COLS), F32),
-            pltpu.VMEM((128, HEAD_COLUMNS), BF16),
-            pltpu.VMEM((HALF, COLS), F32),
-            pltpu.VMEM((HALF, COLS), F32),
+            pltpu.VMEM((KEYS // BK, VROWS, BK), BF16),
+            pltpu.VMEM((UNITS * CHUNKS, COLS, 128), BF16),
+            pltpu.VMEM((UNITS * CHUNKS, 8, COLS), F32),
+            pltpu.VMEM((UNITS * CHUNKS, 8, COLS), F32),
+            pltpu.VMEM((UNITS * CHUNKS, VROWS, COLS), F32),
+            pltpu.VMEM((UNITS, 128, HEAD_COLUMNS), BF16),
+            pltpu.VMEM((BK, COLS), F32),
+            pltpu.VMEM((BK, COLS), F32),
+            pltpu.SMEM((UNITS * CHUNKS,), jnp.int32),
         ],
         compiler_params=pltpu.CompilerParams(vmem_limit_bytes=40 << 20),
         cost_estimate=pl.CostEstimate(

time: 204 us -> 187 us (0.917); the launches traced: 204 us -> 185 us
  Pallas kernels: 133 us -> 114 us
    pallas_call x1, Pallas kernels: 68.8 us -> 50.7 us  [score(): pl.pallas_call(score_kernel, out_shape=(jax.ShapeDtypeStruct((UNITS, 128,...]
  transfers between devices with their start and end apart: 2 -> 2, of which waited for: 0 -> 0; matrix products, arithmetic and copies ran while one was open for 2% -> 2% of each run, Pallas kernels for 65% -> 62%
where the time goes in v2:
time: 187 us; the launch traced here: 185 us
  Pallas kernels  114 us (61%)
  matrix products  24.1 us (13%)
  local copies, waits for them, and re-layouts  22.5 us (12%)
  starting transfers between devices  20.9 us (11%)
  other arithmetic  2.22 us (1%)
    pallas_call x1, Pallas kernels, score(): pl.pallas_call(score_kernel, out_shape=(jax.ShapeDtypeStruct((UNITS, 128,...  50.7 us
    pallas_call x1, Pallas kernels, exchange(): pl.pallas_call(exchange_kernel, out_shape=(jax.ShapeDtypeStruct((16, ROWS...  47.8 us
    pallas_call x1, Pallas kernels, merge(): pl.pallas_call(merge_kernel, out_shape=jax.ShapeDtypeStruct((ROWS, QUERY_...  15.6 us
    dot_general x1, matrix products, per_device(): projected = jnp.dot(arrived, gate_up[0], preferred_element_type=F32)  12.8 us
    all_to_all x1, starting transfers between devices, per_device(): lax.all_to_all(buffer, ('seq', 'ep'), split_axis=0, concat_axis=0, tiled=...  11.6 us
    all_to_all x1, starting transfers between devices, per_device(): lax.all_to_all(result, ('seq', 'ep'), split_axis=0, concat_axis=0, tiled=...  9.29 us
    dot_general x1, matrix products, per_device(): jnp.dot(active, down_proj[0], preferred_element_type=F32).astype(BF16)  9.22 us
    unnamed x22, local copies, waits for them, and re-layouts  6.36 us
  transfers between devices with their start and end apart: 2, of which 0 were waited for; matrix products, arithmetic and copies ran while one was open for 2% of the time, Pallas kernels for 62%

profile of v2, /device:TPU:0, one launch (start us, length us, event | category | flops | bytes accessed | tf_op | source)
XLA Modules:
  0.0 184.7 jit_solution(17307201659390647456)
XLA Ops:
  0.6 0.8 copy.34
  1.4 0.7 broadcast_multiply_fusion
  2.1 1.0 reshape.97
  3.1 1.1 multiply_reduce_fusion
  4.2 0.1 eq.20
  4.3 0.2 convert_reduce_fusion
  4.5 0.1 reduce_sum.30
  4.6 0.1 copy.35
  4.7 0.1 copy.33
  4.8 0.1 mul.67
  4.9 0.1 fusion.16
  5.0 0.1 rsqrt.12
  5.1 1.4 convolution_convert_fusion
  6.5 1.0 copy.37
  7.5 1.5 all_to_all.16
  9.0 0.0 copy-start.5
  9.0 0.0 copy-start.6
  9.0 11.6 %all-to-all-start = ((bf16[128,2,2880]{2,1,0:T(2,128)(2,1)}), bf16[128,2,2880]{2,1,0:T(2,128)(2,1)}, u32[]{:S(2)}, u32[]{:S(2)}) async-start(bf16[128,2,2880]{2,1,0:T(2,128)(2,1)} %all_to_all.16), calls=%async_computation | async-start | bytes 3014656 | tf_op jit(solution)/shard_map/all_to_all | solution.py:536
  20.7 0.0 copy-done.5
  20.7 0.0 copy-done.6
  20.7 0.6 copy.32
  21.4 0.0 copy-start.3
  21.4 0.0 copy-start.4
  21.4 0.0 copy-start.8
  21.4 0.0 copy-start.9
  21.4 0.0 copy-start
  21.4 1.2 reshape.91
  22.7 0.0 copy-done.3
  22.7 0.1 reshape.88.q_ref
  22.7 0.0 copy-done.4
  22.8 0.0 copy-done.8
  22.8 0.1 reshape.93
  22.9 0.1 broadcast_in_dim.40
  23.0 0.1 broadcast_in_dim.41
  23.1 0.0 copy-done.9
  23.1 0.1 dynamic_slice.10
  23.2 0.1 broadcast_in_dim.43
  23.2 0.1 broadcast_in_dim.44
  23.3 0.0 copy-done
  23.3 47.8 %exchange.1 = (bf16[16,32,512]{2,1,0:T(8,128)(2,1)S(1)}, bf16[16,32,128]{2,1,0:T(8,128)(2,1)S(1)}, bf16[2,768,16,128]{3,2,1,0:T(8,128)(2,1)S(1)}, s32[2,8,128]{2,1,0:T(8,128)S(1)}, s32[4,8,128]{2,1,0:T(8,128)S(1)}) custom-call(bf16[32,4096]{1,0:T(8,128)(2,1)S(1)} %reshape.88.q_ref, bf16[32,1024]{1,0:T(8,128)(2,1)S(1)} %reshape.89.f_ref, ...), custom_call_target="tpu_custom_call" | custom-call | tf_op jit(solution)/shard_map/exchange/pallas_call | solution.py:217
  71.2 0.0 copy-start.1
  71.2 2.6 %copy-done.1 = bf16[2,768,16,128]{3,2,1,0:T(8,128)(2,1)} copy-done((bf16[2,768,16,128]{3,2,1,0:T(8,128)(2,1)}, bf16[2,768,16,128]{3,2,1,0:T(8,128)(2,1)S(1)}, u32[]{:S(2)}) %copy-start.1) | copy-done | bytes 6291480
  73.8 0.0 all-to-all-done
  73.8 3.5 %all_to_all.18 = bf16[256,2880]{1,0:T(8,128)(2,1)S(1)} reshape(bf16[128,2,2880]{2,1,0:T(2,128)(2,1)} %all-to-all-done) | data formatting | bytes 2949120 | tf_op jit(solution)/shard_map/all_to_all | solution.py:536
  77.3 12.8 %fusion = f32[256,2880]{0,1:T(8,128)} fusion(bf16[256,2880]{1,0:T(8,128)(2,1)S(1)} %all_to_all.18, bf16[1,2880,2880]{2,1,0:T(8,128)(2,1)} %param.24), kind=kOutput, calls=%fused_computation | convolution fusion | flops 4246732800 | bytes 21012480 | tf_op jit(solution)/shard_map/dot_general | solution.py:558
  90.1 9.2 %fusion.4 = bf16[256,2880]{0,1:T(8,128)(2,1)} fusion(bf16[1,1440,2880]{2,1,0:T(8,128)(2,1)} %param.25, f32[256,2880]{0,1:T(8,128)} %fusion), kind=kOutput, calls=%fused_computation.5 | convolution fusion | flops 2127052800 | bytes 12718080 | tf_op jit(solution)/shard_map/dot_general | solution.py:561
  99.3 1.8 copy.38
  101.1 1.5 all_to_all.19
  102.6 9.3 %all-to-all-start.1 = ((bf16[128,2,2880]{2,1,0:T(2,128)(2,1)}), bf16[128,2,2880]{2,1,0:T(2,128)(2,1)S(1)}, u32[]{:S(2)}, u32[]{:S(2)}) async-start(bf16[128,2,2880]{2,1,0:T(2,128)(2,1)} %all_to_all.19), calls=%async_computation.1 | async-start | bytes 3014656 | tf_op jit(solution)/shard_map/all_to_all | solution.py:562
  111.9 0.0 copy-start.2
  111.9 2.8 %copy-done.2 = bf16[2,768,16,128]{3,2,1,0:T(8,128)(2,1)S(1)} copy-done((bf16[2,768,16,128]{3,2,1,0:T(8,128)(2,1)S(1)}, bf16[2,768,16,128]{3,2,1,0:T(8,128)(2,1)}, u32[]{:S(2)}) %copy-start.2) | copy-done | bytes 6291480
  114.7 0.0 copy-start.7
  114.7 50.7 %score.1 = (bf16[4,128,512]{2,1,0:T(8,128)(2,1)S(1)}, f32[4,8,128]{2,1,0:T(8,128)S(1)}) custom-call(s32[2,8,128]{2,1,0:T(8,128)S(1)} %get-tuple-element.9.tables, s32[4,8,128]{2,1,0:T(8,128)S(1)} %get-tuple-element.10.counts, f32[8,256]{1,0:T(8,128)S(1)} %broadcast_in_dim.45.sinks, bf16[16,32,512]{2,1,0:T(8,128)(2,1)S(1)} %get-tuple-element.11.q_all, ...), custom_call_target="tpu_custom_call" | custom-call | flops 24999999488 | bytes 8000000 | tf_op jit(solution)/shard_map/score/pallas_call | solution.py:404
  165.4 15.6 %merge.1 = bf16[32,4096]{1,0:T(8,128)(2,1)S(1)} custom-call(bf16[4,128,512]{2,1,0:T(8,128)(2,1)S(1)} %get-tuple-element.14.o_ref, f32[4,8,128]{2,1,0:T(8,128)S(1)} %get-tuple-element.15.lse_ref), custom_call_target="tpu_custom_call" | custom-call | tf_op jit(solution)/shard_map/merge/pallas_call | solution.py:494
  181.0 0.8 reshape.95
  181.8 0.0 copy-done.7
  181.8 0.1 copy.36
  181.9 0.1 broadcast_in_dim.46
  182.0 0.1 select_reduce_fusion
  182.1 0.0 all-to-all-done.1
  182.1 1.2 all_to_all.21
  183.3 0.4 fusion.19
  183.6 0.4 fusion.7
  184.0 0.7 reshape.96
  (7 shorter events, 0.1 us)
Async XLA Ops:
  9.0 11.6 %copy-start.5 = (s32[1,4096,2]{1,2,0:T(2,128)S(1)}, s32[1,4096,2]{1,2,0:T(2,128)}, u32[]{:S(2)}) copy-start(s32[1,4096,2]{1,2,0:T(2,128)} %param.17) | copy-start | bytes 98308
  9.0 11.7 %copy-start.6 = (s32[1,4096,2]{1,2,0:T(2,128)S(1)}, s32[1,4096,2]{1,2,0:T(2,128)}, u32[]{:S(2)}) copy-start(s32[1,4096,2]{1,2,0:T(2,128)} %param.16) | copy-start | bytes 98308
  9.0 64.8 %all-to-all-start = ((bf16[128,2,2880]{2,1,0:T(2,128)(2,1)}), bf16[128,2,2880]{2,1,0:T(2,128)(2,1)}, u32[]{:S(2)}, u32[]{:S(2)}) async-start(bf16[128,2,2880]{2,1,0:T(2,128)(2,1)} %all_to_all.16), calls=%async_computation | async-start | bytes 3014656 | tf_op jit(solution)/shard_map/all_to_all | solution.py:536
  21.4 1.3 copy-start.3
  21.4 1.4 copy-start.4
  21.4 1.4 copy-start.8
  21.4 1.7 copy-start.9
  21.4 1.9 %copy-start = (bf16[1,24,16,1024]{3,2,1,0:T(8,128)(2,1)S(1)}, bf16[1,24,16,1024]{3,2,1,0:T(8,128)(2,1)}, u32[]{:S(2)}) copy-start(bf16[1,24,16,1024]{3,2,1,0:T(8,128)(2,1)} %param.15) | copy-start | bytes 2359300
  71.2 2.7 %copy-start.1 = (bf16[2,768,16,128]{3,2,1,0:T(8,128)(2,1)}, bf16[2,768,16,128]{3,2,1,0:T(8,128)(2,1)S(1)}, u32[]{:S(2)}) copy-start(bf16[2,768,16,128]{3,2,1,0:T(8,128)(2,1)S(1)} %get-tuple-element.13) | copy-start | bytes 18874372
  102.6 79.5 %all-to-all-start.1 = ((bf16[128,2,2880]{2,1,0:T(2,128)(2,1)}), bf16[128,2,2880]{2,1,0:T(2,128)(2,1)S(1)}, u32[]{:S(2)}, u32[]{:S(2)}) async-start(bf16[128,2,2880]{2,1,0:T(2,128)(2,1)} %all_to_all.19), calls=%async_computation.1 | async-start | bytes 3014656 | tf_op jit(solution)/shard_map/all_to_all | solution.py:562
  111.9 2.8 %copy-start.2 = (bf16[2,768,16,128]{3,2,1,0:T(8,128)(2,1)S(1)}, bf16[2,768,16,128]{3,2,1,0:T(8,128)(2,1)}, u32[]{:S(2)}) copy-start(bf16[2,768,16,128]{3,2,1,0:T(8,128)(2,1)} %copy-done.1) | copy-start | bytes 18874372
  114.7 67.1 %copy-start.7 = (f32[1,8,4,4]{1,3,2,0:T(4,128)S(1)}, f32[1,8,4,4]{1,3,2,0:T(4,128)}, u32[]{:S(2)}) copy-start(f32[1,8,4,4]{1,3,2,0:T(4,128)} %param.23) | copy-start | bytes 1540

commit v3 on v2

--- a/solution.py
+++ b/solution.py
@@ -63,11 +63,11 @@
 
 
 def exchange_kernel(
-    q_ref, f_ref, page_ref, table_ref, count_ref,
-    q_all, f_all, pool, tables, counts,
-    relay, f_relay,
+    q_ref, f_ref, page_ref, table_ref, count_ref, hidden_ref, gain_ref, spread_ref, up_ref, down_ref,
+    q_all, f_all, pool, tables, counts, expert_out,
+    relay, f_relay, rows_out, rows_mid, rows_sorted, rows_in, up_w, down_w, projected, active,
     q_send, q_recv, f_send, f_recv, a_send, a_recv, z_send, z_recv, c_send, c_recv,
-    i_send, i_recv, local,
+    i_send, i_recv, d_send, d_recv, e_send, e_recv, local, w_sem,
 ):
     y, z, x, c = place()
     mate = 3 - y
@@ -80,9 +80,28 @@
     down = device(y, lax.rem(z + 3, 4), x, c)
     twin = device(y, z, x, 1 - c)
 
+    def beside(dy, dz):
+        return device(lax.rem(y + dy, 4), lax.rem(z + dz, 4), x, c)
+
+    def around(dx, dc):
+        return device(y, z, lax.rem(x + dx, 4), lax.rem(c + dc, 2))
+
+    peers = [at(dy, dx) for dy, dx in plane]
+    peers += [beside(dy, dz) for dy in range(4) for dz in range(1, 4)]
+    peers += [around(dx, 1) for dx in range(4)]
     barrier = pltpu.get_barrier_semaphore()
-    for peer in [at(dy, dx) for dy, dx in plane] + [up, down, twin]:
+    for peer in peers:
         pl.semaphore_signal(barrier, inc=1, device_id=peer, device_id_type=MESH)
+
+    weights = []
+    for n in range(4):
+        part = pl.ds(n * (D // 4), D // 4)
+        weights.append(pltpu.make_async_copy(up_ref.at[0, part], up_w.at[part], w_sem.at[n]))
+    for n in range(2):
+        part = pl.ds(n * (HID // 2), HID // 2)
+        weights.append(pltpu.make_async_copy(down_ref.at[0, part], down_w.at[part], w_sem.at[4 + n]))
+    for copy in weights:
+        copy.start()
 
     for h in range(KEY_VALUE_HEADS):
         low, high = h * HEAD_WIDTH, (h + 1) * HEAD_WIDTH
@@ -94,7 +113,7 @@
         f_relay[h] = jnp.concatenate(
             [f_ref[:, low:high], f_ref[:, split + low : split + high]], axis=1
         )
-    pl.semaphore_wait(barrier, len(plane) + 3)
+    pl.semaphore_wait(barrier, len(peers))
 
     def spot(segment_slot, zz, xx, cc):
         return pool.at[segment_slot, pl.ds((zz * 8 + xx * 2 + cc) * PAGES, PAGES)]
@@ -136,6 +155,26 @@
         )
         other.start()
         small.append(other)
+
+    h32 = hidden_ref[...].astype(F32)
+    scale = lax.rsqrt(jnp.mean(h32 * h32, axis=-1, keepdims=True) + EPSILON)
+    normed = (h32 * scale * gain_ref[...]).astype(BF16)
+    rows_out[...] = nn(spread_ref[...], normed).astype(BF16).reshape(16, 16, D)
+    routed = []
+    for dy in range(4):
+        for dz in range(4):
+            n = dy * 4 + dz
+            source = rows_out.at[lax.rem(y + dy, 4) * 4 + lax.rem(z + dz, 4)]
+            target = rows_mid.at[y * 4 + z]
+            if n == 0:
+                copy = pltpu.make_async_copy(source, target, local.at[5])
+            else:
+                copy = pltpu.make_async_remote_copy(
+                    source, target, d_send.at[n], d_recv.at[n],
+                    device_id=beside(dy, dz), device_id_type=MESH,
+                )
+            copy.start()
+            routed.append(copy)
 
     for dy in range(4):
         for dx in range(4):
@@ -190,6 +229,33 @@
         upward.append(pass_on(n, z, 0, up))
         downward.append(pass_on(n, z, 1, down))
         across.append(pass_on(n, z, 3, twin))
+
+    for copy in routed:
+        copy.wait()
+    ri = iota((256, 256), 0)
+    ci = iota((256, 256), 1)
+
+    def slot_of(i):
+        return lax.div(lax.rem(i, 32), 2) * 16 + lax.div(i, 32) * 2 + lax.rem(i, 2)
+
+    regroup = (slot_of(ri) == ci).astype(BF16)
+    rows_sorted[...] = nn(regroup, rows_mid[...].reshape(256, D)).astype(BF16).reshape(8, 32, D)
+    delivered = []
+    for dx in range(4):
+        for dc in range(2):
+            n = dx * 2 + dc
+            source = rows_sorted.at[lax.rem(x + dx, 4) * 2 + lax.rem(c + dc, 2)]
+            target = rows_in.at[x * 2 + c]
+            if n == 0:
+                copy = pltpu.make_async_copy(source, target, local.at[6])
+            else:
+                copy = pltpu.make_async_remote_copy(
+                    source, target, e_send.at[n], e_recv.at[n],
+                    device_id=around(dx, dc), device_id_type=MESH,
+                )
+            copy.start()
+            delivered.append(copy)
+
     for n in range(8):
         upward[n].wait_recv()
         if n % 2 == 0:
@@ -202,6 +268,37 @@
     for n in range(8):
         further[n].wait_recv()
         across.append(pass_on(n, lax.rem(z + 2, 4), 6, twin))
+
+    for copy in weights + delivered:
+        copy.wait()
+
+    def tiles(work):
+        @pl.loop(0, D // TILE)
+        def _(j):
+            work(pl.ds(pl.multiple_of(j * TILE, TILE), TILE))
+
+        work(pl.ds(D // TILE * TILE, D % TILE))
+
+    def project(part):
+        projected[:, part] = nn(rows_in[...].reshape(256, D), up_w[:, part])
+
+    tiles(project)
+
+    @pl.loop(0, 8)
+    def _(j):
+        part = pl.ds(pl.multiple_of(j * 32, 32), 32)
+        wide = projected[part, :]
+        gate, upper = wide[:, :HID], wide[:, HID:]
+        active[part, :] = ((upper + 1.0) * gate * jax.nn.sigmoid(1.702 * gate)).astype(BF16)
+
+    back = (slot_of(ci) == ri).astype(BF16)
+    active[...] = nn(back, active[...]).astype(BF16)
+
+    def finish(part):
+        expert_out[:, part] = nn(active[...], down_w[:, part]).astype(BF16)
+
+    tiles(finish)
+
     for copy in across:
         copy.wait()
     for copy in first[1:] + upward + downward + further:
@@ -210,7 +307,10 @@
         copy.wait()
 
 
-def exchange(queries, fresh, pages, table, count):
+TILE = 384
+
+
+def exchange(queries, fresh, pages, table, count, hidden, gain, spread, gate_up, down_proj):
     vmem = pl.BlockSpec(memory_space=pltpu.VMEM)
     anywhere = pl.BlockSpec(memory_space=pl.ANY)
     dma = pltpu.SemaphoreType.DMA
@@ -222,20 +322,30 @@
             jax.ShapeDtypeStruct((2, N_EP * PAGES, PAGE_TOKENS, 2 * HEAD_WIDTH), BF16),
             jax.ShapeDtypeStruct((2, 8, 128), jnp.int32),
             jax.ShapeDtypeStruct((4, 8, 128), jnp.int32),
+            jax.ShapeDtypeStruct((256, D), BF16),
         ),
-        in_specs=[vmem] * 5,
-        out_specs=(anywhere,) * 5,
+        in_specs=[vmem] * 8 + [anywhere] * 2,
+        out_specs=(anywhere,) * 5 + (vmem,),
         scratch_shapes=[
             pltpu.VMEM((KEY_VALUE_HEADS, PAGES, PAGE_TOKENS, 2 * HEAD_WIDTH), BF16),
             pltpu.VMEM((KEY_VALUE_HEADS, ROWS, 2 * HEAD_WIDTH), BF16),
+            pltpu.VMEM((16, 16, D), BF16),
+            pltpu.VMEM((16, 16, D), BF16),
+            pltpu.VMEM((8, 32, D), BF16),
+            pltpu.VMEM((8, 32, D), BF16),
+            pltpu.VMEM((D, 2 * HID), BF16),
+            pltpu.VMEM((HID, D), BF16),
+            pltpu.VMEM((256, 2 * HID), F32),
+            pltpu.VMEM((256, HID), BF16),
             dma((16,)), dma((16,)), dma((16,)), dma((16,)), dma((8,)), dma((8,)),
-            dma((24,)), dma((24,)), dma((32,)), dma((32,)), dma((4,)), dma((4,)), dma((5,)),
+            dma((24,)), dma((24,)), dma((32,)), dma((32,)), dma((4,)), dma((4,)),
+            dma((16,)), dma((16,)), dma((8,)), dma((8,)), dma((7,)), dma((6,)),
         ],
         compiler_params=pltpu.CompilerParams(
-            collective_id=1, has_side_effects=True, vmem_limit_bytes=16 << 20
+            collective_id=1, has_side_effects=True, vmem_limit_bytes=56 << 20
         ),
         name="exchange",
-    )(queries, fresh, pages, table, count)
+    )(queries, fresh, pages, table, count, hidden, gain, spread, gate_up, down_proj)
 
 
 BK = 1024
@@ -514,9 +624,6 @@
 ):
     y, z, x, c = place()
 
-    flat_hidden = hidden.reshape(ROWS, D).astype(F32)
-    meansq = jnp.mean(flat_hidden * flat_hidden, axis=-1, keepdims=True)
-    normed = (flat_hidden * lax.rsqrt(meansq + EPSILON) * norm_gain).astype(BF16)
     chosen = expert_ids.reshape(ROWS * TOPK)
     number = jnp.arange(ROWS * TOPK, dtype=jnp.int32)
     same = jnp.logical_and(chosen[:, None] == chosen[None, :], number[None, :] < number[:, None])
@@ -524,7 +631,6 @@
     slots = (chosen * 2 + rank).reshape(ROWS, TOPK)
     hit = slots[None, :, :] == jnp.arange(256, dtype=jnp.int32)[:, None, None]
     spread = jnp.any(hit, axis=-1).astype(BF16)
-    buffer = jnp.dot(spread, normed, preferred_element_type=F32).astype(BF16)
     weights = jnp.sum(
         jnp.where(
             slots[:, :, None] == jnp.arange(256, dtype=jnp.int32)[None, None, :],
@@ -533,19 +639,23 @@
         ),
         axis=1,
     )
-    arrived = lax.all_to_all(buffer, ("seq", "ep"), split_axis=0, concat_axis=0, tiled=True)
 
     index = (page_owner * PAGES + page_slot).reshape(4, 4, 2, NPS)
     index = lax.dynamic_index_in_dim(index, z, 0, keepdims=False)
     index = lax.dynamic_index_in_dim(index, c, 1, keepdims=False)
     table = index.reshape(8, 128)
     count = jnp.broadcast_to(jnp.repeat(page_count.reshape(32), 4)[None, :], (8, 128))
-    q_all, f_all, pool, tables, counts = exchange(
+    q_all, f_all, pool, tables, counts, result = exchange(
         queries.reshape(ROWS, QUERY_HEADS * HEAD_WIDTH),
         fresh_key_values.reshape(ROWS, 2 * KEY_VALUE_HEADS * HEAD_WIDTH),
         key_value_pages.reshape(PAGES * PAGE_TOKENS, 2 * KEY_VALUE_HEADS * HEAD_WIDTH),
         table,
         count,
+        hidden.reshape(ROWS, D),
+        norm_gain.reshape(1, D),
+        spread,
+        gate_up,
+        down_proj,
     )
     head_sinks = lax.dynamic_slice_in_dim(sinks, head_of(y, x) * GROUP, GROUP)
     sink_rows = jnp.broadcast_to(jnp.repeat(head_sinks, ROWS)[None, :], (8, COLS))
@@ -555,10 +665,6 @@
     )
     attention = merge(o, lse).reshape(queries.shape)
 
-    projected = jnp.dot(arrived, gate_up[0], preferred_element_type=F32)
-    gate, upper = projected[:, :HID], projected[:, HID:]
-    active = ((upper + 1.0) * gate * jax.nn.sigmoid(1.702 * gate)).astype(BF16)
-    result = jnp.dot(active, down_proj[0], preferred_element_type=F32).astype(BF16)
     returned = lax.all_to_all(result, ("seq", "ep"), split_axis=0, concat_axis=0, tiled=True)
     high = weights.astype(BF16)
     low = (weights - high.astype(F32)).astype(BF16)

time: 187 us -> 179 us (0.957)
  Pallas kernels: 114 us -> 145 us
  matrix products: 24.1 us -> 0.73 us
  starting transfers between devices: 20.9 us -> 8.08 us
  local copies, waits for them, and re-layouts: 22.5 us -> 20.2 us
    pallas_call x1, Pallas kernels: 47.8 us -> 78 us  [exchange(): pl.pallas_call(exchange_kernel, out_shape=(jax.ShapeDtypeStruct((16, ROWS...]
    dot_general x3 -> x0, matrix products: 23.3 us -> none  [the longest x1 12.8 us: per_device(): projected = jnp.dot(arrived, gate_up[0], preferred_element_type=F32)]
    all_to_all x1 -> x0, starting transfers between devices: 11.6 us -> none  [per_device(): lax.all_to_all(buffer, ('seq', 'ep'), split_axis=0, concat_axis=0, tiled=...]
    all_to_all x2 -> x0, local copies, waits for them, and re-layouts: 5.02 us -> none  [per_device(): lax.all_to_all(buffer, ('seq', 'ep'), split_axis=0, concat_axis=0, tiled=...]
    convert_element_type x3 -> x1, local copies, waits for them, and re-layouts: 3.79 us -> 0.72 us  [per_device(): spread = jnp.any(hit, axis=-1).astype(BF16)]
    all_to_all x2, local copies, waits for them, and re-layouts: 2.65 us -> 5.52 us  [per_device(): lax.all_to_all(result, ('seq', 'ep'), split_axis=0, concat_axis=0, tiled=...]
    unnamed x22, local copies, waits for them, and re-layouts: 6.36 us -> 3.71 us
  transfers between devices with their start and end apart: 2 -> 1, of which waited for: 0 -> 0; matrix products, arithmetic and copies ran while one was open for 2% -> 1% of each run, Pallas kernels for 62% -> 38%
where the time goes in v3:
time: 179 us; the launch traced here: 177 us
  Pallas kernels  145 us (81%)
  local copies, waits for them, and re-layouts  20.2 us (11%)
  starting transfers between devices  8.08 us (5%)
  other arithmetic  1.89 us (1%)
    pallas_call x1, Pallas kernels, exchange(): pl.pallas_call(exchange_kernel, out_shape=(jax.ShapeDtypeStruct((16, ROWS...  78 us
    pallas_call x1, Pallas kernels, score(): pl.pallas_call(score_kernel, out_shape=(jax.ShapeDtypeStruct((UNITS, 128,...  51.5 us
    pallas_call x1, Pallas kernels, merge(): pl.pallas_call(merge_kernel, out_shape=jax.ShapeDtypeStruct((ROWS, QUERY_...  16 us
    all_to_all x1, starting transfers between devices, per_device(): lax.all_to_all(result, ('seq', 'ep'), split_axis=0, concat_axis=0, tiled=...  8.08 us
    all_to_all x2, local copies, waits for them, and re-layouts, per_device(): lax.all_to_all(result, ('seq', 'ep'), split_axis=0, concat_axis=0, tiled=...  5.52 us
    unnamed x22, local copies, waits for them, and re-layouts  3.71 us
  transfers between devices with their start and end apart: 1, of which 0 were waited for; matrix products, arithmetic and copies ran while one was open for 1% of the time, Pallas kernels for 38%

profile of v3, /device:TPU:0, one launch (start us, length us, event | category | flops | bytes accessed | tf_op | source)
XLA Modules:
  0.0 177.2 jit_solution(2089816139690061146)
XLA Ops:
  0.6 0.7 broadcast_multiply_fusion
  1.3 0.8 copy.38
  2.1 1.7 reshape.71.q_ref
  3.8 1.5 reshape.72.f_ref
  5.3 0.8 multiply_add_fusion
  6.1 0.6 copy.36
  6.8 0.0 copy-start.8
  6.8 0.0 copy-start.5
  6.8 0.0 copy-start.6
  6.8 1.2 reshape.74
  8.1 0.0 copy-done.8
  8.1 0.1 reshape.76
  8.2 0.1 broadcast_in_dim.38
  8.3 0.1 broadcast_in_dim.39
  8.4 0.0 copy-done.5
  8.4 0.8 reshape.77.hidden_ref
  9.1 0.0 copy-done.6
  9.1 0.6 reshape.78.gain_ref
  9.7 0.1 copy.37
  9.8 0.1 mul.33
  9.9 0.1 eq.20
  10.0 0.2 convert_reduce_fusion
  10.2 0.1 reduce_sum.21
  10.3 0.1 copy.39
  10.4 0.1 fusion.1
  10.5 0.7 copy.40.spread_ref
  11.3 0.6 constant_dynamic-slice_fusion
  11.8 0.6 broadcast_in_dim.40.count_ref
  12.4 78.0 %exchange.1 = (bf16[16,32,512]{2,1,0:T(8,128)(2,1)}, bf16[16,32,128]{2,1,0:T(8,128)(2,1)}, bf16[2,768,16,128]{3,2,1,0:T(8,128)(2,1)}, s32[2,8,128]{2,1,0:T(8,128...) custom-call(bf16[32,4096]{1,0:T(8,128)(2,1)} %reshape.71.q_ref, bf16[32,1024]{1,0:T(8,128)(2,1)} %reshape.72.f_ref, ...), custom_call_target="tpu_custom_call" | custom-call | tf_op jit(solution)/shard_map/exchange/pallas_call | solution.py:317
  90.4 4.3 %all_to_all.8 = bf16[128,2,2880]{2,1,0:T(2,128)(2,1)} reshape(bf16[256,2880]{1,0:T(8,128)(2,1)} %get-tuple-element.17) | data formatting | bytes 2949120 | tf_op jit(solution)/shard_map/all_to_all | solution.py:668
  94.8 0.0 copy-start.9
  94.8 0.0 copy-start.1
  94.8 0.0 copy-start.2
  94.8 0.0 copy-start.3
  94.8 0.0 copy-start.4
  94.8 8.1 %all-to-all-start = ((bf16[128,2,2880]{2,1,0:T(2,128)(2,1)}), bf16[128,2,2880]{2,1,0:T(2,128)(2,1)S(1)}, u32[]{:S(2)}, u32[]{:S(2)}) async-start(bf16[128,2,2880]{2,1,0:T(2,128)(2,1)} %all_to_all.8), calls=%async_computation | async-start | bytes 3014656 | tf_op jit(solution)/shard_map/all_to_all | solution.py:668
  102.9 0.0 copy-done.9
  102.9 0.1 dynamic_slice.10
  103.0 0.1 broadcast_in_dim.41
  103.0 0.1 broadcast_in_dim.42
  103.1 0.0 copy-done.1
  103.1 0.0 copy-done.2
  103.1 0.0 copy-done.3
  103.1 0.0 copy-done.4
  103.2 0.0 copy-start
  103.2 2.8 %copy-done = bf16[2,768,16,128]{3,2,1,0:T(8,128)(2,1)S(1)} copy-done((bf16[2,768,16,128]{3,2,1,0:T(8,128)(2,1)S(1)}, bf16[2,768,16,128]{3,2,1,0:T(8,128)(2,1)}, u32[]{:S(2)}) %copy-start) | copy-done | bytes 6291480
  105.9 0.0 copy-start.7
  105.9 51.5 %score.1 = (bf16[4,128,512]{2,1,0:T(8,128)(2,1)S(1)}, f32[4,8,128]{2,1,0:T(8,128)S(1)}) custom-call(s32[2,8,128]{2,1,0:T(8,128)S(1)} %copy-done.4, s32[4,8,128]{2,1,0:T(8,128)S(1)} %copy-done.3, f32[8,256]{1,0:T(8,128)S(1)} %broadcast_in_dim.43.sinks, bf16[16,32,512]{2,1,0:T(8,128)(2,1)S(1)} %copy-done.1, bf16[16,32,128]{2,1,0:T(8,128)(2,1)S(1)} %copy-done.2, ...), custom_call_target="tpu_custom_call" | custom-call | flops 24999999488 | bytes 8000000 | tf_op jit(solution)/shard_map/score/pallas_call | solution.py:514
  157.5 16.0 %merge.1 = bf16[32,4096]{1,0:T(8,128)(2,1)S(1)} custom-call(bf16[4,128,512]{2,1,0:T(8,128)(2,1)S(1)} %get-tuple-element.15.o_ref, f32[4,8,128]{2,1,0:T(8,128)S(1)} %get-tuple-element.16.lse_ref), custom_call_target="tpu_custom_call" | custom-call | tf_op jit(solution)/shard_map/merge/pallas_call | solution.py:604
  173.4 0.8 reshape.80
  174.2 0.0 copy-done.7
  174.2 0.1 copy.41
  174.3 0.1 broadcast_in_dim.44
  174.4 0.1 select_reduce_fusion
  174.5 0.0 all-to-all-done
  174.5 1.2 all_to_all.10
  175.7 0.4 fusion.4
  176.1 0.4 fusion
  176.5 0.7 reshape.81
  (3 shorter events, 0.0 us)
Async XLA Ops:
  6.8 1.3 copy-start.8
  6.8 1.6 copy-start.5
  6.8 2.3 %copy-start.6 = (f32[2880]{0:T(1024)S(1)}, f32[2880]{0:T(1024)}, u32[]{:S(2)}) copy-start(f32[2880]{0:T(1024)} %param.21) | copy-start | bytes 34564
  94.8 8.1 %copy-start.9 = (f32[64]{0:T(128)S(1)}, f32[64]{0:T(128)}, u32[]{:S(2)}) copy-start(f32[64]{0:T(128)} %param.19) | copy-start | bytes 772
  94.8 8.4 %copy-start.1 = (bf16[16,32,512]{2,1,0:T(8,128)(2,1)S(1)}, bf16[16,32,512]{2,1,0:T(8,128)(2,1)}, u32[]{:S(2)}) copy-start(bf16[16,32,512]{2,1,0:T(8,128)(2,1)} %get-tuple-element.12.q_all) | copy-start | bytes 1572868
  94.8 8.4 %copy-start.2 = (bf16[16,32,128]{2,1,0:T(8,128)(2,1)S(1)}, bf16[16,32,128]{2,1,0:T(8,128)(2,1)}, u32[]{:S(2)}) copy-start(bf16[16,32,128]{2,1,0:T(8,128)(2,1)} %get-tuple-element.13.f_all) | copy-start | bytes 393220
  94.8 8.4 %copy-start.3 = (s32[4,8,128]{2,1,0:T(8,128)S(1)}, s32[4,8,128]{2,1,0:T(8,128)}, u32[]{:S(2)}) copy-start(s32[4,8,128]{2,1,0:T(8,128)} %get-tuple-element.11.counts) | copy-start | bytes 49156
  94.8 8.4 %copy-start.4 = (s32[2,8,128]{2,1,0:T(8,128)S(1)}, s32[2,8,128]{2,1,0:T(8,128)}, u32[]{:S(2)}) copy-start(s32[2,8,128]{2,1,0:T(8,128)} %get-tuple-element.10.tables) | copy-start | bytes 24580
  94.8 79.8 %all-to-all-start = ((bf16[128,2,2880]{2,1,0:T(2,128)(2,1)}), bf16[128,2,2880]{2,1,0:T(2,128)(2,1)S(1)}, u32[]{:S(2)}, u32[]{:S(2)}) async-start(bf16[128,2,2880]{2,1,0:T(2,128)(2,1)} %all_to_all.8), calls=%async_computation | async-start | bytes 3014656 | tf_op jit(solution)/shard_map/all_to_all | solution.py:668
  103.2 2.8 %copy-start = (bf16[2,768,16,128]{3,2,1,0:T(8,128)(2,1)S(1)}, bf16[2,768,16,128]{3,2,1,0:T(8,128)(2,1)}, u32[]{:S(2)}) copy-start(bf16[2,768,16,128]{3,2,1,0:T(8,128)(2,1)} %get-tuple-element.14) | copy-start | bytes 18874372
  105.9 68.3 %copy-start.7 = (f32[1,8,4,4]{1,3,2,0:T(4,128)S(1)}, f32[1,8,4,4]{1,3,2,0:T(4,128)}, u32[]{:S(2)}) copy-start(f32[1,8,4,4]{1,3,2,0:T(4,128)} %param.23) | copy-start | bytes 1540

commit v4 on v3

--- a/solution.py
+++ b/solution.py
@@ -1,5 +1,3 @@
-import functools
-
 import jax
 import jax.numpy as jnp
 from jax import lax
@@ -62,10 +60,40 @@
     return lax.broadcasted_iota(jnp.int32, shape, axis)
 
 
+def route(id_ref, prob_ref):
+    i0 = iota((128, 128), 0)
+    i1 = iota((128, 128), 1)
+    copies = (iota((8, 128), 0) == lax.rem(iota((8, 128), 1), 8)).astype(F32)
+    group = lax.div(iota((TOPK, 128), 1), 8)
+
+    def as_row(ref):
+        row = jnp.zeros((1, 128), F32)
+        for t in range(SCORED_STEPS):
+            wide = nn(ref[t].astype(F32), copies, HIGHEST)
+            mine = group == iota((TOPK, 128), 0) + t * TOPK
+            row = row + jnp.sum(jnp.where(mine, wide, 0.0), axis=0, keepdims=True)
+        return row
+
+    ids = as_row(id_ref)
+    column = jnp.sum(jnp.where(i0 == i1, ids, 0.0), axis=1, keepdims=True)
+    earlier = jnp.logical_and(column == ids, i0 < i1)
+    rank = jnp.sum(jnp.where(earlier, 1.0, 0.0), axis=0, keepdims=True)
+    slots = iota((256, 128), 0).astype(F32) == 2.0 * ids + rank
+
+    def token(a):
+        return lax.rem(a, 8) * SCORED_STEPS + lax.div(a, 32)
+
+    owner_token = (token(iota((128, ROWS), 0)) == iota((128, ROWS), 1)).astype(BF16)
+    mine = token(iota((ROWS, 128), 1)) == iota((ROWS, 128), 0)
+    share = nt(jnp.where(mine, as_row(prob_ref), 0.0), slots.astype(F32), HIGHEST)
+    return slots.astype(BF16), owner_token, share
+
+
 def exchange_kernel(
-    q_ref, f_ref, page_ref, table_ref, count_ref, hidden_ref, gain_ref, spread_ref, up_ref, down_ref,
-    q_all, f_all, pool, tables, counts, expert_out,
-    relay, f_relay, rows_out, rows_mid, rows_sorted, rows_in, up_w, down_w, projected, active,
+    q_ref, f_ref, page_ref, owner_ref, slot_ref, count_ref, hidden_ref, gain_ref, id_ref, prob_ref,
+    up_ref, down_ref,
+    q_all, f_all, pool, tables, counts, expert_out, share_ref,
+    relay, f_relay, table_ref, rows_out, rows_mid, rows_sorted, rows_in, up_w, down_w, projected, active,
     q_send, q_recv, f_send, f_recv, a_send, a_recv, z_send, z_recv, c_send, c_recv,
     i_send, i_recv, d_send, d_recv, e_send, e_recv, local, w_sem,
 ):
@@ -102,6 +130,31 @@
         weights.append(pltpu.make_async_copy(down_ref.at[0, part], down_w.at[part], w_sem.at[4 + n]))
     for copy in weights:
         copy.start()
+
+    h32 = hidden_ref[...].astype(F32)
+    scale = lax.rsqrt(jnp.mean(h32 * h32, axis=-1, keepdims=True) + EPSILON)
+    normed = (h32 * scale * gain_ref[...]).astype(BF16)
+    slots, owner_token, share = route(id_ref, prob_ref)
+    share_ref[...] = share
+    spread = nn(slots, owner_token).astype(BF16)
+    rows_out[...] = nn(spread, normed).astype(BF16).reshape(16, 16, D)
+    pl.semaphore_wait(barrier, len(peers))
+
+    routed = []
+    for dy in range(4):
+        for dz in range(4):
+            n = dy * 4 + dz
+            source = rows_out.at[lax.rem(y + dy, 4) * 4 + lax.rem(z + dz, 4)]
+            target = rows_mid.at[y * 4 + z]
+            if n == 0:
+                copy = pltpu.make_async_copy(source, target, local.at[5])
+            else:
+                copy = pltpu.make_async_remote_copy(
+                    source, target, d_send.at[n], d_recv.at[n],
+                    device_id=beside(dy, dz), device_id_type=MESH,
+                )
+            copy.start()
+            routed.append(copy)
 
     for h in range(KEY_VALUE_HEADS):
         low, high = h * HEAD_WIDTH, (h + 1) * HEAD_WIDTH
@@ -113,7 +166,9 @@
         f_relay[h] = jnp.concatenate(
             [f_ref[:, low:high], f_ref[:, split + low : split + high]], axis=1
         )
-    pl.semaphore_wait(barrier, len(peers))
+    for xx in range(4):
+        e = z * 8 + xx * 2 + c
+        table_ref[xx] = owner_ref[e] * PAGES + slot_ref[e]
 
     def spot(segment_slot, zz, xx, cc):
         return pool.at[segment_slot, pl.ds((zz * 8 + xx * 2 + cc) * PAGES, PAGES)]
@@ -155,26 +210,6 @@
         )
         other.start()
         small.append(other)
-
-    h32 = hidden_ref[...].astype(F32)
-    scale = lax.rsqrt(jnp.mean(h32 * h32, axis=-1, keepdims=True) + EPSILON)
-    normed = (h32 * scale * gain_ref[...]).astype(BF16)
-    rows_out[...] = nn(spread_ref[...], normed).astype(BF16).reshape(16, 16, D)
-    routed = []
-    for dy in range(4):
-        for dz in range(4):
-            n = dy * 4 + dz
-            source = rows_out.at[lax.rem(y + dy, 4) * 4 + lax.rem(z + dz, 4)]
-            target = rows_mid.at[y * 4 + z]
-            if n == 0:
-                copy = pltpu.make_async_copy(source, target, local.at[5])
-            else:
-                copy = pltpu.make_async_remote_copy(
-                    source, target, d_send.at[n], d_recv.at[n],
-                    device_id=beside(dy, dz), device_id_type=MESH,
-                )
-            copy.start()
-            routed.append(copy)
 
     for dy in range(4):
         for dx in range(4):
@@ -220,16 +255,6 @@
         copy.start()
         return copy
 
-    upward, downward, further, across = [], [], [], []
-    for n in range(8):
-        if n == 0:
-            first[n].wait()
-        else:
-            first[n].wait_recv()
-        upward.append(pass_on(n, z, 0, up))
-        downward.append(pass_on(n, z, 1, down))
-        across.append(pass_on(n, z, 3, twin))
-
     for copy in routed:
         copy.wait()
     ri = iota((256, 256), 0)
@@ -256,6 +281,15 @@
             copy.start()
             delivered.append(copy)
 
+    upward, downward, further, across = [], [], [], []
+    for n in range(8):
+        if n == 0:
+            first[n].wait()
+        else:
+            first[n].wait_recv()
+        upward.append(pass_on(n, z, 0, up))
+        downward.append(pass_on(n, z, 1, down))
+        across.append(pass_on(n, z, 3, twin))
     for n in range(8):
         upward[n].wait_recv()
         if n % 2 == 0:
@@ -265,10 +299,6 @@
         if n % 2 == 1:
             further.append(pass_on(n, lax.rem(z + 1, 4), 2, down))
         across.append(pass_on(n, lax.rem(z + 1, 4), 5, twin))
-    for n in range(8):
-        further[n].wait_recv()
-        across.append(pass_on(n, lax.rem(z + 2, 4), 6, twin))
-
     for copy in weights + delivered:
         copy.wait()
 
@@ -291,6 +321,10 @@
         gate, upper = wide[:, :HID], wide[:, HID:]
         active[part, :] = ((upper + 1.0) * gate * jax.nn.sigmoid(1.702 * gate)).astype(BF16)
 
+    for n in range(8):
+        further[n].wait_recv()
+        across.append(pass_on(n, lax.rem(z + 2, 4), 6, twin))
+
     back = (slot_of(ci) == ri).astype(BF16)
     active[...] = nn(back, active[...]).astype(BF16)
 
@@ -310,7 +344,9 @@
 TILE = 384
 
 
-def exchange(queries, fresh, pages, table, count, hidden, gain, spread, gate_up, down_proj):
+def exchange(
+    queries, fresh, pages, owner, slot, count, hidden, gain, ids, prob, gate_up, down_proj
+):
     vmem = pl.BlockSpec(memory_space=pltpu.VMEM)
     anywhere = pl.BlockSpec(memory_space=pl.ANY)
     dma = pltpu.SemaphoreType.DMA
@@ -320,15 +356,17 @@
             jax.ShapeDtypeStruct((16, ROWS, HEAD_COLUMNS), BF16),
             jax.ShapeDtypeStruct((16, ROWS, 2 * HEAD_WIDTH), BF16),
             jax.ShapeDtypeStruct((2, N_EP * PAGES, PAGE_TOKENS, 2 * HEAD_WIDTH), BF16),
-            jax.ShapeDtypeStruct((2, 8, 128), jnp.int32),
-            jax.ShapeDtypeStruct((4, 8, 128), jnp.int32),
+            jax.ShapeDtypeStruct((2, 4, 2, 128), jnp.int32),
+            jax.ShapeDtypeStruct((4, N_SEQ, PROMPTS), jnp.int32),
             jax.ShapeDtypeStruct((256, D), BF16),
+            jax.ShapeDtypeStruct((ROWS, 256), F32),
         ),
-        in_specs=[vmem] * 8 + [anywhere] * 2,
-        out_specs=(anywhere,) * 5 + (vmem,),
+        in_specs=[vmem] * 10 + [anywhere] * 2,
+        out_specs=(anywhere,) * 5 + (vmem, vmem),
         scratch_shapes=[
             pltpu.VMEM((KEY_VALUE_HEADS, PAGES, PAGE_TOKENS, 2 * HEAD_WIDTH), BF16),
             pltpu.VMEM((KEY_VALUE_HEADS, ROWS, 2 * HEAD_WIDTH), BF16),
+            pltpu.VMEM((4, 2, 128), jnp.int32),
             pltpu.VMEM((16, 16, D), BF16),
             pltpu.VMEM((16, 16, D), BF16),
             pltpu.VMEM((8, 32, D), BF16),
@@ -345,7 +383,7 @@
             collective_id=1, has_side_effects=True, vmem_limit_bytes=56 << 20
         ),
         name="exchange",
-    )(queries, fresh, pages, table, count, hidden, gain, spread, gate_up, down_proj)
+    )(queries, fresh, pages, owner, slot, count, hidden, gain, ids, prob, gate_up, down_proj)
 
 
 BK = 1024
@@ -364,18 +402,24 @@
 
 
 def score_kernel(
-    tables, counts, sinks, q_all, f_all, pool, o_ref, lse_ref,
-    kv, vt, qs, limit_ref, m_ref, acc, sorted_out, s0, s1, lengths,
+    tables, counts, sinks, q_all, f_all, pool_ref, o_ref, lse_ref,
+    pool, kv, vt, qs, limit_ref, m_ref, acc, sorted_out, s0, s1, lengths, pool_sem,
 ):
     y = lax.axis_index("seq")
     outer_pair = jnp.logical_or(y == 0, y == 3)
     sink_row = sinks[0:1, :]
+    load = pltpu.make_async_copy(pool_ref, pool, pool_sem)
+    load.start()
     i0 = iota((128, 128), 0)
     i1 = iota((128, 128), 1)
     lane_row = lax.rem(iota((128, COLS), 1), ROWS).astype(F32)
 
     def ordering(e):
-        c = counts[e][0:1, :].astype(F32)
+        lane = iota((PROMPTS, 128), 1)
+        copies = (iota((PROMPTS, 128), 0) == lax.div(lax.rem(lane, ROWS), SCORED_STEPS)).astype(F32)
+        wide = nn(counts[e].astype(F32), copies, HIGHEST)
+        mine = lax.div(iota((N_SEQ, 128), 1), ROWS) == iota((N_SEQ, 128), 0)
+        c = jnp.sum(jnp.where(mine, wide, 0.0), axis=0, keepdims=True)
         n_row = jnp.where(
             outer_pair,
             jnp.minimum(c, 256.0) + jnp.maximum(c - 768.0, 0.0),
@@ -425,9 +469,10 @@
         def gather(kb, carry):
             p0 = kb * (GK // PAGE_TOKENS)
             ss = lax.div(p0, NPS)
-            row = e * 2 + lax.div(lax.rem(p0, NPS), 128)
+            lane = lax.div(lax.rem(p0, NPS), 2)
             rows = [
-                pool[tables[ss, row, i] + ss * (N_EP * PAGES)] for i in range(GK // PAGE_TOKENS)
+                pool[tables[ss, e, i % 2, lane + i // 2] + ss * (N_EP * PAGES)]
+                for i in range(GK // PAGE_TOKENS)
             ]
             for i in range(GK // BK):
                 part = rows[i * (BK // PAGE_TOKENS) : (i + 1) * (BK // PAGE_TOKENS)]
@@ -485,6 +530,7 @@
 
         return carry
 
+    load.wait()
     lax.fori_loop(0, UNITS, unit, 0)
 
     for e in range(UNITS):
@@ -517,9 +563,11 @@
             jax.ShapeDtypeStruct((UNITS, 128, HEAD_COLUMNS), BF16),
             jax.ShapeDtypeStruct((UNITS, 8, 128), F32),
         ),
-        in_specs=[pl.BlockSpec(memory_space=pltpu.SMEM)] + [vmem] * 5,
+        in_specs=[pl.BlockSpec(memory_space=pltpu.SMEM)] + [vmem] * 4
+        + [pl.BlockSpec(memory_space=pl.ANY)],
         out_specs=(vmem, vmem),
         scratch_shapes=[
+            pltpu.VMEM((2 * N_EP * PAGES, PAGE_TOKENS, 128), BF16),
             pltpu.VMEM((KEYS, 128), BF16),
             pltpu.VMEM((KEYS // BK, VROWS, BK), BF16),
             pltpu.VMEM((UNITS * CHUNKS, COLS, 128), BF16),
@@ -530,8 +578,9 @@
             pltpu.VMEM((BK, COLS), F32),
             pltpu.VMEM((BK, COLS), F32),
             pltpu.SMEM((UNITS * CHUNKS,), jnp.int32),
+            pltpu.SemaphoreType.DMA,
         ],
-        compiler_params=pltpu.CompilerParams(vmem_limit_bytes=40 << 20),
+        compiler_params=pltpu.CompilerParams(vmem_limit_bytes=60 << 20),
         cost_estimate=pl.CostEstimate(
             flops=25_000_000_000, bytes_accessed=8_000_000, transcendentals=20_000_000
         ),
@@ -539,7 +588,9 @@
     )(tables, counts, sinks, q_all, f_all, pool)
 
 
-def merge_kernel(o_ref, lse_ref, out_ref, o_all, lse_all, o_send, o_recv, l_send, l_recv, local):
+def merge_kernel(
+    o_ref, lse_ref, share_ref, rows_ref, out_ref, mix_ref, o_all, lse_all, o_send, o_recv, l_send, l_recv, local,
+):
     y, z, x, c = place()
 
     def at(dy, dx):
@@ -578,6 +629,13 @@
             for copy in pair:
                 copy.start()
             copies.extend(pair)
+
+    share = share_ref[...]
+    high = share.astype(BF16)
+    low = (share - high.astype(F32)).astype(BF16)
+    rows = rows_ref[...]
+    mix_ref[...] = (nn(high, rows) + nn(low, rows)).astype(BF16)
+
     for copy in copies:
         copy.wait()
     mine = (iota((ROWS, 128), 1) == iota((ROWS, 128), 0) + y * ROWS).astype(F32)
@@ -598,14 +656,17 @@
         out_ref[:, h * HEAD_COLUMNS : (h + 1) * HEAD_COLUMNS] = result.astype(BF16)
 
 
-def merge(o, lse):
+def merge(o, lse, share, rows):
     vmem = pl.BlockSpec(memory_space=pltpu.VMEM)
     dma = pltpu.SemaphoreType.DMA
     return pl.pallas_call(
         merge_kernel,
-        out_shape=jax.ShapeDtypeStruct((ROWS, QUERY_HEADS * HEAD_WIDTH), BF16),
-        in_specs=[vmem, vmem],
-        out_specs=vmem,
+        out_shape=(
+            jax.ShapeDtypeStruct((ROWS, QUERY_HEADS * HEAD_WIDTH), BF16),
+            jax.ShapeDtypeStruct((ROWS, D), BF16),
+        ),
+        in_specs=[vmem] * 4,
+        out_specs=(vmem, vmem),
         scratch_shapes=[
             pltpu.VMEM((16, ROWS, HEAD_COLUMNS), BF16),
             pltpu.VMEM((16, 8, 128), F32),
@@ -615,7 +676,11 @@
             collective_id=2, has_side_effects=True, vmem_limit_bytes=16 << 20
         ),
         name="merge",
-    )(o, lse)
+    )(o, lse, share, rows)
+
+
+def by_prefix(table):
+    return table[0].T.reshape(2, N_EP, NPS // 2).transpose(1, 0, 2)
 
 
 def per_device(
@@ -624,55 +689,29 @@
 ):
     y, z, x, c = place()
 
-    chosen = expert_ids.reshape(ROWS * TOPK)
-    number = jnp.arange(ROWS * TOPK, dtype=jnp.int32)
-    same = jnp.logical_and(chosen[:, None] == chosen[None, :], number[None, :] < number[:, None])
-    rank = jnp.sum(same.astype(jnp.int32), axis=1)
-    slots = (chosen * 2 + rank).reshape(ROWS, TOPK)
-    hit = slots[None, :, :] == jnp.arange(256, dtype=jnp.int32)[:, None, None]
-    spread = jnp.any(hit, axis=-1).astype(BF16)
-    weights = jnp.sum(
-        jnp.where(
-            slots[:, :, None] == jnp.arange(256, dtype=jnp.int32)[None, None, :],
-            gate_prob.reshape(ROWS, TOPK, 1),
-            0.0,
-        ),
-        axis=1,
-    )
-
-    index = (page_owner * PAGES + page_slot).reshape(4, 4, 2, NPS)
-    index = lax.dynamic_index_in_dim(index, z, 0, keepdims=False)
-    index = lax.dynamic_index_in_dim(index, c, 1, keepdims=False)
-    table = index.reshape(8, 128)
-    count = jnp.broadcast_to(jnp.repeat(page_count.reshape(32), 4)[None, :], (8, 128))
-    q_all, f_all, pool, tables, counts, result = exchange(
+    q_all, f_all, pool, tables, counts, result, share = exchange(
         queries.reshape(ROWS, QUERY_HEADS * HEAD_WIDTH),
         fresh_key_values.reshape(ROWS, 2 * KEY_VALUE_HEADS * HEAD_WIDTH),
         key_value_pages.reshape(PAGES * PAGE_TOKENS, 2 * KEY_VALUE_HEADS * HEAD_WIDTH),
-        table,
-        count,
+        by_prefix(page_owner),
+        by_prefix(page_slot),
+        page_count,
         hidden.reshape(ROWS, D),
         norm_gain.reshape(1, D),
-        spread,
+        expert_ids[0].transpose(1, 2, 0),
+        gate_prob[0].transpose(1, 2, 0),
         gate_up,
         down_proj,
     )
+    returned = lax.all_to_all(result, ("seq", "ep"), split_axis=0, concat_axis=0, tiled=True)
     head_sinks = lax.dynamic_slice_in_dim(sinks, head_of(y, x) * GROUP, GROUP)
     sink_rows = jnp.broadcast_to(jnp.repeat(head_sinks, ROWS)[None, :], (8, COLS))
     o, lse = score(
         tables, counts, sink_rows, q_all, f_all,
         pool.reshape(2 * N_EP * PAGES, PAGE_TOKENS, 2 * HEAD_WIDTH),
     )
-    attention = merge(o, lse).reshape(queries.shape)
-
-    returned = lax.all_to_all(result, ("seq", "ep"), split_axis=0, concat_axis=0, tiled=True)
-    high = weights.astype(BF16)
-    low = (weights - high.astype(F32)).astype(BF16)
-    mixture = (
-        jnp.dot(high, returned, preferred_element_type=F32)
-        + jnp.dot(low, returned, preferred_element_type=F32)
-    ).astype(BF16).reshape(hidden.shape)
-    return (attention, mixture)
+    attention, mixture = merge(o, lse, share, returned)
+    return (attention.reshape(queries.shape), mixture.reshape(hidden.shape))
 
 
 def solution(mesh):

time: 179 us -> 181 us (1.011)
  Pallas kernels: 145 us -> 155 us
  local copies, waits for them, and re-layouts: 20.2 us -> 16.4 us
  other arithmetic: 1.89 us -> 0 us
    pallas_call x1, Pallas kernels: 51.5 us -> 58.2 us  [score(): pl.pallas_call(score_kernel, out_shape=(jax.ShapeDtypeStruct((UNITS, 128,...]
    unnamed x22 -> x8, local copies, waits for them, and re-layouts: 3.71 us -> 0.02 us
    pallas_call x1, Pallas kernels: 78 us -> 81.6 us  [exchange(): pl.pallas_call(exchange_kernel, out_shape=(jax.ShapeDtypeStruct((16, ROWS...]
    all_to_all x2, local copies, waits for them, and re-layouts: 5.52 us -> 7.87 us  [per_device(): lax.all_to_all(result, ('seq', 'ep'), split_axis=0, concat_axis=0, tiled=...]
  transfers between devices with their start and end apart: 1 -> 1, of which waited for: 0 -> 0; matrix products, arithmetic and copies ran while one was open for 1% -> 0% of each run, Pallas kernels for 38% -> 32%
where the time goes in v4:
time: 181 us; the launch traced here: 180 us
  Pallas kernels  155 us (86%)
  local copies, waits for them, and re-layouts  16.4 us (9%)
  starting transfers between devices  7.68 us (4%)
    pallas_call x1, Pallas kernels, exchange(): pl.pallas_call(exchange_kernel, out_shape=(jax.ShapeDtypeStruct((16, ROWS...  81.6 us
    pallas_call x1, Pallas kernels, score(): pl.pallas_call(score_kernel, out_shape=(jax.ShapeDtypeStruct((UNITS, 128,...  58.2 us
    pallas_call x1, Pallas kernels, merge(): pl.pallas_call(merge_kernel, out_shape=(jax.ShapeDtypeStruct((ROWS, QUERY...  15 us
    all_to_all x2, local copies, waits for them, and re-layouts, per_device(): lax.all_to_all(result, ('seq', 'ep'), split_axis=0, concat_axis=0, tiled=...  7.87 us
    all_to_all x1, starting transfers between devices, per_device(): lax.all_to_all(result, ('seq', 'ep'), split_axis=0, concat_axis=0, tiled=...  7.68 us
  transfers between devices with their start and end apart: 1, of which 0 were waited for; matrix products, arithmetic and copies ran while one was open for 0% of the time, Pallas kernels for 32%

profile of v4, /device:TPU:0, one launch (start us, length us, event | category | flops | bytes accessed | tf_op | source)
XLA Modules:
  0.0 179.7 jit_solution(543667220151643910)
XLA Ops:
  0.6 1.3 reshape.43.gain_ref
  1.9 1.5 reshape.38.f_ref
  3.4 1.7 reshape.42.hidden_ref
  5.1 1.7 reshape.37.q_ref
  6.8 81.6 %exchange.1 = (bf16[16,32,512]{2,1,0:T(8,128)(2,1)}, bf16[16,32,128]{2,1,0:T(8,128)(2,1)}, bf16[2,768,16,128]{3,2,1,0:T(8,128)(2,1)}, s32[2,4,2,128]{3,2,1,0:T(2...) custom-call(bf16[32,4096]{1,0:T(8,128)(2,1)} %reshape.37.q_ref, ...), custom_call_target="tpu_custom_call" | custom-call | tf_op jit(solution)/shard_map/exchange/pallas_call | solution.py:353
  88.4 4.3 %all_to_all.7 = bf16[128,2,2880]{2,1,0:T(2,128)(2,1)} reshape(bf16[256,2880]{1,0:T(8,128)(2,1)} %get-tuple-element.21) | data formatting | bytes 2949120 | tf_op jit(solution)/shard_map/all_to_all | solution.py:706
  92.7 0.0 copy-start.3
  92.7 7.7 %all-to-all-start = ((bf16[128,2,2880]{2,1,0:T(2,128)(2,1)}), bf16[128,2,2880]{2,1,0:T(2,128)(2,1)}, u32[]{:S(2)}, u32[]{:S(2)}) async-start(bf16[128,2,2880]{2,1,0:T(2,128)(2,1)} %all_to_all.7), calls=%async_computation | async-start | bytes 3014656 | tf_op jit(solution)/shard_map/all_to_all | solution.py:706
  100.4 0.0 copy-done.3
  100.4 0.1 dynamic_slice.3
  100.5 0.1 broadcast_in_dim.10
  100.6 0.1 broadcast_in_dim.11
  100.7 0.6 broadcast_in_dim.12.sinks
  101.3 58.2 %score.1 = (bf16[4,128,512]{2,1,0:T(8,128)(2,1)}, f32[4,8,128]{2,1,0:T(8,128)}) custom-call(s32[2,4,2,128]{3,2,1,0:T(2,128)} %get-tuple-element.13.tables, s32[4,4,8]{2,1,0:T(4,128)} %get-tuple-element.14.counts, f32[8,256]{1,0:T(8,128)} %broadcast_in_dim.12.sinks, bf16[16,32,512]{2,1,0:T(8,128)(2,1)} %get-tuple-element.15.q_all, ...), custom_call_target="tpu_custom_call" | custom-call | flops 24999999488 | bytes 8000000 | tf_op jit(solution)/shard_map/score/pallas_call | solution.py:560
  159.5 0.0 copy-start
  159.5 0.0 copy-start.1
  159.5 0.0 copy-start.2
  159.5 0.0 all-to-all-done
  159.6 3.5 %all_to_all.9.rows_ref = bf16[256,2880]{1,0:T(8,128)(2,1)S(1)} reshape(bf16[128,2,2880]{2,1,0:T(2,128)(2,1)} %all-to-all-done) | data formatting | bytes 2949120 | tf_op jit(solution)/shard_map/all_to_all | solution.py:706
  163.1 0.0 copy-done
  163.1 0.0 copy-done.1
  163.1 0.0 copy-done.2
  163.1 15.0 %merge.1 = (bf16[32,4096]{1,0:T(8,128)(2,1)S(1)}, bf16[32,2880]{1,0:T(8,128)(2,1)S(1)}) custom-call(bf16[4,128,512]{2,1,0:T(8,128)(2,1)S(1)} %copy-done, f32[4,8,128]{2,1,0:T(8,128)S(1)} %copy-done.2, f32[32,256]{1,0:T(8,128)S(1)} %copy-done.1, bf16[256,2880]{1,0:T(8,128)(2,1)S(1)} %all_to_all.9.rows_ref), custom_call_target="tpu_custom_call" | custom-call | tf_op jit(solution)/shard_map/merge/pallas_call | solution.py:662
  178.1 0.8 reshape.45
  178.9 0.7 reshape.46
Async XLA Ops:
  92.7 7.7 %copy-start.3 = (f32[64]{0:T(128)S(1)}, f32[64]{0:T(128)}, u32[]{:S(2)}) copy-start(f32[64]{0:T(128)} %param.19) | copy-start | bytes 772
  92.7 66.8 %all-to-all-start = ((bf16[128,2,2880]{2,1,0:T(2,128)(2,1)}), bf16[128,2,2880]{2,1,0:T(2,128)(2,1)}, u32[]{:S(2)}, u32[]{:S(2)}) async-start(bf16[128,2,2880]{2,1,0:T(2,128)(2,1)} %all_to_all.7), calls=%async_computation | async-start | bytes 3014656 | tf_op jit(solution)/shard_map/all_to_all | solution.py:706
  159.5 3.6 %copy-start = (bf16[4,128,512]{2,1,0:T(8,128)(2,1)S(1)}, bf16[4,128,512]{2,1,0:T(8,128)(2,1)}, u32[]{:S(2)}) copy-start(bf16[4,128,512]{2,1,0:T(8,128)(2,1)} %get-tuple-element.18.o_ref) | copy-start | bytes 1572868
  159.5 3.6 %copy-start.1 = (f32[32,256]{1,0:T(8,128)S(1)}, f32[32,256]{1,0:T(8,128)}, u32[]{:S(2)}) copy-start(f32[32,256]{1,0:T(8,128)} %get-tuple-element.20.share_ref) | copy-start | bytes 98308
  159.5 3.6 %copy-start.2 = (f32[4,8,128]{2,1,0:T(8,128)S(1)}, f32[4,8,128]{2,1,0:T(8,128)}, u32[]{:S(2)}) copy-start(f32[4,8,128]{2,1,0:T(8,128)} %get-tuple-element.19.lse_ref) | copy-start | bytes 49156

commit v5 on v4

--- a/solution.py
+++ b/solution.py
@@ -60,6 +60,9 @@
     return lax.broadcasted_iota(jnp.int32, shape, axis)
 
 
+PARTS = ((0, 1024), (1024, 1024), (2048, D - 2048))
+
+
 def route(id_ref, prob_ref):
     i0 = iota((128, 128), 0)
     i1 = iota((128, 128), 1)
@@ -93,12 +96,15 @@
     q_ref, f_ref, page_ref, owner_ref, slot_ref, count_ref, hidden_ref, gain_ref, id_ref, prob_ref,
     up_ref, down_ref,
     q_all, f_all, pool, tables, counts, expert_out, share_ref,
-    relay, f_relay, table_ref, rows_out, rows_mid, rows_sorted, rows_in, up_w, down_w, projected, active,
+    relay, f_relay, table_ref, out0, out1, out2, mid0, mid1, mid2, sorted0, sorted1, sorted2,
+    in0, in1, in2, up_w, down_w, projected, active,
     q_send, q_recv, f_send, f_recv, a_send, a_recv, z_send, z_recv, c_send, c_recv,
     i_send, i_recv, d_send, d_recv, e_send, e_recv, local, w_sem,
 ):
     y, z, x, c = place()
     mate = 3 - y
+    rows_out, rows_mid = (out0, out1, out2), (mid0, mid1, mid2)
+    rows_sorted, rows_in = (sorted0, sorted1, sorted2), (in0, in1, in2)
 
     def at(dy, dx):
         return device(lax.rem(y + dy, 4), z, lax.rem(x + dx, 4), c)
@@ -137,24 +143,27 @@
     slots, owner_token, share = route(id_ref, prob_ref)
     share_ref[...] = share
     spread = nn(slots, owner_token).astype(BF16)
-    rows_out[...] = nn(spread, normed).astype(BF16).reshape(16, 16, D)
+    for k, (first_column, columns) in enumerate(PARTS):
+        piece = normed[:, first_column : first_column + columns]
+        rows_out[k][...] = nn(spread, piece).astype(BF16).reshape(16, 16, columns)
     pl.semaphore_wait(barrier, len(peers))
 
     routed = []
-    for dy in range(4):
-        for dz in range(4):
-            n = dy * 4 + dz
-            source = rows_out.at[lax.rem(y + dy, 4) * 4 + lax.rem(z + dz, 4)]
-            target = rows_mid.at[y * 4 + z]
-            if n == 0:
-                copy = pltpu.make_async_copy(source, target, local.at[5])
-            else:
-                copy = pltpu.make_async_remote_copy(
-                    source, target, d_send.at[n], d_recv.at[n],
-                    device_id=beside(dy, dz), device_id_type=MESH,
-                )
-            copy.start()
-            routed.append(copy)
+    for k in range(len(PARTS)):
+        for dy in range(4):
+            for dz in range(4):
+                n = dy * 4 + dz
+                source = rows_out[k].at[lax.rem(y + dy, 4) * 4 + lax.rem(z + dz, 4)]
+                target = rows_mid[k].at[y * 4 + z]
+                if n == 0:
+                    copy = pltpu.make_async_copy(source, target, local.at[5 + 2 * k])
+                else:
+                    copy = pltpu.make_async_remote_copy(
+                        source, target, d_send.at[k * 16 + n], d_recv.at[k * 16 + n],
+                        device_id=beside(dy, dz), device_id_type=MESH,
+                    )
+                copy.start()
+                routed.append(copy)
 
     for h in range(KEY_VALUE_HEADS):
         low, high = h * HEAD_WIDTH, (h + 1) * HEAD_WIDTH
@@ -255,8 +264,6 @@
         copy.start()
         return copy
 
-    for copy in routed:
-        copy.wait()
     ri = iota((256, 256), 0)
     ci = iota((256, 256), 1)
 
@@ -264,22 +271,26 @@
         return lax.div(lax.rem(i, 32), 2) * 16 + lax.div(i, 32) * 2 + lax.rem(i, 2)
 
     regroup = (slot_of(ri) == ci).astype(BF16)
-    rows_sorted[...] = nn(regroup, rows_mid[...].reshape(256, D)).astype(BF16).reshape(8, 32, D)
-    delivered = []
-    for dx in range(4):
-        for dc in range(2):
-            n = dx * 2 + dc
-            source = rows_sorted.at[lax.rem(x + dx, 4) * 2 + lax.rem(c + dc, 2)]
-            target = rows_in.at[x * 2 + c]
-            if n == 0:
-                copy = pltpu.make_async_copy(source, target, local.at[6])
-            else:
-                copy = pltpu.make_async_remote_copy(
-                    source, target, e_send.at[n], e_recv.at[n],
-                    device_id=around(dx, dc), device_id_type=MESH,
-                )
-            copy.start()
-            delivered.append(copy)
+    delivered = [[], [], []]
+    for k, (_, columns) in enumerate(PARTS):
+        for copy in routed[k * 16 : (k + 1) * 16]:
+            copy.wait()
+        moved = nn(regroup, rows_mid[k][...].reshape(256, columns)).astype(BF16)
+        rows_sorted[k][...] = moved.reshape(8, 32, columns)
+        for dx in range(4):
+            for dc in range(2):
+                n = dx * 2 + dc
+                source = rows_sorted[k].at[lax.rem(x + dx, 4) * 2 + lax.rem(c + dc, 2)]
+                target = rows_in[k].at[x * 2 + c]
+                if n == 0:
+                    copy = pltpu.make_async_copy(source, target, local.at[6 + 2 * k])
+                else:
+                    copy = pltpu.make_async_remote_copy(
+                        source, target, e_send.at[k * 8 + n], e_recv.at[k * 8 + n],
+                        device_id=around(dx, dc), device_id_type=MESH,
+                    )
+                copy.start()
+                delivered[k].append(copy)
 
     upward, downward, further, across = [], [], [], []
     for n in range(8):
@@ -290,7 +301,8 @@
         upward.append(pass_on(n, z, 0, up))
         downward.append(pass_on(n, z, 1, down))
         across.append(pass_on(n, z, 3, twin))
-    for n in range(8):
+
+    def forward(n):
         upward[n].wait_recv()
         if n % 2 == 0:
             further.append(pass_on(n, lax.rem(z + 3, 4), 2, up))
@@ -299,7 +311,8 @@
         if n % 2 == 1:
             further.append(pass_on(n, lax.rem(z + 1, 4), 2, down))
         across.append(pass_on(n, lax.rem(z + 1, 4), 5, twin))
-    for copy in weights + delivered:
+
+    for copy in weights:
         copy.wait()
 
     def tiles(work):
@@ -309,10 +322,25 @@
 
         work(pl.ds(D // TILE * TILE, D % TILE))
 
-    def project(part):
-        projected[:, part] = nn(rows_in[...].reshape(256, D), up_w[:, part])
-
-    tiles(project)
+    def project(k):
+        first_column, columns = PARTS[k]
+        for copy in delivered[k]:
+            copy.wait()
+
+        def work(part):
+            rows = rows_in[k][...].reshape(256, columns)
+            term = nn(rows, up_w[first_column : first_column + columns, part])
+            projected[:, part] = term if k == 0 else projected[:, part] + term
+
+        tiles(work)
+
+    project(0)
+    project(1)
+    for n in range(4):
+        forward(n)
+    project(2)
+    for n in range(4, 8):
+        forward(n)
 
     @pl.loop(0, 8)
     def _(j):
@@ -321,18 +349,18 @@
         gate, upper = wide[:, :HID], wide[:, HID:]
         active[part, :] = ((upper + 1.0) * gate * jax.nn.sigmoid(1.702 * gate)).astype(BF16)
 
+    back = (slot_of(ci) == ri).astype(BF16)
+    active[...] = nn(back, active[...]).astype(BF16)
+
+    def finish(part):
+        rows = nn(active[...], down_w[:, part]).astype(BF16)
+        expert_out[:, :, part] = rows.reshape(128, 2, rows.shape[1])
+
+    tiles(finish)
+
     for n in range(8):
         further[n].wait_recv()
         across.append(pass_on(n, lax.rem(z + 2, 4), 6, twin))
-
-    back = (slot_of(ci) == ri).astype(BF16)
-    active[...] = nn(back, active[...]).astype(BF16)
-
-    def finish(part):
-        expert_out[:, part] = nn(active[...], down_w[:, part]).astype(BF16)
-
-    tiles(finish)
-
     for copy in across:
         copy.wait()
     for copy in first[1:] + upward + downward + further:
@@ -341,7 +369,7 @@
         copy.wait()
 
 
-TILE = 384
+TILE = 512
 
 
 def exchange(
@@ -358,7 +386,7 @@
             jax.ShapeDtypeStruct((2, N_EP * PAGES, PAGE_TOKENS, 2 * HEAD_WIDTH), BF16),
             jax.ShapeDtypeStruct((2, 4, 2, 128), jnp.int32),
             jax.ShapeDtypeStruct((4, N_SEQ, PROMPTS), jnp.int32),
-            jax.ShapeDtypeStruct((256, D), BF16),
+            jax.ShapeDtypeStruct((128, 2, D), BF16),
             jax.ShapeDtypeStruct((ROWS, 256), F32),
         ),
         in_specs=[vmem] * 10 + [anywhere] * 2,
@@ -367,17 +395,15 @@
             pltpu.VMEM((KEY_VALUE_HEADS, PAGES, PAGE_TOKENS, 2 * HEAD_WIDTH), BF16),
             pltpu.VMEM((KEY_VALUE_HEADS, ROWS, 2 * HEAD_WIDTH), BF16),
             pltpu.VMEM((4, 2, 128), jnp.int32),
-            pltpu.VMEM((16, 16, D), BF16),
-            pltpu.VMEM((16, 16, D), BF16),
-            pltpu.VMEM((8, 32, D), BF16),
-            pltpu.VMEM((8, 32, D), BF16),
+            *[pltpu.VMEM((16, 16, columns), BF16) for _, columns in PARTS * 2],
+            *[pltpu.VMEM((8, 32, columns), BF16) for _, columns in PARTS * 2],
             pltpu.VMEM((D, 2 * HID), BF16),
             pltpu.VMEM((HID, D), BF16),
             pltpu.VMEM((256, 2 * HID), F32),
             pltpu.VMEM((256, HID), BF16),
             dma((16,)), dma((16,)), dma((16,)), dma((16,)), dma((8,)), dma((8,)),
             dma((24,)), dma((24,)), dma((32,)), dma((32,)), dma((4,)), dma((4,)),
-            dma((16,)), dma((16,)), dma((8,)), dma((8,)), dma((7,)), dma((6,)),
+            dma((48,)), dma((48,)), dma((24,)), dma((24,)), dma((11,)), dma((6,)),
         ],
         compiler_params=pltpu.CompilerParams(
             collective_id=1, has_side_effects=True, vmem_limit_bytes=56 << 20
@@ -402,14 +428,12 @@
 
 
 def score_kernel(
-    tables, counts, sinks, q_all, f_all, pool_ref, o_ref, lse_ref,
-    pool, kv, vt, qs, limit_ref, m_ref, acc, sorted_out, s0, s1, lengths, pool_sem,
+    tables, counts, sinks, q_all, f_all, pool, o_ref, lse_ref,
+    kv, vt, qs, limit_ref, m_ref, acc, sorted_out, s0, s1, places, lengths,
 ):
     y = lax.axis_index("seq")
     outer_pair = jnp.logical_or(y == 0, y == 3)
     sink_row = sinks[0:1, :]
-    load = pltpu.make_async_copy(pool_ref, pool, pool_sem)
-    load.start()
     i0 = iota((128, 128), 0)
     i1 = iota((128, 128), 1)
     lane_row = lax.rem(iota((128, COLS), 1), ROWS).astype(F32)
@@ -432,6 +456,7 @@
 
     for e in range(UNITS):
         n_row, n_col, pos_col = ordering(e)
+        places[e] = pos_col
         ahead = jnp.logical_or(n_col > n_row, jnp.logical_and(n_col == n_row, i0 < i1))
         pos_row = jnp.sum(jnp.where(ahead, 1.0, 0.0), axis=0, keepdims=True)
         perm = (pos_row == i0.astype(F32)).astype(BF16)
@@ -530,11 +555,10 @@
 
         return carry
 
-    load.wait()
     lax.fori_loop(0, UNITS, unit, 0)
 
     for e in range(UNITS):
-        _, _, pos_col = ordering(e)
+        pos_col = places[e]
         perm_t = (pos_col == i1.astype(F32)).astype(BF16)
         lse = jnp.zeros((8, 128), F32)
         for ch in range(CHUNKS):
@@ -563,11 +587,9 @@
             jax.ShapeDtypeStruct((UNITS, 128, HEAD_COLUMNS), BF16),
             jax.ShapeDtypeStruct((UNITS, 8, 128), F32),
         ),
-        in_specs=[pl.BlockSpec(memory_space=pltpu.SMEM)] + [vmem] * 4
-        + [pl.BlockSpec(memory_space=pl.ANY)],
+        in_specs=[pl.BlockSpec(memory_space=pltpu.SMEM)] + [vmem] * 5,
         out_specs=(vmem, vmem),
         scratch_shapes=[
-            pltpu.VMEM((2 * N_EP * PAGES, PAGE_TOKENS, 128), BF16),
             pltpu.VMEM((KEYS, 128), BF16),
             pltpu.VMEM((KEYS // BK, VROWS, BK), BF16),
             pltpu.VMEM((UNITS * CHUNKS, COLS, 128), BF16),
@@ -577,10 +599,10 @@
             pltpu.VMEM((UNITS, 128, HEAD_COLUMNS), BF16),
             pltpu.VMEM((BK, COLS), F32),
             pltpu.VMEM((BK, COLS), F32),
+            pltpu.VMEM((UNITS, 128, 1), F32),
             pltpu.SMEM((UNITS * CHUNKS,), jnp.int32),
-            pltpu.SemaphoreType.DMA,
         ],
-        compiler_params=pltpu.CompilerParams(vmem_limit_bytes=60 << 20),
+        compiler_params=pltpu.CompilerParams(vmem_limit_bytes=40 << 20),
         cost_estimate=pl.CostEstimate(
             flops=25_000_000_000, bytes_accessed=8_000_000, transcendentals=20_000_000
         ),
@@ -633,7 +655,7 @@
     share = share_ref[...]
     high = share.astype(BF16)
     low = (share - high.astype(F32)).astype(BF16)
-    rows = rows_ref[...]
+    rows = rows_ref[...].reshape(256, D)
     mix_ref[...] = (nn(high, rows) + nn(low, rows)).astype(BF16)
 
     for copy in copies:

time: 181 us -> 166 us (0.917)
  Pallas kernels: 155 us -> 144 us
  local copies, waits for them, and re-layouts: 16.4 us -> 14.1 us
    all_to_all x2 -> x0, local copies, waits for them, and re-layouts: 7.87 us -> none  [per_device(): lax.all_to_all(result, ('seq', 'ep'), split_axis=0, concat_axis=0, tiled=...]
    pallas_call x1, Pallas kernels: 81.6 us -> 73.9 us  [exchange(): pl.pallas_call(exchange_kernel, out_shape=(jax.ShapeDtypeStruct((16, ROWS...]
    unnamed x8 -> x14, local copies, waits for them, and re-layouts: 0.02 us -> 6.13 us
    pallas_call x1, Pallas kernels: 58.2 us -> 53.3 us  [score(): pl.pallas_call(score_kernel, out_shape=(jax.ShapeDtypeStruct((UNITS, 128,...]
where the time goes in v5:
time: 166 us
  Pallas kernels  144 us (87%)
  local copies, waits for them, and re-layouts  14.1 us (8%)
  starting transfers between devices  7.43 us (4%)
    pallas_call x1, Pallas kernels, exchange(): pl.pallas_call(exchange_kernel, out_shape=(jax.ShapeDtypeStruct((16, ROWS...  73.9 us
    pallas_call x1, Pallas kernels, score(): pl.pallas_call(score_kernel, out_shape=(jax.ShapeDtypeStruct((UNITS, 128,...  53.3 us
    pallas_call x1, Pallas kernels, merge(): pl.pallas_call(merge_kernel, out_shape=(jax.ShapeDtypeStruct((ROWS, QUERY...  16.5 us
    all_to_all x1, starting transfers between devices, per_device(): lax.all_to_all(result, ('seq', 'ep'), split_axis=0, concat_axis=0, tiled=...  7.43 us
    unnamed x14, local copies, waits for them, and re-layouts  6.13 us
  transfers between devices with their start and end apart: 1, of which 0 were waited for; matrix products, arithmetic and copies ran while one was open for 0% of the time, Pallas kernels for 32%

profile of v5, /device:TPU:0, one launch (start us, length us, event | category | flops | bytes accessed | tf_op | source)
XLA Modules:
  0.0 165.9 jit_solution(9403942170969606125)
XLA Ops:
  0.6 1.3 reshape.41.gain_ref
  1.9 1.5 reshape.36.f_ref
  3.4 1.7 %reshape.40.hidden_ref = bf16[32,2880]{1,0:T(8,128)(2,1)} reshape(bf16[1,8,4,2880]{3,2,1,0:T(4,128)(2,1)} %param.20) | data formatting | bytes 368640 | tf_op jit(solution)/shard_map/reshape | solution.py:721
  5.1 1.7 %reshape.35.q_ref = bf16[32,4096]{1,0:T(8,128)(2,1)} reshape(bf16[1,8,4,4096]{3,2,1,0:T(4,128)(2,1)} %param.13) | data formatting | bytes 524288 | tf_op jit(solution)/shard_map/reshape | solution.py:715
  6.8 0.0 copy-start.6
  6.8 73.9 %exchange.1 = (bf16[16,32,512]{2,1,0:T(8,128)(2,1)}, bf16[16,32,128]{2,1,0:T(8,128)(2,1)}, bf16[2,768,16,128]{3,2,1,0:T(8,128)(2,1)}, s32[2,4,2,128]{3,2,1,0:T(2...) custom-call(bf16[32,4096]{1,0:T(8,128)(2,1)} %reshape.35.q_ref, ...), custom_call_target="tpu_custom_call" | custom-call | tf_op jit(solution)/shard_map/exchange/pallas_call | solution.py:381
  80.7 7.4 %all-to-all-start = ((bf16[128,2,2880]{2,1,0:T(2,128)(2,1)}), bf16[128,2,2880]{2,1,0:T(2,128)(2,1)S(1)}, u32[]{:S(2)}, u32[]{:S(2)}) async-start(bf16[128,2,2880]{2,1,0:T(2,128)(2,1)} %get-tuple-element.21), calls=%async_computation | async-start | bytes 3014656 | tf_op jit(solution)/shard_map/all_to_all | solution.py:728
  88.2 0.0 copy-done.6
  88.2 0.1 dynamic_slice.3
  88.3 0.1 broadcast_in_dim.10
  88.3 0.1 broadcast_in_dim.11
  88.4 0.0 copy-start.1
  88.4 2.8 %copy-done.1 = bf16[2,768,16,128]{3,2,1,0:T(8,128)(2,1)S(1)} copy-done((bf16[2,768,16,128]{3,2,1,0:T(8,128)(2,1)S(1)}, bf16[2,768,16,128]{3,2,1,0:T(8,128)(2,1)}, u32[]{:S(2)}) %copy-start.1) | copy-done | bytes 6291480
  91.2 0.0 copy-start.2
  91.2 1.0 copy-done.2
  92.3 0.0 copy-start.3
  92.3 0.9 copy-done.3
  93.2 0.0 copy-start.4
  93.2 0.7 copy-done.4
  93.9 0.0 copy-start.5
  93.9 0.7 copy-done.5
  94.6 0.0 copy-start
  94.6 53.3 %score.1 = (bf16[4,128,512]{2,1,0:T(8,128)(2,1)S(1)}, f32[4,8,128]{2,1,0:T(8,128)S(1)}) custom-call(s32[2,4,2,128]{3,2,1,0:T(2,128)S(1)} %copy-done.4, s32[4,4,8]{2,1,0:T(4,128)S(1)} %copy-done.5, f32[8,256]{1,0:T(8,128)S(1)} %broadcast_in_dim.12.sinks, bf16[16,32,512]{2,1,0:T(8,128)(2,1)S(1)} %copy-done.2, bf16[16,32,128]{2,1,0:T(8,128)(2,1)S(1)} %copy-done.3, ...), custom_call_target="tpu_custom_call" | custom-call | flops 24999999488 | bytes 8000000 | tf_op jit(solution)/shard_map/score/pallas_call | solution.py:584
  147.8 0.0 all-to-all-done.rows_ref
  147.8 0.0 copy-done
  147.9 16.5 %merge.1 = (bf16[32,4096]{1,0:T(8,128)(2,1)S(1)}, bf16[32,2880]{1,0:T(8,128)(2,1)S(1)}) custom-call(bf16[4,128,512]{2,1,0:T(8,128)(2,1)S(1)} %get-tuple-element.18.o_ref, f32[4,8,128]{2,1,0:T(8,128)S(1)} %get-tuple-element.19.lse_ref, f32[32,256]{1,0:T(8,128)S(1)} %copy-done, bf16[128,2,2880]{2,1,0:T(2,128)(2,1)S(1)} %all-to-all-done.rows_ref), custom_call_target="tpu_custom_call" | custom-call | tf_op jit(solution)/shard_map/merge/pallas_call | solution.py:684
  164.4 0.8 reshape.43
  165.2 0.7 reshape.44
  (1 shorter events, 0.0 us)
Async XLA Ops:
  6.8 81.4 %copy-start.6 = (f32[64]{0:T(128)S(1)}, f32[64]{0:T(128)}, u32[]{:S(2)}) copy-start(f32[64]{0:T(128)} %param.19) | copy-start | bytes 772
  80.7 67.1 %all-to-all-start = ((bf16[128,2,2880]{2,1,0:T(2,128)(2,1)}), bf16[128,2,2880]{2,1,0:T(2,128)(2,1)S(1)}, u32[]{:S(2)}, u32[]{:S(2)}) async-start(bf16[128,2,2880]{2,1,0:T(2,128)(2,1)} %get-tuple-element.21), calls=%async_computation | async-start | bytes 3014656 | tf_op jit(solution)/shard_map/all_to_all | solution.py:728
  88.4 2.8 %copy-start.1 = (bf16[2,768,16,128]{3,2,1,0:T(8,128)(2,1)S(1)}, bf16[2,768,16,128]{3,2,1,0:T(8,128)(2,1)}, u32[]{:S(2)}) copy-start(bf16[2,768,16,128]{3,2,1,0:T(8,128)(2,1)} %get-tuple-element.17) | copy-start | bytes 18874372
  91.2 1.0 copy-start.2
  92.3 0.9 copy-start.3
  93.2 0.7 copy-start.4
  93.9 0.7 copy-start.5
  94.6 53.3 %copy-start = (f32[32,256]{1,0:T(8,128)S(1)}, f32[32,256]{1,0:T(8,128)}, u32[]{:S(2)}) copy-start(f32[32,256]{1,0:T(8,128)} %get-tuple-element.20.share_ref) | copy-start | bytes 98308

commit v6 on v5

--- a/solution.py
+++ b/solution.py
@@ -96,7 +96,7 @@
     q_ref, f_ref, page_ref, owner_ref, slot_ref, count_ref, hidden_ref, gain_ref, id_ref, prob_ref,
     up_ref, down_ref,
     q_all, f_all, pool, tables, counts, expert_out, share_ref,
-    relay, f_relay, table_ref, out0, out1, out2, mid0, mid1, mid2, sorted0, sorted1, sorted2,
+    relay, f_relay, q_rows, table_ref, out0, out1, out2, mid0, mid1, mid2, sorted0, sorted1, sorted2,
     in0, in1, in2, up_w, down_w, projected, active,
     q_send, q_recv, f_send, f_recv, a_send, a_recv, z_send, z_recv, c_send, c_recv,
     i_send, i_recv, d_send, d_recv, e_send, e_recv, local, w_sem,
@@ -137,34 +137,7 @@
     for copy in weights:
         copy.start()
 
-    h32 = hidden_ref[...].astype(F32)
-    scale = lax.rsqrt(jnp.mean(h32 * h32, axis=-1, keepdims=True) + EPSILON)
-    normed = (h32 * scale * gain_ref[...]).astype(BF16)
-    slots, owner_token, share = route(id_ref, prob_ref)
-    share_ref[...] = share
-    spread = nn(slots, owner_token).astype(BF16)
-    for k, (first_column, columns) in enumerate(PARTS):
-        piece = normed[:, first_column : first_column + columns]
-        rows_out[k][...] = nn(spread, piece).astype(BF16).reshape(16, 16, columns)
-    pl.semaphore_wait(barrier, len(peers))
-
-    routed = []
-    for k in range(len(PARTS)):
-        for dy in range(4):
-            for dz in range(4):
-                n = dy * 4 + dz
-                source = rows_out[k].at[lax.rem(y + dy, 4) * 4 + lax.rem(z + dz, 4)]
-                target = rows_mid[k].at[y * 4 + z]
-                if n == 0:
-                    copy = pltpu.make_async_copy(source, target, local.at[5 + 2 * k])
-                else:
-                    copy = pltpu.make_async_remote_copy(
-                        source, target, d_send.at[k * 16 + n], d_recv.at[k * 16 + n],
-                        device_id=beside(dy, dz), device_id_type=MESH,
-                    )
-                copy.start()
-                routed.append(copy)
-
+    fresh = f_ref[...].reshape(ROWS, f_ref.shape[2])
     for h in range(KEY_VALUE_HEADS):
         low, high = h * HEAD_WIDTH, (h + 1) * HEAD_WIDTH
         split = KEY_VALUE_HEADS * HEAD_WIDTH
@@ -173,11 +146,13 @@
         )
         relay[h] = rows.reshape(PAGES, PAGE_TOKENS, 2 * HEAD_WIDTH)
         f_relay[h] = jnp.concatenate(
-            [f_ref[:, low:high], f_ref[:, split + low : split + high]], axis=1
+            [fresh[:, low:high], fresh[:, split + low : split + high]], axis=1
         )
     for xx in range(4):
         e = z * 8 + xx * 2 + c
         table_ref[xx] = owner_ref[e] * PAGES + slot_ref[e]
+
+    pl.semaphore_wait(barrier, len(peers))
 
     def spot(segment_slot, zz, xx, cc):
         return pool.at[segment_slot, pl.ds((zz * 8 + xx * 2 + cc) * PAGES, PAGES)]
@@ -220,11 +195,94 @@
         other.start()
         small.append(other)
 
+    h32 = hidden_ref[...].reshape(ROWS, D).astype(F32)
+    scale = lax.rsqrt(jnp.mean(h32 * h32, axis=-1, keepdims=True) + EPSILON)
+    normed = (h32 * scale * gain_ref[...].reshape(1, D)).astype(BF16)
+    slots, owner_token, share = route(id_ref, prob_ref)
+    share_ref[...] = share
+    spread = nn(slots, owner_token).astype(BF16)
+    for k, (first_column, columns) in enumerate(PARTS):
+        piece = normed[:, first_column : first_column + columns]
+        rows_out[k][...] = nn(spread, piece).astype(BF16).reshape(16, 16, columns)
+    routed = []
+    for k in range(len(PARTS)):
+        for dy in range(4):
+            for dz in range(4):
+                n = dy * 4 + dz
+                source = rows_out[k].at[lax.rem(y + dy, 4) * 4 + lax.rem(z + dz, 4)]
+                target = rows_mid[k].at[y * 4 + z]
+                if n == 0:
+                    copy = pltpu.make_async_copy(source, target, local.at[5 + 2 * k])
+                else:
+                    copy = pltpu.make_async_remote_copy(
+                        source, target, d_send.at[k * 16 + n], d_recv.at[k * 16 + n],
+                        device_id=beside(dy, dz), device_id_type=MESH,
+                    )
+                copy.start()
+                routed.append(copy)
+
+    def chunk(n):
+        p, dx = order[n]
+        yy = y if p == 0 else mate
+        return lax.div(yy, 2), lax.rem(x - dx + 4, 4)
+
+    def pass_on(n, zz, way, peer):
+        segment_slot, xx = chunk(n)
+        block = spot(segment_slot, zz, xx, c)
+        sends, recvs = (c_send, c_recv) if way >= 3 else (z_send, z_recv)
+        number = (way - 3 if way >= 3 else way) * 8 + n
+        copy = pltpu.make_async_remote_copy(
+            block, block, sends.at[number], recvs.at[number],
+            device_id=peer, device_id_type=MESH,
+        )
+        copy.start()
+        return copy
+
+    upward, downward, further, across = [], [], [], []
+    for n in range(8):
+        if n == 0:
+            first[n].wait()
+        else:
+            first[n].wait_recv()
+        upward.append(pass_on(n, z, 0, up))
+        downward.append(pass_on(n, z, 1, down))
+        across.append(pass_on(n, z, 3, twin))
+
+    ri = iota((256, 256), 0)
+    ci = iota((256, 256), 1)
+
+    def slot_of(i):
+        return lax.div(lax.rem(i, 32), 2) * 16 + lax.div(i, 32) * 2 + lax.rem(i, 2)
+
+    regroup = (slot_of(ri) == ci).astype(BF16)
+    delivered = [[], [], []]
+    for k, (_, columns) in enumerate(PARTS):
+        for copy in routed[k * 16 : (k + 1) * 16]:
+            copy.wait()
+        moved = nn(regroup, rows_mid[k][...].reshape(256, columns)).astype(BF16)
+        rows_sorted[k][...] = moved.reshape(8, 32, columns)
+        for dx in range(4):
+            for dc in range(2):
+                n = dx * 2 + dc
+                source = rows_sorted[k].at[lax.rem(x + dx, 4) * 2 + lax.rem(c + dc, 2)]
+                target = rows_in[k].at[x * 2 + c]
+                if n == 0:
+                    copy = pltpu.make_async_copy(source, target, local.at[6 + 2 * k])
+                else:
+                    copy = pltpu.make_async_remote_copy(
+                        source, target, e_send.at[k * 8 + n], e_recv.at[k * 8 + n],
+                        device_id=around(dx, dc), device_id_type=MESH,
+                    )
+                copy.start()
+                delivered[k].append(copy)
+
+
+    q_rows[...] = q_ref[...].reshape(ROWS, q_ref.shape[2])
     for dy in range(4):
         for dx in range(4):
             n = dy * 4 + dx
             h = head_of(lax.rem(y + dy, 4), lax.rem(x + dx, 4))
-            q_source = q_ref.at[:, pl.ds(pl.multiple_of(h * HEAD_COLUMNS, HEAD_COLUMNS), HEAD_COLUMNS)]
+            q_source = q_rows.at[:, pl.ds(pl.multiple_of(h * HEAD_COLUMNS, HEAD_COLUMNS), HEAD_COLUMNS)]
             f_source = f_relay.at[h]
             slot = x * 4 + y
             if n == 0:
@@ -247,61 +305,6 @@
                 copy.start()
             small.extend(copies)
 
-    def chunk(n):
-        p, dx = order[n]
-        yy = y if p == 0 else mate
-        return lax.div(yy, 2), lax.rem(x - dx + 4, 4)
-
-    def pass_on(n, zz, way, peer):
-        segment_slot, xx = chunk(n)
-        block = spot(segment_slot, zz, xx, c)
-        sends, recvs = (c_send, c_recv) if way >= 3 else (z_send, z_recv)
-        number = (way - 3 if way >= 3 else way) * 8 + n
-        copy = pltpu.make_async_remote_copy(
-            block, block, sends.at[number], recvs.at[number],
-            device_id=peer, device_id_type=MESH,
-        )
-        copy.start()
-        return copy
-
-    ri = iota((256, 256), 0)
-    ci = iota((256, 256), 1)
-
-    def slot_of(i):
-        return lax.div(lax.rem(i, 32), 2) * 16 + lax.div(i, 32) * 2 + lax.rem(i, 2)
-
-    regroup = (slot_of(ri) == ci).astype(BF16)
-    delivered = [[], [], []]
-    for k, (_, columns) in enumerate(PARTS):
-        for copy in routed[k * 16 : (k + 1) * 16]:
-            copy.wait()
-        moved = nn(regroup, rows_mid[k][...].reshape(256, columns)).astype(BF16)
-        rows_sorted[k][...] = moved.reshape(8, 32, columns)
-        for dx in range(4):
-            for dc in range(2):
-                n = dx * 2 + dc
-                source = rows_sorted[k].at[lax.rem(x + dx, 4) * 2 + lax.rem(c + dc, 2)]
-                target = rows_in[k].at[x * 2 + c]
-                if n == 0:
-                    copy = pltpu.make_async_copy(source, target, local.at[6 + 2 * k])
-                else:
-                    copy = pltpu.make_async_remote_copy(
-                        source, target, e_send.at[k * 8 + n], e_recv.at[k * 8 + n],
-                        device_id=around(dx, dc), device_id_type=MESH,
-                    )
-                copy.start()
-                delivered[k].append(copy)
-
-    upward, downward, further, across = [], [], [], []
-    for n in range(8):
-        if n == 0:
-            first[n].wait()
-        else:
-            first[n].wait_recv()
-        upward.append(pass_on(n, z, 0, up))
-        downward.append(pass_on(n, z, 1, down))
-        across.append(pass_on(n, z, 3, twin))
-
     def forward(n):
         upward[n].wait_recv()
         if n % 2 == 0:
@@ -335,12 +338,12 @@
         tiles(work)
 
     project(0)
-    project(1)
     for n in range(4):
         forward(n)
-    project(2)
+    project(1)
     for n in range(4, 8):
         forward(n)
+    project(2)
 
     @pl.loop(0, 8)
     def _(j):
@@ -356,11 +359,20 @@
         rows = nn(active[...], down_w[:, part]).astype(BF16)
         expert_out[:, :, part] = rows.reshape(128, 2, rows.shape[1])
 
-    tiles(finish)
+    @pl.loop(0, 3)
+    def _(j):
+        finish(pl.ds(pl.multiple_of(j * TILE, TILE), TILE))
 
     for n in range(8):
         further[n].wait_recv()
         across.append(pass_on(n, lax.rem(z + 2, 4), 6, twin))
+
+    @pl.loop(3, D // TILE)
+    def _(j):
+        finish(pl.ds(pl.multiple_of(j * TILE, TILE), TILE))
+
+    finish(pl.ds(D // TILE * TILE, D % TILE))
+
     for copy in across:
         copy.wait()
     for copy in first[1:] + upward + downward + further:
@@ -394,6 +406,7 @@
         scratch_shapes=[
             pltpu.VMEM((KEY_VALUE_HEADS, PAGES, PAGE_TOKENS, 2 * HEAD_WIDTH), BF16),
             pltpu.VMEM((KEY_VALUE_HEADS, ROWS, 2 * HEAD_WIDTH), BF16),
+            pltpu.VMEM((ROWS, QUERY_HEADS * HEAD_WIDTH), BF16),
             pltpu.VMEM((4, 2, 128), jnp.int32),
             *[pltpu.VMEM((16, 16, columns), BF16) for _, columns in PARTS * 2],
             *[pltpu.VMEM((8, 32, columns), BF16) for _, columns in PARTS * 2],
@@ -428,11 +441,26 @@
 
 
 def score_kernel(
-    tables, counts, sinks, q_all, f_all, pool, o_ref, lse_ref,
-    kv, vt, qs, limit_ref, m_ref, acc, sorted_out, s0, s1, places, lengths,
+    table_ref, count_ref, sinks, q_ref, f_ref, pool_ref, o_ref, lse_ref,
+    tables, counts, q_all, f_all, pool,
+    kv, vt, qs, limit_ref, m_ref, acc, sorted_out, s0, s1, places, lengths, sem,
 ):
     y = lax.axis_index("seq")
     outer_pair = jnp.logical_or(y == 0, y == 3)
+    loads = [
+        pltpu.make_async_copy(source, target, sem.at[n])
+        for n, (source, target) in enumerate(
+            [(count_ref, counts), (q_ref, q_all), (f_ref, f_all), (table_ref, tables)]
+        )
+    ]
+    share = pool.shape[0] // 8
+    for n in range(8):
+        part = pl.ds(n * share, share)
+        loads.append(pltpu.make_async_copy(pool_ref.at[part], pool.at[part], sem.at[4 + n]))
+    for copy in loads:
+        copy.start()
+    for copy in loads[:3]:
+        copy.wait()
     sink_row = sinks[0:1, :]
     i0 = iota((128, 128), 0)
     i1 = iota((128, 128), 1)
@@ -555,6 +583,8 @@
 
         return carry
 
+    for copy in loads[3:]:
+        copy.wait()
     lax.fori_loop(0, UNITS, unit, 0)
 
     for e in range(UNITS):
@@ -581,15 +611,21 @@
 
 def score(tables, counts, sinks, q_all, f_all, pool):
     vmem = pl.BlockSpec(memory_space=pltpu.VMEM)
+    anywhere = pl.BlockSpec(memory_space=pl.ANY)
     return pl.pallas_call(
         score_kernel,
         out_shape=(
             jax.ShapeDtypeStruct((UNITS, 128, HEAD_COLUMNS), BF16),
             jax.ShapeDtypeStruct((UNITS, 8, 128), F32),
         ),
-        in_specs=[pl.BlockSpec(memory_space=pltpu.SMEM)] + [vmem] * 5,
+        in_specs=[anywhere, anywhere, vmem, anywhere, anywhere, anywhere],
         out_specs=(vmem, vmem),
         scratch_shapes=[
+            pltpu.SMEM((2, UNITS, 2, 128), jnp.int32),
+            pltpu.VMEM((UNITS, N_SEQ, PROMPTS), jnp.int32),
+            pltpu.VMEM((16, ROWS, HEAD_COLUMNS), BF16),
+            pltpu.VMEM((16, ROWS, 2 * HEAD_WIDTH), BF16),
+            pltpu.VMEM((2 * N_EP * PAGES, PAGE_TOKENS, 2 * HEAD_WIDTH), BF16),
             pltpu.VMEM((KEYS, 128), BF16),
             pltpu.VMEM((KEYS // BK, VROWS, BK), BF16),
             pltpu.VMEM((UNITS * CHUNKS, COLS, 128), BF16),
@@ -601,8 +637,9 @@
             pltpu.VMEM((BK, COLS), F32),
             pltpu.VMEM((UNITS, 128, 1), F32),
             pltpu.SMEM((UNITS * CHUNKS,), jnp.int32),
+            pltpu.SemaphoreType.DMA((12,)),
         ],
-        compiler_params=pltpu.CompilerParams(vmem_limit_bytes=40 << 20),
+        compiler_params=pltpu.CompilerParams(vmem_limit_bytes=60 << 20),
         cost_estimate=pl.CostEstimate(
             flops=25_000_000_000, bytes_accessed=8_000_000, transcendentals=20_000_000
         ),
@@ -712,14 +749,14 @@
     y, z, x, c = place()
 
     q_all, f_all, pool, tables, counts, result, share = exchange(
-        queries.reshape(ROWS, QUERY_HEADS * HEAD_WIDTH),
-        fresh_key_values.reshape(ROWS, 2 * KEY_VALUE_HEADS * HEAD_WIDTH),
+        queries[0],
+        fresh_key_values[0],
         key_value_pages.reshape(PAGES * PAGE_TOKENS, 2 * KEY_VALUE_HEADS * HEAD_WIDTH),
         by_prefix(page_owner),
         by_prefix(page_slot),
         page_count,
-        hidden.reshape(ROWS, D),
-        norm_gain.reshape(1, D),
+        hidden[0],
+        norm_gain,
         expert_ids[0].transpose(1, 2, 0),
         gate_prob[0].transpose(1, 2, 0),
         gate_up,

time: 166 us -> 151 us (0.910)
  the two profiles are of different devices: /device:TPU:0 before, /device:TPU:88 now
where the time goes in v6:
time: 151 us; the launch traced here: 150 us
  Pallas kernels  136 us (90%)
  starting transfers between devices  8.96 us (6%)
  local copies, waits for them, and re-layouts  4.12 us (3%)
    pallas_call x1, Pallas kernels, exchange(): pl.pallas_call(exchange_kernel, out_shape=(jax.ShapeDtypeStruct((16, ROWS...  62.1 us
    pallas_call x1, Pallas kernels, score(): pl.pallas_call(score_kernel, out_shape=(jax.ShapeDtypeStruct((UNITS, 128,...  57.1 us
    pallas_call x1, Pallas kernels, merge(): pl.pallas_call(merge_kernel, out_shape=(jax.ShapeDtypeStruct((ROWS, QUERY...  17.1 us
    all_to_all x1, starting transfers between devices, per_device(): lax.all_to_all(result, ('seq', 'ep'), split_axis=0, concat_axis=0, tiled=...  8.96 us
  transfers between devices with their start and end apart: 1, of which 0 were waited for; matrix products, arithmetic and copies ran while one was open for 1% of the time, Pallas kernels for 38%

profile of v6, /device:TPU:88, one launch (start us, length us, event | category | flops | bytes accessed | tf_op | source)
XLA Modules:
  0.0 150.1 jit_solution(224783694147608678)
XLA Ops:
  0.6 0.0 copy-start.3
  0.6 62.1 %exchange.1 = (bf16[16,32,512]{2,1,0:T(8,128)(2,1)}, bf16[16,32,128]{2,1,0:T(8,128)(2,1)}, bf16[2,768,16,128]{3,2,1,0:T(8,128)(2,1)}, s32[2,4,2,128]{3,2,1,0:T(2...) custom-call(bf16[8,4,4096]{2,1,0:T(4,128)(2,1)} %bitcast.26, ...), custom_call_target="tpu_custom_call" | custom-call | tf_op jit(solution)/shard_map/exchange/pallas_call | solution.py:393
  62.8 9.0 %all-to-all-start = ((bf16[128,2,2880]{2,1,0:T(2,128)(2,1)}), bf16[128,2,2880]{2,1,0:T(2,128)(2,1)S(1)}, u32[]{:S(2)}, u32[]{:S(2)}) async-start(bf16[128,2,2880]{2,1,0:T(2,128)(2,1)} %get-tuple-element.21), calls=%async_computation | async-start | bytes 3014656 | tf_op jit(solution)/shard_map/all_to_all | solution.py:765
  71.8 0.0 copy-done.3
  71.8 0.1 dynamic_slice.3
  71.9 0.1 broadcast_in_dim.10
  71.9 0.1 broadcast_in_dim.11
  72.0 0.6 broadcast_in_dim.12.sinks
  72.6 0.0 copy-start.1
  72.6 57.1 %score.1 = (bf16[4,128,512]{2,1,0:T(8,128)(2,1)}, f32[4,8,128]{2,1,0:T(8,128)}) custom-call(s32[2,4,2,128]{3,2,1,0:T(2,128)} %get-tuple-element.13.table_ref, s32[4,4,8]{2,1,0:T(4,128)} %get-tuple-element.14.count_ref, f32[8,256]{1,0:T(8,128)} %broadcast_in_dim.12.sinks, bf16[16,32,512]{2,1,0:T(8,128)(2,1)} %get-tuple-element.15.q_ref, ...), custom_call_target="tpu_custom_call" | custom-call | flops 24999999488 | bytes 8000000 | tf_op jit(solution)/shard_map/score/pallas_call | solution.py:615
  129.7 0.0 all-to-all-done.rows_ref
  129.7 0.0 copy-done.1
  129.7 0.0 copy-start
  129.8 1.0 copy-done
  130.8 0.0 copy-start.2
  130.8 0.7 copy-done.2
  131.5 17.1 %merge.1 = (bf16[32,4096]{1,0:T(8,128)(2,1)S(1)}, bf16[32,2880]{1,0:T(8,128)(2,1)S(1)}) custom-call(bf16[4,128,512]{2,1,0:T(8,128)(2,1)S(1)} %copy-done, f32[4,8,128]{2,1,0:T(8,128)S(1)} %copy-done.2, f32[32,256]{1,0:T(8,128)S(1)} %copy-done.1, bf16[128,2,2880]{2,1,0:T(2,128)(2,1)S(1)} %all-to-all-done.rows_ref), custom_call_target="tpu_custom_call" | custom-call | tf_op jit(solution)/shard_map/merge/pallas_call | solution.py:721
  148.6 0.8 reshape.27
  149.4 0.7 reshape.28
Async XLA Ops:
  0.6 71.1 %copy-start.3 = (f32[64]{0:T(128)S(1)}, f32[64]{0:T(128)}, u32[]{:S(2)}) copy-start(f32[64]{0:T(128)} %param.19) | copy-start | bytes 772
  62.8 66.9 %all-to-all-start = ((bf16[128,2,2880]{2,1,0:T(2,128)(2,1)}), bf16[128,2,2880]{2,1,0:T(2,128)(2,1)S(1)}, u32[]{:S(2)}, u32[]{:S(2)}) async-start(bf16[128,2,2880]{2,1,0:T(2,128)(2,1)} %get-tuple-element.21), calls=%async_computation | async-start | bytes 3014656 | tf_op jit(solution)/shard_map/all_to_all | solution.py:765
  72.6 57.1 %copy-start.1 = (f32[32,256]{1,0:T(8,128)S(1)}, f32[32,256]{1,0:T(8,128)}, u32[]{:S(2)}) copy-start(f32[32,256]{1,0:T(8,128)} %get-tuple-element.20.share_ref) | copy-start | bytes 98308
  129.7 1.0 copy-start
  130.8 0.7 copy-start.2

commit v7 on v6

--- a/solution.py
+++ b/solution.py
@@ -96,7 +96,7 @@
     q_ref, f_ref, page_ref, owner_ref, slot_ref, count_ref, hidden_ref, gain_ref, id_ref, prob_ref,
     up_ref, down_ref,
     q_all, f_all, pool, tables, counts, expert_out, share_ref,
-    relay, f_relay, q_rows, table_ref, out0, out1, out2, mid0, mid1, mid2, sorted0, sorted1, sorted2,
+    relay, f_relay, q_rows, table_ref, count_rows, out0, out1, out2, mid0, mid1, mid2, sorted0, sorted1, sorted2,
     in0, in1, in2, up_w, down_w, projected, active,
     q_send, q_recv, f_send, f_recv, a_send, a_recv, z_send, z_recv, c_send, c_recv,
     i_send, i_recv, d_send, d_recv, e_send, e_recv, local, w_sem,
@@ -150,7 +150,18 @@
         )
     for xx in range(4):
         e = z * 8 + xx * 2 + c
-        table_ref[xx] = owner_ref[e] * PAGES + slot_ref[e]
+        pages = owner_ref[e] * PAGES + slot_ref[e]
+        for half in range(2):
+            lanes = slice(half * 64, half * 64 + 64)
+            table_ref[xx, half : half + 1, :] = jnp.concatenate(
+                [pages[0:1, lanes], pages[1:2, lanes]], axis=1
+            )
+    lane = iota((PROMPTS, 128), 1)
+    copies = (iota((PROMPTS, 128), 0) == lax.div(lax.rem(lane, ROWS), SCORED_STEPS)).astype(F32)
+    wide = nn(count_ref[...].astype(F32), copies, HIGHEST)
+    mine = lax.div(iota((N_SEQ, 128), 1), ROWS) == iota((N_SEQ, 128), 0)
+    wide = jnp.sum(jnp.where(mine, wide, 0.0), axis=0, keepdims=True)
+    count_rows[...] = jnp.broadcast_to(wide, (8, 128))
 
     pl.semaphore_wait(barrier, len(peers))
 
@@ -178,7 +189,7 @@
     mine = pltpu.make_async_copy(table_ref, tables.at[lax.div(y, 2)], local.at[1])
     mine.start()
     small.append(mine)
-    mine = pltpu.make_async_copy(count_ref, counts.at[x], local.at[2])
+    mine = pltpu.make_async_copy(count_rows, counts.at[x], local.at[2])
     mine.start()
     small.append(mine)
     other = pltpu.make_async_remote_copy(
@@ -189,7 +200,7 @@
     small.append(other)
     for dx in range(1, 4):
         other = pltpu.make_async_remote_copy(
-            count_ref, counts.at[x], i_send.at[dx], i_recv.at[dx],
+            count_rows, counts.at[x], i_send.at[dx], i_recv.at[dx],
             device_id=at(0, dx), device_id_type=MESH,
         )
         other.start()
@@ -239,7 +250,8 @@
         return copy
 
     upward, downward, further, across = [], [], [], []
-    for n in range(8):
+
+    def begin(n):
         if n == 0:
             first[n].wait()
         else:
@@ -247,6 +259,19 @@
         upward.append(pass_on(n, z, 0, up))
         downward.append(pass_on(n, z, 1, down))
         across.append(pass_on(n, z, 3, twin))
+
+    def forward(n):
+        upward[n].wait_recv()
+        if n % 2 == 0:
+            further.append(pass_on(n, lax.rem(z + 3, 4), 2, up))
+        across.append(pass_on(n, lax.rem(z + 3, 4), 4, twin))
+        downward[n].wait_recv()
+        if n % 2 == 1:
+            further.append(pass_on(n, lax.rem(z + 1, 4), 2, down))
+        across.append(pass_on(n, lax.rem(z + 1, 4), 5, twin))
+
+    begin(0)
+    begin(1)
 
     ri = iota((256, 256), 0)
     ci = iota((256, 256), 1)
@@ -275,6 +300,11 @@
                     )
                 copy.start()
                 delivered[k].append(copy)
+        begin(2 + 2 * k)
+        begin(3 + 2 * k)
+        if k > 0:
+            forward(2 * k - 2)
+            forward(2 * k - 1)
 
 
     q_rows[...] = q_ref[...].reshape(ROWS, q_ref.shape[2])
@@ -305,16 +335,6 @@
                 copy.start()
             small.extend(copies)
 
-    def forward(n):
-        upward[n].wait_recv()
-        if n % 2 == 0:
-            further.append(pass_on(n, lax.rem(z + 3, 4), 2, up))
-        across.append(pass_on(n, lax.rem(z + 3, 4), 4, twin))
-        downward[n].wait_recv()
-        if n % 2 == 1:
-            further.append(pass_on(n, lax.rem(z + 1, 4), 2, down))
-        across.append(pass_on(n, lax.rem(z + 1, 4), 5, twin))
-
     for copy in weights:
         copy.wait()
 
@@ -338,11 +358,11 @@
         tiles(work)
 
     project(0)
-    for n in range(4):
-        forward(n)
+    forward(4)
+    forward(5)
     project(1)
-    for n in range(4, 8):
-        forward(n)
+    forward(6)
+    forward(7)
     project(2)
 
     @pl.loop(0, 8)
@@ -397,7 +417,7 @@
             jax.ShapeDtypeStruct((16, ROWS, 2 * HEAD_WIDTH), BF16),
             jax.ShapeDtypeStruct((2, N_EP * PAGES, PAGE_TOKENS, 2 * HEAD_WIDTH), BF16),
             jax.ShapeDtypeStruct((2, 4, 2, 128), jnp.int32),
-            jax.ShapeDtypeStruct((4, N_SEQ, PROMPTS), jnp.int32),
+            jax.ShapeDtypeStruct((4, 8, 128), F32),
             jax.ShapeDtypeStruct((128, 2, D), BF16),
             jax.ShapeDtypeStruct((ROWS, 256), F32),
         ),
@@ -408,6 +428,7 @@
             pltpu.VMEM((KEY_VALUE_HEADS, ROWS, 2 * HEAD_WIDTH), BF16),
             pltpu.VMEM((ROWS, QUERY_HEADS * HEAD_WIDTH), BF16),
             pltpu.VMEM((4, 2, 128), jnp.int32),
+            pltpu.VMEM((8, 128), F32),
             *[pltpu.VMEM((16, 16, columns), BF16) for _, columns in PARTS * 2],
             *[pltpu.VMEM((8, 32, columns), BF16) for _, columns in PARTS * 2],
             pltpu.VMEM((D, 2 * HID), BF16),
@@ -467,11 +488,7 @@
     lane_row = lax.rem(iota((128, COLS), 1), ROWS).astype(F32)
 
     def ordering(e):
-        lane = iota((PROMPTS, 128), 1)
-        copies = (iota((PROMPTS, 128), 0) == lax.div(lax.rem(lane, ROWS), SCORED_STEPS)).astype(F32)
-        wide = nn(counts[e].astype(F32), copies, HIGHEST)
-        mine = lax.div(iota((N_SEQ, 128), 1), ROWS) == iota((N_SEQ, 128), 0)
-        c = jnp.sum(jnp.where(mine, wide, 0.0), axis=0, keepdims=True)
+        c = counts[e][0:1, :]
         n_row = jnp.where(
             outer_pair,
             jnp.minimum(c, 256.0) + jnp.maximum(c - 768.0, 0.0),
@@ -520,11 +537,10 @@
 
     def unit(e, carry):
         def gather(kb, carry):
-            p0 = kb * (GK // PAGE_TOKENS)
-            ss = lax.div(p0, NPS)
-            lane = lax.div(lax.rem(p0, NPS), 2)
+            ss = lax.div(kb, 2)
+            half = lax.rem(kb, 2)
             rows = [
-                pool[tables[ss, e, i % 2, lane + i // 2] + ss * (N_EP * PAGES)]
+                pool[tables[ss, e, half, i % 2 * 64 + i // 2] + ss * (N_EP * PAGES)]
                 for i in range(GK // PAGE_TOKENS)
             ]
             for i in range(GK // BK):
@@ -622,7 +638,7 @@
         out_specs=(vmem, vmem),
         scratch_shapes=[
             pltpu.SMEM((2, UNITS, 2, 128), jnp.int32),
-            pltpu.VMEM((UNITS, N_SEQ, PROMPTS), jnp.int32),
+            pltpu.VMEM((UNITS, 8, 128), F32),
             pltpu.VMEM((16, ROWS, HEAD_COLUMNS), BF16),
             pltpu.VMEM((16, ROWS, 2 * HEAD_WIDTH), BF16),
             pltpu.VMEM((2 * N_EP * PAGES, PAGE_TOKENS, 2 * HEAD_WIDTH), BF16),
@@ -648,13 +664,15 @@
 
 
 def merge_kernel(
-    o_ref, lse_ref, share_ref, rows_ref, out_ref, mix_ref, o_all, lse_all, o_send, o_recv, l_send, l_recv, local,
+    o_ref, lse_ref, share_ref, rows_ref, out_ref, mix_ref, rows_here, o_all, lse_all, o_send, o_recv, l_send, l_recv, local,
 ):
     y, z, x, c = place()
 
     def at(dy, dx):
         return device(lax.rem(y + dy, 4), z, lax.rem(x + dx, 4), c)
 
+    load = pltpu.make_async_copy(rows_ref, rows_here, local.at[2])
+    load.start()
     plane = [(dy, dx) for dy in range(4) for dx in range(4) if (dy, dx) != (0, 0)]
     barrier = pltpu.get_barrier_semaphore()
     for dy, dx in plane:
@@ -692,7 +710,8 @@
     share = share_ref[...]
     high = share.astype(BF16)
     low = (share - high.astype(F32)).astype(BF16)
-    rows = rows_ref[...].reshape(256, D)
+    load.wait()
+    rows = rows_here[...].reshape(256, D)
     mix_ref[...] = (nn(high, rows) + nn(low, rows)).astype(BF16)
 
     for copy in copies:
@@ -717,6 +736,7 @@
 
 def merge(o, lse, share, rows):
     vmem = pl.BlockSpec(memory_space=pltpu.VMEM)
+    anywhere = pl.BlockSpec(memory_space=pl.ANY)
     dma = pltpu.SemaphoreType.DMA
     return pl.pallas_call(
         merge_kernel,
@@ -724,15 +744,16 @@
             jax.ShapeDtypeStruct((ROWS, QUERY_HEADS * HEAD_WIDTH), BF16),
             jax.ShapeDtypeStruct((ROWS, D), BF16),
         ),
-        in_specs=[vmem] * 4,
+        in_specs=[anywhere, anywhere, vmem, anywhere],
         out_specs=(vmem, vmem),
         scratch_shapes=[
+            pltpu.VMEM((128, 2, D), BF16),
             pltpu.VMEM((16, ROWS, HEAD_COLUMNS), BF16),
             pltpu.VMEM((16, 8, 128), F32),
-            dma((16,)), dma((16,)), dma((16,)), dma((16,)), dma((2,)),
+            dma((16,)), dma((16,)), dma((16,)), dma((16,)), dma((3,)),
         ],
         compiler_params=pltpu.CompilerParams(
-            collective_id=2, has_side_effects=True, vmem_limit_bytes=16 << 20
+            collective_id=2, has_side_effects=True, vmem_limit_bytes=60 << 20
         ),
         name="merge",
     )(o, lse, share, rows)

time: 151 us -> 151 us (level)
  the two profiles are of different devices: /device:TPU:88 before, /device:TPU:104 now
where the time goes in v7:
time: 151 us; the launch traced here: 150 us
  Pallas kernels  135 us (89%)
  starting transfers between devices  9.18 us (6%)
  local copies, waits for them, and re-layouts  5.39 us (4%)
    pallas_call x1, Pallas kernels, exchange(): pl.pallas_call(exchange_kernel, out_shape=(jax.ShapeDtypeStruct((16, ROWS...  61.9 us
    pallas_call x1, Pallas kernels, score(): pl.pallas_call(score_kernel, out_shape=(jax.ShapeDtypeStruct((UNITS, 128,...  54.8 us
    pallas_call x1, Pallas kernels, merge(): pl.pallas_call(merge_kernel, out_shape=(jax.ShapeDtypeStruct((ROWS, QUERY...  18.4 us
    all_to_all x1, starting transfers between devices, per_device(): lax.all_to_all(result, ('seq', 'ep'), split_axis=0, concat_axis=0, tiled=...  9.18 us
    reshape x2, local copies, waits for them, and re-layouts, per_device(): return (attention.reshape(queries.shape), mixture.reshape(hidden.shape))  3.41 us
  transfers between devices with their start and end apart: 1, of which 0 were waited for; matrix products, arithmetic and copies ran while one was open for 1% of the time, Pallas kernels for 36%

profile of v7, /device:TPU:104, one launch (start us, length us, event | category | flops | bytes accessed | tf_op | source)
XLA Modules:
  0.0 150.3 jit_solution(4918874949790323082)
XLA Ops:
  0.6 0.0 copy-start.1
  0.6 61.9 %exchange.1 = (bf16[16,32,512]{2,1,0:T(8,128)(2,1)}, bf16[16,32,128]{2,1,0:T(8,128)(2,1)}, bf16[2,768,16,128]{3,2,1,0:T(8,128)(2,1)}, s32[2,4,2,128]{3,2,1,0:T(2...) custom-call(bf16[8,4,4096]{2,1,0:T(4,128)(2,1)} %bitcast.26, ...), custom_call_target="tpu_custom_call" | custom-call | tf_op jit(solution)/shard_map/exchange/pallas_call | solution.py:413
  62.5 9.2 %all-to-all-start = ((bf16[128,2,2880]{2,1,0:T(2,128)(2,1)}), bf16[128,2,2880]{2,1,0:T(2,128)(2,1)S(1)}, u32[]{:S(2)}, u32[]{:S(2)}) async-start(bf16[128,2,2880]{2,1,0:T(2,128)(2,1)} %get-tuple-element.21), calls=%async_computation | async-start | bytes 3014656 | tf_op jit(solution)/shard_map/all_to_all | solution.py:786
  71.7 0.0 copy-done.1
  71.7 0.1 dynamic_slice.3
  71.8 0.1 broadcast_in_dim.10
  71.9 0.1 broadcast_in_dim.11
  72.0 0.6 broadcast_in_dim.12.sinks
  72.6 54.8 %score.1 = (bf16[4,128,512]{2,1,0:T(8,128)(2,1)}, f32[4,8,128]{2,1,0:T(8,128)}) custom-call(s32[2,4,2,128]{3,2,1,0:T(2,128)} %get-tuple-element.13.table_ref, f32[4,8,128]{2,1,0:T(8,128)} %get-tuple-element.14.count_ref, f32[8,256]{1,0:T(8,128)} %broadcast_in_dim.12.sinks, bf16[16,32,512]{2,1,0:T(8,128)(2,1)} %get-tuple-element.15.q_ref, ...), custom_call_target="tpu_custom_call" | custom-call | flops 24999999488 | bytes 8000000 | tf_op jit(solution)/shard_map/score/pallas_call | solution.py:631
  127.3 0.0 all-to-all-done.rows_ref
  127.3 0.0 copy-start
  127.3 1.1 copy-done
  128.5 18.4 %merge.1 = (bf16[32,4096]{1,0:T(8,128)(2,1)}, bf16[32,2880]{1,0:T(8,128)(2,1)}) custom-call(bf16[4,128,512]{2,1,0:T(8,128)(2,1)} %get-tuple-element.18.o_ref, f32[4,8,128]{2,1,0:T(8,128)} %get-tuple-element.19.lse_ref, f32[32,256]{1,0:T(8,128)} %get-tuple-element.20.share_ref, bf16[128,2,2880]{2,1,0:T(2,128)(2,1)} %copy-done), custom_call_target="tpu_custom_call" | custom-call | tf_op jit(solution)/shard_map/merge/pallas_call | solution.py:741
  146.9 1.8 %reshape.27 = bf16[1,8,4,4096]{3,2,1,0:T(4,128)(2,1)} reshape(bf16[32,4096]{1,0:T(8,128)(2,1)} %get-tuple-element.22) | data formatting | bytes 524288 | tf_op jit(solution)/shard_map/reshape | solution.py:794
  148.7 1.6 %reshape.28 = bf16[1,8,4,2880]{3,2,1,0:T(4,128)(2,1)} reshape(bf16[32,2880]{1,0:T(8,128)(2,1)} %get-tuple-element.23) | data formatting | bytes 368640 | tf_op jit(solution)/shard_map/reshape | solution.py:794
Async XLA Ops:
  0.6 71.1 %copy-start.1 = (f32[64]{0:T(128)S(1)}, f32[64]{0:T(128)}, u32[]{:S(2)}) copy-start(f32[64]{0:T(128)} %param.19) | copy-start | bytes 772
  62.5 64.8 %all-to-all-start = ((bf16[128,2,2880]{2,1,0:T(2,128)(2,1)}), bf16[128,2,2880]{2,1,0:T(2,128)(2,1)S(1)}, u32[]{:S(2)}, u32[]{:S(2)}) async-start(bf16[128,2,2880]{2,1,0:T(2,128)(2,1)} %get-tuple-element.21), calls=%async_computation | async-start | bytes 3014656 | tf_op jit(solution)/shard_map/all_to_all | solution.py:786
  127.3 1.2 copy-start

commit v8 on v7

--- a/solution.py
+++ b/solution.py
@@ -163,14 +163,25 @@
     wide = jnp.sum(jnp.where(mine, wide, 0.0), axis=0, keepdims=True)
     count_rows[...] = jnp.broadcast_to(wide, (8, 128))
 
+    h32 = hidden_ref[...].reshape(ROWS, D).astype(F32)
+    scale = lax.rsqrt(jnp.mean(h32 * h32, axis=-1, keepdims=True) + EPSILON)
+    normed = (h32 * scale * gain_ref[...].reshape(1, D)).astype(BF16)
+    slots, owner_token, share = route(id_ref, prob_ref)
+    share_ref[...] = share
+    spread = nn(slots, owner_token).astype(BF16)
+    for k, (first_column, columns) in enumerate(PARTS):
+        piece = normed[:, first_column : first_column + columns]
+        rows_out[k][...] = nn(spread, piece).astype(BF16).reshape(16, 16, columns)
     pl.semaphore_wait(barrier, len(peers))
 
     def spot(segment_slot, zz, xx, cc):
         return pool.at[segment_slot, pl.ds((zz * 8 + xx * 2 + cc) * PAGES, PAGES)]
 
-    order = [(0, 0), (0, 1), (0, 3), (1, 0), (1, 1), (1, 3), (0, 2), (1, 2)]
+    order = [(0, 0), (0, 1), (0, 3), (0, 2), (1, 0), (1, 1), (1, 3), (1, 2)]
     first = []
-    for n, (p, dx) in enumerate(order):
+
+    def hand_out(n):
+        p, dx = order[n]
         yy = y if p == 0 else mate
         xx = lax.rem(x + dx, 4)
         target = spot(lax.div(y, 2), z, x, c)
@@ -184,6 +195,28 @@
             )
         copy.start()
         first.append(copy)
+
+    for n in range(4):
+        hand_out(n)
+    routed = []
+    for k in range(len(PARTS)):
+        for dy in range(4):
+            for dz in range(4):
+                n = dy * 4 + dz
+                source = rows_out[k].at[lax.rem(y + dy, 4) * 4 + lax.rem(z + dz, 4)]
+                target = rows_mid[k].at[y * 4 + z]
+                if n == 0:
+                    copy = pltpu.make_async_copy(source, target, local.at[5 + 2 * k])
+                else:
+                    copy = pltpu.make_async_remote_copy(
+                        source, target, d_send.at[k * 16 + n], d_recv.at[k * 16 + n],
+                        device_id=beside(dy, dz), device_id_type=MESH,
+                    )
+                copy.start()
+                routed.append(copy)
+
+    for n in range(4, 8):
+        hand_out(n)
 
     small = []
     mine = pltpu.make_async_copy(table_ref, tables.at[lax.div(y, 2)], local.at[1])
@@ -206,32 +239,6 @@
         other.start()
         small.append(other)
 
-    h32 = hidden_ref[...].reshape(ROWS, D).astype(F32)
-    scale = lax.rsqrt(jnp.mean(h32 * h32, axis=-1, keepdims=True) + EPSILON)
-    normed = (h32 * scale * gain_ref[...].reshape(1, D)).astype(BF16)
-    slots, owner_token, share = route(id_ref, prob_ref)
-    share_ref[...] = share
-    spread = nn(slots, owner_token).astype(BF16)
-    for k, (first_column, columns) in enumerate(PARTS):
-        piece = normed[:, first_column : first_column + columns]
-        rows_out[k][...] = nn(spread, piece).astype(BF16).reshape(16, 16, columns)
-    routed = []
-    for k in range(len(PARTS)):
-        for dy in range(4):
-            for dz in range(4):
-                n = dy * 4 + dz
-                source = rows_out[k].at[lax.rem(y + dy, 4) * 4 + lax.rem(z + dz, 4)]
-                target = rows_mid[k].at[y * 4 + z]
-                if n == 0:
-                    copy = pltpu.make_async_copy(source, target, local.at[5 + 2 * k])
-                else:
-                    copy = pltpu.make_async_remote_copy(
-                        source, target, d_send.at[k * 16 + n], d_recv.at[k * 16 + n],
-                        device_id=beside(dy, dz), device_id_type=MESH,
-                    )
-                copy.start()
-                routed.append(copy)
-
     def chunk(n):
         p, dx = order[n]
         yy = y if p == 0 else mate
@@ -270,20 +277,24 @@
             further.append(pass_on(n, lax.rem(z + 1, 4), 2, down))
         across.append(pass_on(n, lax.rem(z + 1, 4), 5, twin))
 
-    begin(0)
-    begin(1)
+    for n in range(4):
+        begin(n)
 
     ri = iota((256, 256), 0)
     ci = iota((256, 256), 1)
 
     def slot_of(i):
         return lax.div(lax.rem(i, 32), 2) * 16 + lax.div(i, 32) * 2 + lax.rem(i, 2)
+
+    def arrive(copies):
+        copies[0].wait()
+        for copy in copies[1:]:
+            copy.wait_recv()
 
     regroup = (slot_of(ri) == ci).astype(BF16)
     delivered = [[], [], []]
     for k, (_, columns) in enumerate(PARTS):
-        for copy in routed[k * 16 : (k + 1) * 16]:
-            copy.wait()
+        arrive(routed[k * 16 : (k + 1) * 16])
         moved = nn(regroup, rows_mid[k][...].reshape(256, columns)).astype(BF16)
         rows_sorted[k][...] = moved.reshape(8, 32, columns)
         for dx in range(4):
@@ -300,12 +311,13 @@
                     )
                 copy.start()
                 delivered[k].append(copy)
-        begin(2 + 2 * k)
-        begin(3 + 2 * k)
-        if k > 0:
-            forward(2 * k - 2)
-            forward(2 * k - 1)
-
+        if k == 1:
+            for n in (0, 1):
+                forward(n)
+    for n in range(4, 8):
+        begin(n)
+    for n in (2, 3):
+        forward(n)
 
     q_rows[...] = q_ref[...].reshape(ROWS, q_ref.shape[2])
     for dy in range(4):
@@ -347,8 +359,7 @@
 
     def project(k):
         first_column, columns = PARTS[k]
-        for copy in delivered[k]:
-            copy.wait()
+        arrive(delivered[k])
 
         def work(part):
             rows = rows_in[k][...].reshape(256, columns)
@@ -358,12 +369,12 @@
         tiles(work)
 
     project(0)
+    project(1)
     forward(4)
     forward(5)
-    project(1)
+    project(2)
     forward(6)
     forward(7)
-    project(2)
 
     @pl.loop(0, 8)
     def _(j):
@@ -396,6 +407,11 @@
     for copy in across:
         copy.wait()
     for copy in first[1:] + upward + downward + further:
+        copy.wait_send()
+    for n, copy in enumerate(routed):
+        if n % 16 > 0:
+            copy.wait_send()
+    for copy in sum([copies[1:] for copies in delivered], []):
         copy.wait_send()
     for copy in small:
         copy.wait()
@@ -664,15 +680,13 @@
 
 
 def merge_kernel(
-    o_ref, lse_ref, share_ref, rows_ref, out_ref, mix_ref, rows_here, o_all, lse_all, o_send, o_recv, l_send, l_recv, local,
+    o_ref, lse_ref, share_ref, rows_ref, out_ref, mix_ref, o_all, lse_all, o_send, o_recv, l_send, l_recv, local,
 ):
     y, z, x, c = place()
 
     def at(dy, dx):
         return device(lax.rem(y + dy, 4), z, lax.rem(x + dx, 4), c)
 
-    load = pltpu.make_async_copy(rows_ref, rows_here, local.at[2])
-    load.start()
     plane = [(dy, dx) for dy in range(4) for dx in range(4) if (dy, dx) != (0, 0)]
     barrier = pltpu.get_barrier_semaphore()
     for dy, dx in plane:
@@ -710,8 +724,7 @@
     share = share_ref[...]
     high = share.astype(BF16)
     low = (share - high.astype(F32)).astype(BF16)
-    load.wait()
-    rows = rows_here[...].reshape(256, D)
+    rows = rows_ref[...].reshape(256, D)
     mix_ref[...] = (nn(high, rows) + nn(low, rows)).astype(BF16)
 
     for copy in copies:
@@ -744,16 +757,15 @@
             jax.ShapeDtypeStruct((ROWS, QUERY_HEADS * HEAD_WIDTH), BF16),
             jax.ShapeDtypeStruct((ROWS, D), BF16),
         ),
-        in_specs=[anywhere, anywhere, vmem, anywhere],
+        in_specs=[anywhere, anywhere, vmem, vmem],
         out_specs=(vmem, vmem),
         scratch_shapes=[
-            pltpu.VMEM((128, 2, D), BF16),
             pltpu.VMEM((16, ROWS, HEAD_COLUMNS), BF16),
             pltpu.VMEM((16, 8, 128), F32),
-            dma((16,)), dma((16,)), dma((16,)), dma((16,)), dma((3,)),
+            dma((16,)), dma((16,)), dma((16,)), dma((16,)), dma((2,)),
         ],
         compiler_params=pltpu.CompilerParams(
-            collective_id=2, has_side_effects=True, vmem_limit_bytes=60 << 20
+            collective_id=2, has_side_effects=True, vmem_limit_bytes=16 << 20
         ),
         name="merge",
     )(o, lse, share, rows)

time: 151 us -> 145 us (0.960)
  the two profiles are of different devices: /device:TPU:104 before, /device:TPU:0 now
where the time goes in v8:
time: 145 us; the launch traced here: 143 us
  Pallas kernels  131 us (90%)
  starting transfers between devices  7.58 us (5%)
  local copies, waits for them, and re-layouts  4.12 us (3%)
    pallas_call x1, Pallas kernels, exchange(): pl.pallas_call(exchange_kernel, out_shape=(jax.ShapeDtypeStruct((16, ROWS...  62 us
    pallas_call x1, Pallas kernels, score(): pl.pallas_call(score_kernel, out_shape=(jax.ShapeDtypeStruct((UNITS, 128,...  51.7 us
    pallas_call x1, Pallas kernels, merge(): pl.pallas_call(merge_kernel, out_shape=(jax.ShapeDtypeStruct((ROWS, QUERY...  17.3 us
    all_to_all x1, starting transfers between devices, per_device(): lax.all_to_all(result, ('seq', 'ep'), split_axis=0, concat_axis=0, tiled=...  7.58 us
  transfers between devices with their start and end apart: 1, of which 0 were waited for; matrix products, arithmetic and copies ran while one was open for 1% of the time, Pallas kernels for 36%

profile of v8, /device:TPU:0, one launch (start us, length us, event | category | flops | bytes accessed | tf_op | source)
XLA Modules:
  0.0 143.4 jit_solution(4339640749924256221)
XLA Ops:
  0.6 0.0 copy-start.3
  0.6 62.0 %exchange.1 = (bf16[16,32,512]{2,1,0:T(8,128)(2,1)}, bf16[16,32,128]{2,1,0:T(8,128)(2,1)}, bf16[2,768,16,128]{3,2,1,0:T(8,128)(2,1)}, s32[2,4,2,128]{3,2,1,0:T(2...) custom-call(bf16[8,4,4096]{2,1,0:T(4,128)(2,1)} %bitcast.26, ...), custom_call_target="tpu_custom_call" | custom-call | tf_op jit(solution)/shard_map/exchange/pallas_call | solution.py:429
  62.6 7.6 %all-to-all-start = ((bf16[128,2,2880]{2,1,0:T(2,128)(2,1)}), bf16[128,2,2880]{2,1,0:T(2,128)(2,1)S(1)}, u32[]{:S(2)}, u32[]{:S(2)}) async-start(bf16[128,2,2880]{2,1,0:T(2,128)(2,1)} %get-tuple-element.21), calls=%async_computation | async-start | bytes 3014656 | tf_op jit(solution)/shard_map/all_to_all | solution.py:798
  70.2 0.0 copy-done.3
  70.2 0.1 dynamic_slice.3
  70.3 0.1 broadcast_in_dim.10
  70.4 0.1 broadcast_in_dim.11
  70.5 0.6 broadcast_in_dim.12.sinks
  71.1 0.0 copy-start.1
  71.1 51.7 %score.1 = (bf16[4,128,512]{2,1,0:T(8,128)(2,1)}, f32[4,8,128]{2,1,0:T(8,128)}) custom-call(s32[2,4,2,128]{3,2,1,0:T(2,128)} %get-tuple-element.13.table_ref, f32[4,8,128]{2,1,0:T(8,128)} %get-tuple-element.14.count_ref, f32[8,256]{1,0:T(8,128)} %broadcast_in_dim.12.sinks, bf16[16,32,512]{2,1,0:T(8,128)(2,1)} %get-tuple-element.15.q_ref, ...), custom_call_target="tpu_custom_call" | custom-call | flops 24999999488 | bytes 8000000 | tf_op jit(solution)/shard_map/score/pallas_call | solution.py:647
  122.7 0.0 all-to-all-done.rows_ref
  122.8 0.0 copy-done.1
  122.8 0.0 copy-start
  122.8 1.0 copy-done
  123.8 0.0 copy-start.2
  123.8 0.7 copy-done.2
  124.5 17.3 %merge.1 = (bf16[32,4096]{1,0:T(8,128)(2,1)S(1)}, bf16[32,2880]{1,0:T(8,128)(2,1)S(1)}) custom-call(bf16[4,128,512]{2,1,0:T(8,128)(2,1)S(1)} %copy-done, f32[4,8,128]{2,1,0:T(8,128)S(1)} %copy-done.2, f32[32,256]{1,0:T(8,128)S(1)} %copy-done.1, bf16[128,2,2880]{2,1,0:T(2,128)(2,1)S(1)} %all-to-all-done.rows_ref), custom_call_target="tpu_custom_call" | custom-call | tf_op jit(solution)/shard_map/merge/pallas_call | solution.py:754
  141.8 0.8 reshape.27
  142.6 0.7 reshape.28
Async XLA Ops:
  0.6 69.6 %copy-start.3 = (f32[64]{0:T(128)S(1)}, f32[64]{0:T(128)}, u32[]{:S(2)}) copy-start(f32[64]{0:T(128)} %param.19) | copy-start | bytes 772
  62.6 60.1 %all-to-all-start = ((bf16[128,2,2880]{2,1,0:T(2,128)(2,1)}), bf16[128,2,2880]{2,1,0:T(2,128)(2,1)S(1)}, u32[]{:S(2)}, u32[]{:S(2)}) async-start(bf16[128,2,2880]{2,1,0:T(2,128)(2,1)} %get-tuple-element.21), calls=%async_computation | async-start | bytes 3014656 | tf_op jit(solution)/shard_map/all_to_all | solution.py:798
  71.1 51.7 %copy-start.1 = (f32[32,256]{1,0:T(8,128)S(1)}, f32[32,256]{1,0:T(8,128)}, u32[]{:S(2)}) copy-start(f32[32,256]{1,0:T(8,128)} %get-tuple-element.20.share_ref) | copy-start | bytes 98308
  122.8 1.0 copy-start
  123.8 0.7 copy-start.2

commit v9 on v8

--- a/solution.py
+++ b/solution.py
@@ -463,7 +463,7 @@
 
 
 BK = 1024
-GK = 2048
+GK = 4096
 KEYS = 2 * NPS * PAGE_TOKENS
 UNITS = 4
 CHUNKS = 4
@@ -522,20 +522,22 @@
         pos_row = jnp.sum(jnp.where(ahead, 1.0, 0.0), axis=0, keepdims=True)
         perm = (pos_row == i0.astype(F32)).astype(BF16)
         q_sorted = nn(perm, q_all[e * 4 : e * 4 + 4].reshape(128, HEAD_COLUMNS)) * 0.125
-        q_sorted = q_sorted.astype(BF16)
         f_sorted = nn(perm, f_all[e * 4 : e * 4 + 4].reshape(128, 128)).astype(BF16)
-        none = jnp.zeros((ROWS, HEAD_WIDTH), BF16)
+        none = jnp.zeros((COLS, HEAD_WIDTH), F32)
         for ch in range(CHUNKS):
             u = e * CHUNKS + ch
-            for g in range(GROUP):
-                piece = q_sorted[ch * ROWS : (ch + 1) * ROWS, g * HEAD_WIDTH : (g + 1) * HEAD_WIDTH]
-                qs[u, g * ROWS : (g + 1) * ROWS, :] = jnp.concatenate([piece, none], axis=1)
+            pieces = [
+                q_sorted[ch * ROWS : (ch + 1) * ROWS, g * HEAD_WIDTH : (g + 1) * HEAD_WIDTH]
+                for g in range(GROUP)
+            ]
+            stacked = jnp.concatenate([jnp.concatenate(pieces, axis=0), none], axis=1)
+            qs[u] = stacked.T.astype(BF16)
             member = pos_col == lane_row + float(ch * ROWS)
             limit = jnp.sum(jnp.where(member, n_col, 0.0), axis=0, keepdims=True) * PAGE_TOKENS
             limit_ref[u] = jnp.broadcast_to(limit, (8, COLS))
             lengths[u] = jnp.max(limit).astype(jnp.int32)
             rows = f_sorted[ch * ROWS : (ch + 1) * ROWS, :]
-            s = nt(rows, qs[u])
+            s = nn(rows, qs[u])
             ki = iota((ROWS, COLS), 0)
             ri = lax.rem(iota((ROWS, COLS), 1), ROWS)
             seen = jnp.logical_and(
@@ -553,10 +555,8 @@
 
     def unit(e, carry):
         def gather(kb, carry):
-            ss = lax.div(kb, 2)
-            half = lax.rem(kb, 2)
             rows = [
-                pool[tables[ss, e, half, i % 2 * 64 + i // 2] + ss * (N_EP * PAGES)]
+                pool[tables[kb, e, i // 128, i % 2 * 64 + i % 128 // 2] + kb * (N_EP * PAGES)]
                 for i in range(GK // PAGE_TOKENS)
             ]
             for i in range(GK // BK):
@@ -572,7 +572,7 @@
 
         def produce(store, u, kb):
             keys = kv[pl.ds(pl.multiple_of(kb * BK, BK), BK), :]
-            s = nt(keys, qs[u])
+            s = nn(keys, qs[u])
             limit = limit_ref[u][0:1, :] - (kb * BK).astype(F32)
             s = jnp.where(key < limit, s, NEGATIVE)
             store[...] = s
@@ -635,8 +635,14 @@
                 )
             row = m_ref[u][0:1, :] + jnp.log(total)
             mine = lax.div(iota((8, COLS), 1), ROWS) == iota((8, COLS), 0)
-            member = (pos_col == lane_row + float(ch * ROWS)).astype(F32)
-            lse = lse + nt(jnp.where(mine, row, 0.0), member, HIGHEST)
+            member = (pos_col == lane_row + float(ch * ROWS)).astype(BF16)
+            rest = jnp.where(mine, row, 0.0)
+            layers = []
+            for _ in range(3):
+                layers.append(rest.astype(BF16))
+                rest = rest - layers[-1].astype(F32)
+            moved = nt(jnp.concatenate([layer.astype(F32) for layer in layers], axis=0).astype(BF16), member)
+            lse = lse + (moved[0:8] + moved[8:16] + moved[16:24])
         lse_ref[e] = lse
         o_ref[e] = nn(perm_t, sorted_out[e]).astype(BF16)
 
@@ -660,7 +666,7 @@
             pltpu.VMEM((2 * N_EP * PAGES, PAGE_TOKENS, 2 * HEAD_WIDTH), BF16),
             pltpu.VMEM((KEYS, 128), BF16),
             pltpu.VMEM((KEYS // BK, VROWS, BK), BF16),
-            pltpu.VMEM((UNITS * CHUNKS, COLS, 128), BF16),
+            pltpu.VMEM((UNITS * CHUNKS, 128, COLS), BF16),
             pltpu.VMEM((UNITS * CHUNKS, 8, COLS), F32),
             pltpu.VMEM((UNITS * CHUNKS, 8, COLS), F32),
             pltpu.VMEM((UNITS * CHUNKS, VROWS, COLS), F32),
@@ -735,15 +741,16 @@
     top = jnp.maximum(log0, log1)
     w0, w1 = jnp.exp(log0 - top), jnp.exp(log1 - top)
     share0, share1 = w0 / (w0 + w1), w1 / (w0 + w1)
-    parts = []
-    for share in (share0, share1):
-        high = share.astype(BF16)
-        parts.append((high, (share - high.astype(F32)).astype(BF16)))
+    shares = jnp.concatenate([share0, share1], axis=0)
+    high = shares.astype(BF16)
+    low = (shares - high.astype(F32)).astype(BF16)
+    both = jnp.concatenate([high, low], axis=1)
     for h in range(KEY_VALUE_HEADS):
-        shape = (64, HEAD_COLUMNS)
-        spread = (iota(shape, 0) == lax.div(iota(shape, 1), HEAD_WIDTH) + h * GROUP).astype(BF16)
-        wide = [nn(high, spread) + nn(low, spread) for high, low in parts]
-        result = wide[0] * o_all[h].astype(F32) + wide[1] * o_all[8 + h].astype(F32)
+        shape = (128, HEAD_COLUMNS)
+        head = lax.div(iota(shape, 1), HEAD_WIDTH) + h * GROUP
+        spread = (lax.rem(iota(shape, 0), QUERY_HEADS) == head).astype(BF16)
+        wide = nn(both, spread)
+        result = wide[:ROWS] * o_all[h].astype(F32) + wide[ROWS:] * o_all[8 + h].astype(F32)
         out_ref[:, h * HEAD_COLUMNS : (h + 1) * HEAD_COLUMNS] = result.astype(BF16)
 
 

time: 145 us -> 142 us (0.979)
  Pallas kernels: 131 us -> 128 us
    pallas_call x1, Pallas kernels: 51.7 us -> 49.7 us  [score(): pl.pallas_call(score_kernel, out_shape=(jax.ShapeDtypeStruct((UNITS, 128,...]
  transfers between devices with their start and end apart: 1 -> 1, of which waited for: 0 -> 0; matrix products, arithmetic and copies ran while one was open for 1% -> 1% of each run, Pallas kernels for 36% -> 35%
where the time goes in v9:
time: 142 us; the launch traced here: 141 us
  Pallas kernels  128 us (90%)
  starting transfers between devices  7.58 us (5%)
  local copies, waits for them, and re-layouts  4.12 us (3%)
    pallas_call x1, Pallas kernels, exchange(): pl.pallas_call(exchange_kernel, out_shape=(jax.ShapeDtypeStruct((16, ROWS...  62 us
    pallas_call x1, Pallas kernels, score(): pl.pallas_call(score_kernel, out_shape=(jax.ShapeDtypeStruct((UNITS, 128,...  49.7 us
    pallas_call x1, Pallas kernels, merge(): pl.pallas_call(merge_kernel, out_shape=(jax.ShapeDtypeStruct((ROWS, QUERY...  16.5 us
    all_to_all x1, starting transfers between devices, per_device(): lax.all_to_all(result, ('seq', 'ep'), split_axis=0, concat_axis=0, tiled=...  7.58 us
  transfers between devices with their start and end apart: 1, of which 0 were waited for; matrix products, arithmetic and copies ran while one was open for 1% of the time, Pallas kernels for 35%

profile of v9, /device:TPU:0, one launch (start us, length us, event | category | flops | bytes accessed | tf_op | source)
XLA Modules:
  0.0 140.7 jit_solution(5274654027064209349)
XLA Ops:
  0.6 0.0 copy-start.3
  0.6 62.0 %exchange.1 = (bf16[16,32,512]{2,1,0:T(8,128)(2,1)}, bf16[16,32,128]{2,1,0:T(8,128)(2,1)}, bf16[2,768,16,128]{3,2,1,0:T(8,128)(2,1)}, s32[2,4,2,128]{3,2,1,0:T(2...) custom-call(bf16[8,4,4096]{2,1,0:T(4,128)(2,1)} %bitcast.26, ...), custom_call_target="tpu_custom_call" | custom-call | tf_op jit(solution)/shard_map/exchange/pallas_call | solution.py:429
  62.6 7.6 %all-to-all-start = ((bf16[128,2,2880]{2,1,0:T(2,128)(2,1)}), bf16[128,2,2880]{2,1,0:T(2,128)(2,1)S(1)}, u32[]{:S(2)}, u32[]{:S(2)}) async-start(bf16[128,2,2880]{2,1,0:T(2,128)(2,1)} %get-tuple-element.21), calls=%async_computation | async-start | bytes 3014656 | tf_op jit(solution)/shard_map/all_to_all | solution.py:805
  70.2 0.0 copy-done.3
  70.2 0.1 dynamic_slice.3
  70.3 0.1 broadcast_in_dim.10
  70.4 0.1 broadcast_in_dim.11
  70.5 0.6 broadcast_in_dim.12.sinks
  71.1 0.0 copy-start.1
  71.1 49.7 %score.1 = (bf16[4,128,512]{2,1,0:T(8,128)(2,1)}, f32[4,8,128]{2,1,0:T(8,128)}) custom-call(s32[2,4,2,128]{3,2,1,0:T(2,128)} %get-tuple-element.13.table_ref, f32[4,8,128]{2,1,0:T(8,128)} %get-tuple-element.14.count_ref, f32[8,256]{1,0:T(8,128)} %broadcast_in_dim.12.sinks, bf16[16,32,512]{2,1,0:T(8,128)(2,1)} %get-tuple-element.15.q_ref, ...), custom_call_target="tpu_custom_call" | custom-call | flops 24999999488 | bytes 8000000 | tf_op jit(solution)/shard_map/score/pallas_call | solution.py:653
  120.8 0.0 all-to-all-done.rows_ref
  120.8 0.0 copy-done.1
  120.8 0.0 copy-start
  120.9 1.0 copy-done
  121.9 0.0 copy-start.2
  121.9 0.7 copy-done.2
  122.6 16.5 %merge.1 = (bf16[32,4096]{1,0:T(8,128)(2,1)S(1)}, bf16[32,2880]{1,0:T(8,128)(2,1)S(1)}) custom-call(bf16[4,128,512]{2,1,0:T(8,128)(2,1)S(1)} %copy-done, f32[4,8,128]{2,1,0:T(8,128)S(1)} %copy-done.2, f32[32,256]{1,0:T(8,128)S(1)} %copy-done.1, bf16[128,2,2880]{2,1,0:T(2,128)(2,1)S(1)} %all-to-all-done.rows_ref), custom_call_target="tpu_custom_call" | custom-call | tf_op jit(solution)/shard_map/merge/pallas_call | solution.py:761
  139.1 0.8 reshape.27
  139.9 0.7 reshape.28
Async XLA Ops:
  0.6 69.6 %copy-start.3 = (f32[64]{0:T(128)S(1)}, f32[64]{0:T(128)}, u32[]{:S(2)}) copy-start(f32[64]{0:T(128)} %param.19) | copy-start | bytes 772
  62.6 58.2 %all-to-all-start = ((bf16[128,2,2880]{2,1,0:T(2,128)(2,1)}), bf16[128,2,2880]{2,1,0:T(2,128)(2,1)S(1)}, u32[]{:S(2)}, u32[]{:S(2)}) async-start(bf16[128,2,2880]{2,1,0:T(2,128)(2,1)} %get-tuple-element.21), calls=%async_computation | async-start | bytes 3014656 | tf_op jit(solution)/shard_map/all_to_all | solution.py:805
  71.1 49.8 %copy-start.1 = (f32[32,256]{1,0:T(8,128)S(1)}, f32[32,256]{1,0:T(8,128)}, u32[]{:S(2)}) copy-start(f32[32,256]{1,0:T(8,128)} %get-tuple-element.20.share_ref) | copy-start | bytes 98308
  120.8 1.0 copy-start
  121.9 0.7 copy-start.2

commit v10 on v9

--- a/solution.py
+++ b/solution.py
@@ -498,7 +498,9 @@
         copy.start()
     for copy in loads[:3]:
         copy.wait()
-    sink_row = sinks[0:1, :]
+    head = head_of(y, lax.rem(lax.div(lax.axis_index("ep"), 2), 4))
+    spread = iota((QUERY_HEADS, COLS), 0) == head * GROUP + lax.div(iota((QUERY_HEADS, COLS), 1), ROWS)
+    sink_row = nn(sinks[...].reshape(1, QUERY_HEADS), spread.astype(F32), HIGHEST)
     i0 = iota((128, 128), 0)
     i1 = iota((128, 128), 1)
     lane_row = lax.rem(iota((128, COLS), 1), ROWS).astype(F32)
@@ -533,9 +535,9 @@
             stacked = jnp.concatenate([jnp.concatenate(pieces, axis=0), none], axis=1)
             qs[u] = stacked.T.astype(BF16)
             member = pos_col == lane_row + float(ch * ROWS)
-            limit = jnp.sum(jnp.where(member, n_col, 0.0), axis=0, keepdims=True) * PAGE_TOKENS
-            limit_ref[u] = jnp.broadcast_to(limit, (8, COLS))
-            lengths[u] = jnp.max(limit).astype(jnp.int32)
+            limit = jnp.sum(jnp.where(member, n_col, 0.0), axis=0, keepdims=True)
+            limit_ref[u] = jnp.broadcast_to(limit.astype(jnp.int32), (8, COLS))
+            lengths[u] = jnp.max(limit).astype(jnp.int32) * PAGE_TOKENS
             rows = f_sorted[ch * ROWS : (ch + 1) * ROWS, :]
             s = nn(rows, qs[u])
             ki = iota((ROWS, COLS), 0)
@@ -568,13 +570,13 @@
 
         lax.fori_loop(0, lax.div(lengths[e * CHUNKS] + (GK - 1), GK), gather, 0)
 
-        key = iota((BK, COLS), 0).astype(F32)
+        page = iota((BK // PAGE_TOKENS, PAGE_TOKENS // 8, 8, COLS), 0)
 
         def produce(store, u, kb):
             keys = kv[pl.ds(pl.multiple_of(kb * BK, BK), BK), :]
             s = nn(keys, qs[u])
-            limit = limit_ref[u][0:1, :] - (kb * BK).astype(F32)
-            s = jnp.where(key < limit, s, NEGATIVE)
+            live = page < (limit_ref[u] - kb * (BK // PAGE_TOKENS))[None, None]
+            s = jnp.where(live, s.reshape(page.shape), NEGATIVE).reshape(BK, COLS)
             store[...] = s
             return jnp.max(s, axis=0, keepdims=True)
 
@@ -667,7 +669,7 @@
             pltpu.VMEM((KEYS, 128), BF16),
             pltpu.VMEM((KEYS // BK, VROWS, BK), BF16),
             pltpu.VMEM((UNITS * CHUNKS, 128, COLS), BF16),
-            pltpu.VMEM((UNITS * CHUNKS, 8, COLS), F32),
+            pltpu.VMEM((UNITS * CHUNKS, 8, COLS), jnp.int32),
             pltpu.VMEM((UNITS * CHUNKS, 8, COLS), F32),
             pltpu.VMEM((UNITS * CHUNKS, VROWS, COLS), F32),
             pltpu.VMEM((UNITS, 128, HEAD_COLUMNS), BF16),
@@ -786,8 +788,6 @@
     queries, fresh_key_values, key_value_pages, page_owner, page_slot, page_count, sinks,
     hidden, norm_gain, expert_ids, gate_prob, gate_up, down_proj,
 ):
-    y, z, x, c = place()
-
     q_all, f_all, pool, tables, counts, result, share = exchange(
         queries[0],
         fresh_key_values[0],
@@ -803,10 +803,8 @@
         down_proj,
     )
     returned = lax.all_to_all(result, ("seq", "ep"), split_axis=0, concat_axis=0, tiled=True)
-    head_sinks = lax.dynamic_slice_in_dim(sinks, head_of(y, x) * GROUP, GROUP)
-    sink_rows = jnp.broadcast_to(jnp.repeat(head_sinks, ROWS)[None, :], (8, COLS))
     o, lse = score(
-        tables, counts, sink_rows, q_all, f_all,
+        tables, counts, sinks, q_all, f_all,
         pool.reshape(2 * N_EP * PAGES, PAGE_TOKENS, 2 * HEAD_WIDTH),
     )
     attention, mixture = merge(o, lse, share, returned)

time: 142 us -> 139 us (0.979)
  Pallas kernels: 128 us -> 126 us
    pallas_call x1, Pallas kernels: 49.7 us -> 47.5 us  [score(): pl.pallas_call(score_kernel, out_shape=(jax.ShapeDtypeStruct((UNITS, 128,...]
  transfers between devices with their start and end apart: 1 -> 1, of which waited for: 0 -> 0; matrix products, arithmetic and copies ran while one was open for 1% -> 0% of each run, Pallas kernels for 35% -> 34%
where the time goes in v10:
time: 139 us; the launch traced here: 138 us
  Pallas kernels  126 us (91%)
  starting transfers between devices  7.57 us (5%)
  local copies, waits for them, and re-layouts  3.29 us (2%)
    pallas_call x1, Pallas kernels, exchange(): pl.pallas_call(exchange_kernel, out_shape=(jax.ShapeDtypeStruct((16, ROWS...  62 us
    pallas_call x1, Pallas kernels, score(): pl.pallas_call(score_kernel, out_shape=(jax.ShapeDtypeStruct((UNITS, 128,...  47.5 us
    pallas_call x1, Pallas kernels, merge(): pl.pallas_call(merge_kernel, out_shape=(jax.ShapeDtypeStruct((ROWS, QUERY...  16.7 us
    all_to_all x1, starting transfers between devices, per_device(): lax.all_to_all(result, ('seq', 'ep'), split_axis=0, concat_axis=0, tiled=...  7.57 us
  transfers between devices with their start and end apart: 1, of which 0 were waited for; matrix products, arithmetic and copies ran while one was open for 0% of the time, Pallas kernels for 34%

profile of v10, /device:TPU:0, one launch (start us, length us, event | category | flops | bytes accessed | tf_op | source)
XLA Modules:
  0.0 137.8 jit_solution(15468931427581134196)
XLA Ops:
  0.6 62.0 %exchange.1 = (bf16[16,32,512]{2,1,0:T(8,128)(2,1)}, bf16[16,32,128]{2,1,0:T(8,128)(2,1)}, bf16[2,768,16,128]{3,2,1,0:T(8,128)(2,1)}, s32[2,4,2,128]{3,2,1,0:T(2...) custom-call(bf16[8,4,4096]{2,1,0:T(4,128)(2,1)} %bitcast.26, ...), custom_call_target="tpu_custom_call" | custom-call | tf_op jit(solution)/shard_map/exchange/pallas_call | solution.py:429
  62.6 7.6 %all-to-all-start = ((bf16[128,2,2880]{2,1,0:T(2,128)(2,1)}), bf16[128,2,2880]{2,1,0:T(2,128)(2,1)S(1)}, u32[]{:S(2)}, u32[]{:S(2)}) async-start(bf16[128,2,2880]{2,1,0:T(2,128)(2,1)} %get-tuple-element.21), calls=%async_computation | async-start | bytes 3014656 | tf_op jit(solution)/shard_map/all_to_all | solution.py:805
  70.2 0.0 copy-start.1
  70.2 47.5 %score.1 = (bf16[4,128,512]{2,1,0:T(8,128)(2,1)}, f32[4,8,128]{2,1,0:T(8,128)}) custom-call(s32[2,4,2,128]{3,2,1,0:T(2,128)} %get-tuple-element.13.table_ref, f32[4,8,128]{2,1,0:T(8,128)} %get-tuple-element.14.count_ref, f32[64]{0:T(128)} %sinks.1, bf16[16,32,512]{2,1,0:T(8,128)(2,1)} %get-tuple-element.15.q_ref, ...), custom_call_target="tpu_custom_call" | custom-call | flops 24999999488 | bytes 8000000 | tf_op jit(solution)/shard_map/score/pallas_call | solution.py:655
  117.7 0.0 all-to-all-done.rows_ref
  117.8 0.0 copy-done.1
  117.8 0.0 copy-start
  117.8 1.0 copy-done
  118.8 0.0 copy-start.2
  118.8 0.7 copy-done.2
  119.5 16.7 %merge.1 = (bf16[32,4096]{1,0:T(8,128)(2,1)S(1)}, bf16[32,2880]{1,0:T(8,128)(2,1)S(1)}) custom-call(bf16[4,128,512]{2,1,0:T(8,128)(2,1)S(1)} %copy-done, f32[4,8,128]{2,1,0:T(8,128)S(1)} %copy-done.2, f32[32,256]{1,0:T(8,128)S(1)} %copy-done.1, bf16[128,2,2880]{2,1,0:T(2,128)(2,1)S(1)} %all-to-all-done.rows_ref), custom_call_target="tpu_custom_call" | custom-call | tf_op jit(solution)/shard_map/merge/pallas_call | solution.py:763
  136.3 0.8 reshape.26
  137.1 0.7 reshape.27
Async XLA Ops:
  62.6 55.1 %all-to-all-start = ((bf16[128,2,2880]{2,1,0:T(2,128)(2,1)}), bf16[128,2,2880]{2,1,0:T(2,128)(2,1)S(1)}, u32[]{:S(2)}, u32[]{:S(2)}) async-start(bf16[128,2,2880]{2,1,0:T(2,128)(2,1)} %get-tuple-element.21), calls=%async_computation | async-start | bytes 3014656 | tf_op jit(solution)/shard_map/all_to_all | solution.py:805
  70.2 47.5 %copy-start.1 = (f32[32,256]{1,0:T(8,128)S(1)}, f32[32,256]{1,0:T(8,128)}, u32[]{:S(2)}) copy-start(f32[32,256]{1,0:T(8,128)} %get-tuple-element.20.share_ref) | copy-start | bytes 98308
  117.8 1.0 copy-start
  118.8 0.7 copy-start.2

commit v11 on v10

--- a/solution.py
+++ b/solution.py
@@ -463,6 +463,7 @@
 
 
 BK = 1024
+PIECE = 256
 GK = 4096
 KEYS = 2 * NPS * PAGE_TOKENS
 UNITS = 4
@@ -570,22 +571,30 @@
 
         lax.fori_loop(0, lax.div(lengths[e * CHUNKS] + (GK - 1), GK), gather, 0)
 
-        page = iota((BK // PAGE_TOKENS, PAGE_TOKENS // 8, 8, COLS), 0)
-
-        def produce(store, u, kb):
-            keys = kv[pl.ds(pl.multiple_of(kb * BK, BK), BK), :]
-            s = nn(keys, qs[u])
-            live = page < (limit_ref[u] - kb * (BK // PAGE_TOKENS))[None, None]
-            s = jnp.where(live, s.reshape(page.shape), NEGATIVE).reshape(BK, COLS)
-            store[...] = s
+        page = iota((PIECE // PAGE_TOKENS, PAGE_TOKENS // 8, 8, COLS), 0)
+
+        def produce(store, u, kb, i):
+            start = pl.multiple_of(kb * BK + i * PIECE, PIECE)
+            s = nn(kv[pl.ds(start, PIECE), :], qs[u])
+            live = page < (limit_ref[u] - lax.div(start, PAGE_TOKENS))[None, None]
+            s = jnp.where(live, s.reshape(page.shape), NEGATIVE).reshape(PIECE, COLS)
+            store[i * PIECE : (i + 1) * PIECE, :] = s
             return jnp.max(s, axis=0, keepdims=True)
 
-        def absorb(store, u, kb, top):
+        def step(store, u, kb, top, next_store, next_u, next_kb):
             before = m_ref[u][0:1, :]
             after = jnp.maximum(before, top)
-            p = jnp.exp(store[...] - after).astype(BF16)
-            acc[u] = acc[u] * jnp.exp(before - after) + nn(vt[kb], p)
+            total = acc[u] * jnp.exp(before - after)
+            next_top = None
+            for i in range(BK // PIECE):
+                part = slice(i * PIECE, (i + 1) * PIECE)
+                p = jnp.exp(store[part, :] - after).astype(BF16)
+                found = produce(next_store, next_u, next_kb, i)
+                next_top = found if i == 0 else jnp.maximum(next_top, found)
+                total = total + nn(vt[kb, :, part], p)
+            acc[u] = total
             m_ref[u] = jnp.broadcast_to(after, (8, COLS))
+            return next_top
 
         def chunk(ch, top):
             u = e * CHUNKS + ch
@@ -594,17 +603,14 @@
 
             def pair(i, top):
                 last = 2 * i + 2 >= count
-                next_top = produce(s1, u, 2 * i + 1)
-                absorb(s0, u, 2 * i, top)
-                top = produce(s0, jnp.where(last, after_u, u), jnp.where(last, 0, 2 * i + 2))
-                absorb(s1, u, 2 * i + 1, next_top)
-                return top
+                top = step(s0, u, 2 * i, top, s1, u, 2 * i + 1)
+                next_u = jnp.where(last, after_u, u)
+                return step(s1, u, 2 * i + 1, top, s0, next_u, jnp.where(last, 0, 2 * i + 2))
 
             top = lax.fori_loop(0, lax.div(count, 2), pair, top)
 
             def odd(top):
-                absorb(s0, u, count - 1, top)
-                return produce(s0, after_u, jnp.int32(0))
+                return step(s0, u, count - 1, top, s0, after_u, jnp.int32(0))
 
             return lax.cond(lax.rem(count, 2) == 1, odd, lambda top: top, top)
 
@@ -612,7 +618,8 @@
 
         @pl.when(used > 0)
         def _():
-            top = produce(s0, e * CHUNKS, jnp.int32(0))
+            tops = [produce(s0, e * CHUNKS, jnp.int32(0), i) for i in range(BK // PIECE)]
+            top = jnp.max(jnp.concatenate(tops, axis=0), axis=0, keepdims=True)
             lax.fori_loop(0, used, chunk, top)
 
         return carry

time: 139 us -> 135 us (0.971)
  Pallas kernels: 126 us -> 123 us
    pallas_call x1, Pallas kernels: 47.5 us -> 45.1 us  [score(): pl.pallas_call(score_kernel, out_shape=(jax.ShapeDtypeStruct((UNITS, 128,...]
where the time goes in v11:
time: 135 us; the launch traced here: 134 us
  Pallas kernels  123 us (91%)
  starting transfers between devices  7.57 us (6%)
  local copies, waits for them, and re-layouts  3.29 us (2%)
    pallas_call x1, Pallas kernels, exchange(): pl.pallas_call(exchange_kernel, out_shape=(jax.ShapeDtypeStruct((16, ROWS...  62 us
    pallas_call x1, Pallas kernels, score(): pl.pallas_call(score_kernel, out_shape=(jax.ShapeDtypeStruct((UNITS, 128,...  45.1 us
    pallas_call x1, Pallas kernels, merge(): pl.pallas_call(merge_kernel, out_shape=(jax.ShapeDtypeStruct((ROWS, QUERY...  15.6 us
    all_to_all x1, starting transfers between devices, per_device(): lax.all_to_all(result, ('seq', 'ep'), split_axis=0, concat_axis=0, tiled=...  7.57 us
  transfers between devices with their start and end apart: 1, of which 0 were waited for; matrix products, arithmetic and copies ran while one was open for 0% of the time, Pallas kernels for 34%

profile of v11, /device:TPU:0, one launch (start us, length us, event | category | flops | bytes accessed | tf_op | source)
XLA Modules:
  0.0 134.3 jit_solution(1226899308619360875)
XLA Ops:
  0.6 62.0 %exchange.1 = (bf16[16,32,512]{2,1,0:T(8,128)(2,1)}, bf16[16,32,128]{2,1,0:T(8,128)(2,1)}, bf16[2,768,16,128]{3,2,1,0:T(8,128)(2,1)}, s32[2,4,2,128]{3,2,1,0:T(2...) custom-call(bf16[8,4,4096]{2,1,0:T(4,128)(2,1)} %bitcast.26, ...), custom_call_target="tpu_custom_call" | custom-call | tf_op jit(solution)/shard_map/exchange/pallas_call | solution.py:429
  62.6 7.6 %all-to-all-start = ((bf16[128,2,2880]{2,1,0:T(2,128)(2,1)}), bf16[128,2,2880]{2,1,0:T(2,128)(2,1)S(1)}, u32[]{:S(2)}, u32[]{:S(2)}) async-start(bf16[128,2,2880]{2,1,0:T(2,128)(2,1)} %get-tuple-element.21), calls=%async_computation | async-start | bytes 3014656 | tf_op jit(solution)/shard_map/all_to_all | solution.py:812
  70.2 0.0 copy-start.1
  70.2 45.1 %score.1 = (bf16[4,128,512]{2,1,0:T(8,128)(2,1)}, f32[4,8,128]{2,1,0:T(8,128)}) custom-call(s32[2,4,2,128]{3,2,1,0:T(2,128)} %get-tuple-element.13.table_ref, f32[4,8,128]{2,1,0:T(8,128)} %get-tuple-element.14.count_ref, f32[64]{0:T(128)} %sinks.1, bf16[16,32,512]{2,1,0:T(8,128)(2,1)} %get-tuple-element.15.q_ref, ...), custom_call_target="tpu_custom_call" | custom-call | flops 24999999488 | bytes 8000000 | tf_op jit(solution)/shard_map/score/pallas_call | solution.py:662
  115.4 0.0 all-to-all-done.rows_ref
  115.4 0.0 copy-done.1
  115.4 0.0 copy-start
  115.4 1.0 copy-done
  116.4 0.0 copy-start.2
  116.4 0.7 copy-done.2
  117.1 15.6 %merge.1 = (bf16[32,4096]{1,0:T(8,128)(2,1)S(1)}, bf16[32,2880]{1,0:T(8,128)(2,1)S(1)}) custom-call(bf16[4,128,512]{2,1,0:T(8,128)(2,1)S(1)} %copy-done, f32[4,8,128]{2,1,0:T(8,128)S(1)} %copy-done.2, f32[32,256]{1,0:T(8,128)S(1)} %copy-done.1, bf16[128,2,2880]{2,1,0:T(2,128)(2,1)S(1)} %all-to-all-done.rows_ref), custom_call_target="tpu_custom_call" | custom-call | tf_op jit(solution)/shard_map/merge/pallas_call | solution.py:770
  132.7 0.8 reshape.26
  133.5 0.7 reshape.27
Async XLA Ops:
  62.6 52.7 %all-to-all-start = ((bf16[128,2,2880]{2,1,0:T(2,128)(2,1)}), bf16[128,2,2880]{2,1,0:T(2,128)(2,1)S(1)}, u32[]{:S(2)}, u32[]{:S(2)}) async-start(bf16[128,2,2880]{2,1,0:T(2,128)(2,1)} %get-tuple-element.21), calls=%async_computation | async-start | bytes 3014656 | tf_op jit(solution)/shard_map/all_to_all | solution.py:812
  70.2 45.2 %copy-start.1 = (f32[32,256]{1,0:T(8,128)S(1)}, f32[32,256]{1,0:T(8,128)}, u32[]{:S(2)}) copy-start(f32[32,256]{1,0:T(8,128)} %get-tuple-element.20.share_ref) | copy-start | bytes 98308
  115.4 1.0 copy-start
  116.4 0.7 copy-start.2

commit v12 on v11

--- a/solution.py
+++ b/solution.py
@@ -462,7 +462,7 @@
     )(queries, fresh, pages, owner, slot, count, hidden, gain, ids, prob, gate_up, down_proj)
 
 
-BK = 1024
+BK = 2048
 PIECE = 256
 GK = 4096
 KEYS = 2 * NPS * PAGE_TOKENS
@@ -497,8 +497,7 @@
         loads.append(pltpu.make_async_copy(pool_ref.at[part], pool.at[part], sem.at[4 + n]))
     for copy in loads:
         copy.start()
-    for copy in loads[:3]:
-        copy.wait()
+    loads[0].wait()
     head = head_of(y, lax.rem(lax.div(lax.axis_index("ep"), 2), 4))
     spread = iota((QUERY_HEADS, COLS), 0) == head * GROUP + lax.div(iota((QUERY_HEADS, COLS), 1), ROWS)
     sink_row = nn(sinks[...].reshape(1, QUERY_HEADS), spread.astype(F32), HIGHEST)
@@ -518,8 +517,11 @@
         pos_col = jnp.sum(jnp.where(behind, 1.0, 0.0), axis=1, keepdims=True)
         return n_row, n_col, pos_col
 
+    orders = [ordering(e) for e in range(UNITS)]
+    for copy in loads[1:3]:
+        copy.wait()
     for e in range(UNITS):
-        n_row, n_col, pos_col = ordering(e)
+        n_row, n_col, pos_col = orders[e]
         places[e] = pos_col
         ahead = jnp.logical_or(n_col > n_row, jnp.logical_and(n_col == n_row, i0 < i1))
         pos_row = jnp.sum(jnp.where(ahead, 1.0, 0.0), axis=0, keepdims=True)

time: 135 us -> 133 us (0.985)
  Pallas kernels: 123 us -> 120 us
    pallas_call x1, Pallas kernels: 45.1 us -> 41.7 us  [score(): pl.pallas_call(score_kernel, out_shape=(jax.ShapeDtypeStruct((UNITS, 128,...]
  transfers between devices with their start and end apart: 1 -> 1, of which waited for: 0 -> 0; matrix products, arithmetic and copies ran while one was open for 0% -> 0% of each run, Pallas kernels for 34% -> 32%
where the time goes in v12:
time: 133 us; the launch traced here: 132 us
  Pallas kernels  120 us (90%)
  starting transfers between devices  7.57 us (6%)
  local copies, waits for them, and re-layouts  3.29 us (2%)
    pallas_call x1, Pallas kernels, exchange(): pl.pallas_call(exchange_kernel, out_shape=(jax.ShapeDtypeStruct((16, ROWS...  62 us
    pallas_call x1, Pallas kernels, score(): pl.pallas_call(score_kernel, out_shape=(jax.ShapeDtypeStruct((UNITS, 128,...  41.7 us
    pallas_call x1, Pallas kernels, merge(): pl.pallas_call(merge_kernel, out_shape=(jax.ShapeDtypeStruct((ROWS, QUERY...  16.6 us
    all_to_all x1, starting transfers between devices, per_device(): lax.all_to_all(result, ('seq', 'ep'), split_axis=0, concat_axis=0, tiled=...  7.57 us
  transfers between devices with their start and end apart: 1, of which 0 were waited for; matrix products, arithmetic and copies ran while one was open for 0% of the time, Pallas kernels for 32%

profile of v12, /device:TPU:0, one launch (start us, length us, event | category | flops | bytes accessed | tf_op | source)
XLA Modules:
  0.0 131.8 jit_solution(127368791275392907)
XLA Ops:
  0.6 62.0 %exchange.1 = (bf16[16,32,512]{2,1,0:T(8,128)(2,1)}, bf16[16,32,128]{2,1,0:T(8,128)(2,1)}, bf16[2,768,16,128]{3,2,1,0:T(8,128)(2,1)}, s32[2,4,2,128]{3,2,1,0:T(2...) custom-call(bf16[8,4,4096]{2,1,0:T(4,128)(2,1)} %bitcast.26, ...), custom_call_target="tpu_custom_call" | custom-call | tf_op jit(solution)/shard_map/exchange/pallas_call | solution.py:429
  62.6 7.6 %all-to-all-start = ((bf16[128,2,2880]{2,1,0:T(2,128)(2,1)}), bf16[128,2,2880]{2,1,0:T(2,128)(2,1)S(1)}, u32[]{:S(2)}, u32[]{:S(2)}) async-start(bf16[128,2,2880]{2,1,0:T(2,128)(2,1)} %get-tuple-element.21), calls=%async_computation | async-start | bytes 3014656 | tf_op jit(solution)/shard_map/all_to_all | solution.py:814
  70.2 0.0 copy-start.1
  70.2 41.7 %score.1 = (bf16[4,128,512]{2,1,0:T(8,128)(2,1)}, f32[4,8,128]{2,1,0:T(8,128)}) custom-call(s32[2,4,2,128]{3,2,1,0:T(2,128)} %get-tuple-element.13.table_ref, f32[4,8,128]{2,1,0:T(8,128)} %get-tuple-element.14.count_ref, f32[64]{0:T(128)} %sinks.1, bf16[16,32,512]{2,1,0:T(8,128)(2,1)} %get-tuple-element.15.q_ref, ...), custom_call_target="tpu_custom_call" | custom-call | flops 24999999488 | bytes 8000000 | tf_op jit(solution)/shard_map/score/pallas_call | solution.py:664
  111.9 0.0 all-to-all-done.rows_ref
  111.9 0.0 copy-done.1
  111.9 0.0 copy-start
  111.9 1.0 copy-done
  113.0 0.0 copy-start.2
  113.0 0.7 copy-done.2
  113.7 16.6 %merge.1 = (bf16[32,4096]{1,0:T(8,128)(2,1)S(1)}, bf16[32,2880]{1,0:T(8,128)(2,1)S(1)}) custom-call(bf16[4,128,512]{2,1,0:T(8,128)(2,1)S(1)} %copy-done, f32[4,8,128]{2,1,0:T(8,128)S(1)} %copy-done.2, f32[32,256]{1,0:T(8,128)S(1)} %copy-done.1, bf16[128,2,2880]{2,1,0:T(2,128)(2,1)S(1)} %all-to-all-done.rows_ref), custom_call_target="tpu_custom_call" | custom-call | tf_op jit(solution)/shard_map/merge/pallas_call | solution.py:772
  130.3 0.8 reshape.26
  131.1 0.7 reshape.27
Async XLA Ops:
  62.6 49.3 %all-to-all-start = ((bf16[128,2,2880]{2,1,0:T(2,128)(2,1)}), bf16[128,2,2880]{2,1,0:T(2,128)(2,1)S(1)}, u32[]{:S(2)}, u32[]{:S(2)}) async-start(bf16[128,2,2880]{2,1,0:T(2,128)(2,1)} %get-tuple-element.21), calls=%async_computation | async-start | bytes 3014656 | tf_op jit(solution)/shard_map/all_to_all | solution.py:814
  70.2 41.7 %copy-start.1 = (f32[32,256]{1,0:T(8,128)S(1)}, f32[32,256]{1,0:T(8,128)}, u32[]{:S(2)}) copy-start(f32[32,256]{1,0:T(8,128)} %get-tuple-element.20.share_ref) | copy-start | bytes 98308
  111.9 1.0 copy-start
  113.0 0.7 copy-start.2
